TPU v7x, 32 devices: a whole 2x2x4 slice. The times are simulated.
32 devices in a mesh: row: 8 (over z, x), col: 4 (over y, core).
Axes of the slice: x: 2, y: 2, z: 4, core: 2. Of those that a mesh axis runs over, the one named last changes fastest.
Arguments:
- hidden_in: bfloat16 [16384, 1024], P('row', 'col'), may hold values from -6 to 6
- out_grad: bfloat16 [16384, 1024], P('row', 'col'), may hold values from -6 to 6
- lengths: int32 [8], P('row'), may hold values from 512 to 2048, as said below
- global_blocks: int32 [8, 2], P('row'), may hold values from 0 to 15, as said below
- rand_blocks: int32 [8, 32, 16, 3], P('row', None, 'col'), may hold values from 0 to 31, as said below
- w_query: float32 [1024, 1024], P('row', 'col'), may hold values from -0.1875 to 0.1875
- b_query: float32 [1024], replicated, may hold values from -3 to 3
- w_key: float32 [1024, 1024], P('row', 'col'), may hold values from -0.1875 to 0.1875
- w_value: float32 [1024, 1024], P('row', 'col'), may hold values from -0.1875 to 0.1875
- b_value: float32 [1024], replicated, may hold values from -3 to 3
- w_out: float32 [1024, 1024], P('col', 'row'), may hold values from -0.75 to 0.75
- b_out: float32 [1024], replicated, may hold values from -3 to 3
- ln1_gain: float32 [1024], replicated, may hold values from 0.25 to 1.75
- ln1_bias: float32 [1024], replicated, may hold values from -3 to 3
- w_up: float32 [1024, 4096], P('row', 'col'), may hold values from -0.1875 to 0.1875
- b_up: float32 [4096], replicated, may hold values from -3 to 3
- w_down: float32 [4096, 1024], P('col', 'row'), may hold values from -0.1875 to 0.1875
- b_down: float32 [1024], replicated, may hold values from -3 to 3
- ln2_gain: float32 [1024], replicated, may hold values from 0.25 to 1.75
- ln2_bias: float32 [1024], replicated, may hold values from -3 to 3
Outputs:
- layer_out: bfloat16 [16384, 1024], P('row', 'col')
- grad_input: bfloat16 [16384, 1024], P('row', 'col')
- grad_w_query: float32 [1024, 1024], P('row', 'col')
- grad_b_query: float32 [1024], replicated
- grad_w_key: float32 [1024, 1024], P('row', 'col')
- grad_w_value: float32 [1024, 1024], P('row', 'col')
- grad_b_value: float32 [1024], replicated
- grad_w_out: float32 [1024, 1024], P('col', 'row')
- grad_b_out: float32 [1024], replicated
- grad_ln1_gain: float32 [1024], replicated
- grad_ln1_bias: float32 [1024], replicated
- grad_w_up: float32 [1024, 4096], P('row', 'col')
- grad_b_up: float32 [4096], replicated
- grad_w_down: float32 [4096, 1024], P('col', 'row')
- grad_b_down: float32 [1024], replicated
- grad_ln2_gain: float32 [1024], replicated
- grad_ln2_bias: float32 [1024], replicated
Inputs may be any that keep to these rules, and one draw needn't show every extreme that they name: `lengths`: tokens after the valid ones of a sequence are padding; some sequence is full and some holds 512 valid tokens. `global_blocks`: two different blocks of each sequence, both among its first 16 blocks. `rand_blocks`: for query block i and a head: three different blocks, none of i - 1, i, i + 1 or the sequence's global blocks; they may lie in padding.
All inputs are finite; a program needn't handle non-finite values.
Results may differ from a plain program's by a relative error of at most 0.018.
The roundings to bfloat16 on the way count: a program that leaves them out, or rounds other values in their place, can miss the bound.
Values may be sent and summed in bfloat16 or wider, within the bound.
A program may use at most 256 MiB of HBM per device.

v0:
```python
import math

import jax
import jax.numpy as jnp
from jax import lax
from jax.sharding import PartitionSpec as P

DH = 64
BLK = 64


epsilon = 1e-06


def gelu_tanh(values_in):
    return jax.nn.gelu(values_in, approximate=True)


def layout(length, global_ids, random_ids, num_blocks, head_count):
    blocks = jnp.arange(num_blocks, dtype=jnp.int32)
    nearby_raw = blocks[:, None] + jnp.arange(-1, 2, dtype=jnp.int32)[None, :]
    near_ok = (nearby_raw >= 0) & (nearby_raw < num_blocks)
    nearby = jnp.clip(nearby_raw, 0, num_blocks - 1)
    global_rows = jnp.broadcast_to(global_ids[None, :], (num_blocks, 2))
    global_ok = jnp.all(global_rows[:, :, None] != nearby_raw[:, None, :], axis=2)
    common = jnp.concatenate([nearby, global_rows], axis=1)
    common_ok = jnp.concatenate([near_ok, global_ok], axis=1)
    key_blocks = jnp.concatenate(
        [jnp.broadcast_to(common[:, None, :], (num_blocks, head_count, 5)), random_ids], axis=2
    )
    block_ok = jnp.concatenate(
        [
            jnp.broadcast_to(common_ok[:, None, :], (num_blocks, head_count, 5)),
            jnp.ones((num_blocks, head_count, 3), jnp.bool_),
        ],
        axis=2,
    )
    positions = key_blocks[:, :, :, None] * BLK + jnp.arange(BLK, dtype=jnp.int32)
    allowed = block_ok[:, :, :, None] & (positions < length)
    return (key_blocks, allowed.reshape(num_blocks, head_count, 8 * BLK))


def take_blocks(rows, key_blocks):
    num_blocks = key_blocks.shape[0]
    head_count = key_blocks.shape[1]
    arranged = rows.reshape(num_blocks, BLK, head_count, DH).transpose(2, 0, 1, 3)
    head_ids = jnp.arange(head_count)[None, :, None]
    return arranged[head_ids, key_blocks].reshape(num_blocks, head_count, 8 * BLK, DH)


def put_blocks(pieces, key_blocks):
    num_blocks = key_blocks.shape[0]
    head_count = key_blocks.shape[1]
    shaped = pieces.reshape(num_blocks, head_count, 8, BLK, DH)
    head_ids = jnp.arange(head_count)[None, :, None]
    summed = (
        jnp.zeros((head_count, num_blocks, BLK, DH), jnp.float32)
        .at[head_ids, key_blocks]
        .add(shaped)
    )
    return summed.transpose(1, 2, 0, 3).reshape(num_blocks * BLK, head_count * DH)


def by_heads(rows, num_blocks, head_count):
    return rows.reshape(num_blocks, BLK, head_count, DH).transpose(0, 2, 1, 3)


def by_tokens(grouped):
    num_blocks = grouped.shape[0]
    head_count = grouped.shape[1]
    return grouped.transpose(0, 2, 1, 3).reshape(num_blocks * BLK, head_count * DH)


def scores_of(grouped, picked_keys, allowed):
    factor = 1.0 / math.sqrt(DH)
    scores = (
        jnp.einsum("nhqd,nhkd->nhqk", grouped, picked_keys, preferred_element_type=jnp.float32)
        * factor
    )
    return jnp.where(allowed[:, :, None, :], scores, -1e30)


def attend(queries, key_rows, value_rows, key_blocks, allowed):
    num_blocks = key_blocks.shape[0]
    head_count = key_blocks.shape[1]
    grouped = by_heads(queries, num_blocks, head_count)
    scores = scores_of(grouped, take_blocks(key_rows, key_blocks), allowed)
    highest = jnp.max(scores, axis=3, keepdims=True)
    exponent = jnp.exp(scores - highest)
    denominator = jnp.sum(exponent, axis=3, keepdims=True)
    attn_probs = (exponent / denominator).astype(jnp.bfloat16)
    context = jnp.einsum(
        "nhqk,nhkd->nhqd",
        attn_probs,
        take_blocks(value_rows, key_blocks),
        preferred_element_type=jnp.float32,
    )
    return (by_tokens(context).astype(jnp.bfloat16), highest + jnp.log(denominator))


def attend_back(queries, key_rows, value_rows, key_blocks, allowed, logsum, context_grad):
    num_blocks = key_blocks.shape[0]
    head_count = key_blocks.shape[1]
    factor = 1.0 / math.sqrt(DH)
    grouped = by_heads(queries, num_blocks, head_count)
    picked_keys = take_blocks(key_rows, key_blocks)
    picked_values = take_blocks(value_rows, key_blocks)
    attn_probs = jnp.exp(scores_of(grouped, picked_keys, allowed) - logsum)
    grouped_grad = by_heads(context_grad, num_blocks, head_count)
    prob_grad = jnp.einsum(
        "nhqd,nhkd->nhqk", grouped_grad, picked_values, preferred_element_type=jnp.float32
    )
    value_grad = jnp.einsum(
        "nhqk,nhqd->nhkd",
        attn_probs.astype(jnp.bfloat16),
        grouped_grad,
        preferred_element_type=jnp.float32,
    )
    score_grad = (
        attn_probs * (prob_grad - jnp.sum(attn_probs * prob_grad, axis=3, keepdims=True))
    ).astype(jnp.bfloat16)
    query_grad = (
        jnp.einsum("nhqk,nhkd->nhqd", score_grad, picked_keys, preferred_element_type=jnp.float32)
        * factor
    )
    key_grad = (
        jnp.einsum("nhqk,nhqd->nhkd", score_grad, grouped, preferred_element_type=jnp.float32)
        * factor
    )
    return (
        by_tokens(query_grad).astype(jnp.bfloat16),
        put_blocks(key_grad, key_blocks).astype(jnp.bfloat16),
        put_blocks(value_grad, key_blocks).astype(jnp.bfloat16),
    )


def spread(portion):
    return lax.all_gather(portion, "col", axis=1, tiled=True)


def reduce_cols(partial_value):
    return lax.psum_scatter(partial_value, "col", scatter_dimension=1, tiled=True)


def col_totals(left_sum, right_sum):
    return lax.psum((left_sum, right_sum), "col")


def norm_stats(left_sum, right_sum, features_all):
    average = left_sum / features_all
    return (average, lax.rsqrt(right_sum / features_all - average * average + epsilon))


def residual_norm(partial_value, resid, bias_vec, gain_vec, offset_vec, feat_start, want_full):
    feat_cols = resid.shape[1]
    features_all = partial_value.shape[1]
    summed = (
        resid
        + reduce_cols(partial_value)
        + lax.dynamic_slice_in_dim(bias_vec, feat_start, feat_cols)
    )
    left_sum, right_sum = col_totals(
        jnp.sum(summed, axis=1, keepdims=True), jnp.sum(summed * summed, axis=1, keepdims=True)
    )
    average, inv_std = norm_stats(left_sum, right_sum, features_all)
    normed = (summed - average) * inv_std
    result = normed * lax.dynamic_slice_in_dim(
        gain_vec, feat_start, feat_cols
    ) + lax.dynamic_slice_in_dim(offset_vec, feat_start, feat_cols)
    result_full = result
    if want_full:
        result_full = spread(result.astype(jnp.bfloat16))
    return (result, result_full, normed, inv_std)


def norm_back(upstream, normed, inv_std, gain_share, features_all):
    scaled = upstream * gain_share
    left_sum, right_sum = col_totals(
        jnp.sum(scaled, axis=1, keepdims=True), jnp.sum(scaled * normed, axis=1, keepdims=True)
    )
    result = inv_std * (scaled - left_sum / features_all - normed * right_sum / features_all)
    return (result, jnp.sum(upstream * normed, axis=0), jnp.sum(upstream, axis=0))


def into_full(portion, start_at, full_len):
    return lax.dynamic_update_slice_in_dim(
        jnp.zeros((full_len,), jnp.float32), portion, start_at, 0
    )


def on_device(
    hidden_in,
    out_grad,
    lengths,
    global_blocks,
    rand_blocks,
    w_query,
    b_query,
    w_key,
    w_value,
    b_value,
    w_out,
    b_out,
    ln1_gain,
    ln1_bias,
    w_up,
    b_up,
    w_down,
    b_down,
    ln2_gain,
    ln2_bias,
):
    seq_len = hidden_in.shape[0]
    feat_cols = hidden_in.shape[1]
    unit_cols = w_up.shape[1]
    features_all = feat_cols * lax.axis_size("col")
    units_all = unit_cols * lax.axis_size("col")
    num_blocks = seq_len // BLK
    head_count = feat_cols // DH
    column = lax.axis_index("col")
    feat_start = column * feat_cols
    unit_start = column * unit_cols
    length = lengths[0]
    valid_rows = (jnp.arange(seq_len) < length)[:, None]
    key_blocks, allowed = layout(length, global_blocks[0], rand_blocks[0], num_blocks, head_count)
    full_query, full_key, full_value, full_up, full_out, full_down = (
        lax.all_gather(w_query.astype(jnp.bfloat16), "row", axis=0, tiled=True),
        lax.all_gather(w_key.astype(jnp.bfloat16), "row", axis=0, tiled=True),
        lax.all_gather(w_value.astype(jnp.bfloat16), "row", axis=0, tiled=True),
        lax.all_gather(w_up.astype(jnp.bfloat16), "row", axis=0, tiled=True),
        lax.all_gather(w_out.astype(jnp.bfloat16), "row", axis=1, tiled=True),
        lax.all_gather(w_down.astype(jnp.bfloat16), "row", axis=1, tiled=True),
    )
    features = spread(hidden_in)
    queries = (
        jnp.dot(features, full_query, preferred_element_type=jnp.float32)
        + lax.dynamic_slice_in_dim(b_query, feat_start, feat_cols)
    ).astype(jnp.bfloat16)
    key_rows = jnp.dot(features, full_key, preferred_element_type=jnp.float32).astype(jnp.bfloat16)
    value_rows = (
        jnp.dot(features, full_value, preferred_element_type=jnp.float32)
        + lax.dynamic_slice_in_dim(b_value, feat_start, feat_cols)
    ).astype(jnp.bfloat16)
    context, logsum = attend(queries, key_rows, value_rows, key_blocks, allowed)
    attn_part = jnp.dot(context, full_out, preferred_element_type=jnp.float32)
    normed1, normed1_full, unit1, inv_std1 = residual_norm(
        attn_part, hidden_in.astype(jnp.float32), b_out, ln1_gain, ln1_bias, feat_start, True
    )
    pre_act = jnp.dot(
        normed1_full, full_up, preferred_element_type=jnp.float32
    ) + lax.dynamic_slice_in_dim(b_up, unit_start, unit_cols)
    activated, gelu_back = jax.vjp(gelu_tanh, pre_act)
    hidden = activated.astype(jnp.bfloat16)
    ffn_part = jnp.dot(hidden, full_down, preferred_element_type=jnp.float32)
    normed2, unused, unit2, inv_std2 = residual_norm(
        ffn_part, normed1, b_down, ln2_gain, ln2_bias, feat_start, False
    )
    layer_out = jnp.where(valid_rows, normed2, 0.0).astype(jnp.bfloat16)
    upstream = jnp.where(valid_rows, out_grad.astype(jnp.float32), 0.0)
    ffn_grad, gain2_grad, shift2_grad = norm_back(
        upstream,
        unit2,
        inv_std2,
        lax.dynamic_slice_in_dim(ln2_gain, feat_start, feat_cols),
        features_all,
    )
    ffn_low = ffn_grad.astype(jnp.bfloat16)
    ffn_full = spread(ffn_low)
    grad_down = jnp.einsum("sf,sd->fd", hidden, ffn_full, preferred_element_type=jnp.float32)
    hidden_grad = jnp.einsum("sd,fd->sf", ffn_full, full_down, preferred_element_type=jnp.float32)
    pre_grad = gelu_back(hidden_grad)[0].astype(jnp.bfloat16)
    grad_up = jnp.einsum("sd,sf->df", normed1_full, pre_grad, preferred_element_type=jnp.float32)
    normed1_grad = ffn_grad + reduce_cols(
        jnp.einsum("sf,df->sd", pre_grad, full_up, preferred_element_type=jnp.float32)
    )
    attn_grad, gain1_grad, shift1_grad = norm_back(
        normed1_grad,
        unit1,
        inv_std1,
        lax.dynamic_slice_in_dim(ln1_gain, feat_start, feat_cols),
        features_all,
    )
    attn_low = attn_grad.astype(jnp.bfloat16)
    attn_full = spread(attn_low)
    grad_out = jnp.einsum("sc,sd->cd", context, attn_full, preferred_element_type=jnp.float32)
    context_grad = jnp.einsum(
        "sd,cd->sc", attn_full, full_out, preferred_element_type=jnp.float32
    ).astype(jnp.bfloat16)
    query_grad, key_grad, value_grad = attend_back(
        queries, key_rows, value_rows, key_blocks, allowed, logsum, context_grad
    )
    grad_query = jnp.einsum("sd,sc->dc", features, query_grad, preferred_element_type=jnp.float32)
    grad_key = jnp.einsum("sd,sc->dc", features, key_grad, preferred_element_type=jnp.float32)
    grad_value = jnp.einsum("sd,sc->dc", features, value_grad, preferred_element_type=jnp.float32)
    input_part = (
        jnp.einsum("sc,dc->sd", query_grad, full_query, preferred_element_type=jnp.float32)
        + jnp.einsum("sc,dc->sd", key_grad, full_key, preferred_element_type=jnp.float32)
        + jnp.einsum("sc,dc->sd", value_grad, full_value, preferred_element_type=jnp.float32)
    )
    grad_input = (attn_grad + reduce_cols(input_part)).astype(jnp.bfloat16)
    weight_grads = (
        lax.psum_scatter(
            grad_query.astype(jnp.bfloat16), "row", scatter_dimension=0, tiled=True
        ).astype(jnp.float32),
        lax.psum_scatter(
            grad_key.astype(jnp.bfloat16), "row", scatter_dimension=0, tiled=True
        ).astype(jnp.float32),
        lax.psum_scatter(
            grad_value.astype(jnp.bfloat16), "row", scatter_dimension=0, tiled=True
        ).astype(jnp.float32),
        lax.psum_scatter(
            grad_up.astype(jnp.bfloat16), "row", scatter_dimension=0, tiled=True
        ).astype(jnp.float32),
        lax.psum_scatter(
            grad_out.astype(jnp.bfloat16), "row", scatter_dimension=1, tiled=True
        ).astype(jnp.float32),
        lax.psum_scatter(
            grad_down.astype(jnp.bfloat16), "row", scatter_dimension=1, tiled=True
        ).astype(jnp.float32),
    )
    small_grads = lax.psum(
        (
            into_full(jnp.sum(query_grad, axis=0, dtype=jnp.float32), feat_start, features_all),
            into_full(jnp.sum(value_grad, axis=0, dtype=jnp.float32), feat_start, features_all),
            into_full(jnp.sum(attn_low, axis=0, dtype=jnp.float32), feat_start, features_all),
            into_full(gain1_grad, feat_start, features_all),
            into_full(shift1_grad, feat_start, features_all),
            into_full(jnp.sum(pre_grad, axis=0, dtype=jnp.float32), unit_start, units_all),
            into_full(jnp.sum(ffn_low, axis=0, dtype=jnp.float32), feat_start, features_all),
            into_full(gain2_grad, feat_start, features_all),
            into_full(shift2_grad, feat_start, features_all),
        ),
        ("row", "col"),
    )
    return (
        layer_out,
        grad_input,
        weight_grads[0],
        small_grads[0],
        weight_grads[1],
        weight_grads[2],
        small_grads[1],
        weight_grads[4],
        small_grads[2],
        small_grads[3],
        small_grads[4],
        weight_grads[3],
        small_grads[5],
        weight_grads[5],
        small_grads[6],
        small_grads[7],
        small_grads[8],
    )


def solution(mesh):
    placed = (
        P("row", "col"),
        P("row", "col"),
        P("row"),
        P("row", None),
        P("row", None, "col", None),
        P("row", "col"),
        P(),
        P("row", "col"),
        P("row", "col"),
        P(),
        P("col", "row"),
        P(),
        P(),
        P(),
        P("row", "col"),
        P(),
        P("col", "row"),
        P(),
        P(),
        P(),
    )
    return jax.shard_map(
        on_device,
        mesh=mesh,
        in_specs=placed,
        out_specs=(
            P("row", "col"),
            P("row", "col"),
            P("row", "col"),
            P(),
            P("row", "col"),
            P("row", "col"),
            P(),
            P("col", "row"),
            P(),
            P(),
            P(),
            P("row", "col"),
            P(),
            P("col", "row"),
            P(),
            P(),
            P(),
        ),
        check_vma=False,
    )
```

profile of v0, /device:TPU:0, one launch (start us, length us, event | category | flops | bytes accessed | tf_op | source)
XLA Modules:
  0.0 1358.1 jit_solution(6171378586047331281)
XLA Ops:
  19.1 30.7 %all_gather.34 = bf16[256,1024]{1,0:T(8,128)(2,1)} all-gather(bf16[256,128]{1,0:T(8,128)(2,1)S(1)} %convert_element_type.181), channel_id=1, replica_groups=mesh['row'=8,'col'=4] {'row'}, dimensions={1}, use_global_device_ids=true | all-gather | bytes 589824 | tf_op jit(solution)/shard_map/all_gather | solution.py:231
  49.8 31.4 %all_gather.33 = bf16[1024,256]{1,0:T(8,128)(2,1)S(1)} all-gather(bf16[128,256]{1,0:T(8,128)(2,1)S(1)} %convert_element_type.176), channel_id=1, replica_groups=mesh['row'=8,'col'=4] {'row'}, dimensions={0}, use_global_device_ids=true | all-gather | bytes 589824 | tf_op jit(solution)/shard_map/all_gather | solution.py:229
  81.1 31.6 %all_gather.32 = bf16[1024,256]{1,0:T(8,128)(2,1)S(1)} all-gather(bf16[128,256]{1,0:T(8,128)(2,1)S(1)} %convert_element_type.173), channel_id=1, replica_groups=mesh['row'=8,'col'=4] {'row'}, dimensions={0}, use_global_device_ids=true | all-gather | bytes 589824 | tf_op jit(solution)/shard_map/all_gather | solution.py:228
  112.7 31.2 %all_gather.31 = bf16[1024,256]{1,0:T(8,128)(2,1)S(1)} all-gather(bf16[128,256]{1,0:T(8,128)(2,1)S(1)} %convert_element_type.171), channel_id=1, replica_groups=mesh['row'=8,'col'=4] {'row'}, dimensions={0}, use_global_device_ids=true | all-gather | bytes 589824 | tf_op jit(solution)/shard_map/all_gather | solution.py:227
  177.0 16.4 %gather_fusion = bf16[1024,64,64]{2,1,0:T(8,128)(2,1)} fusion(bf16[4,32,64,64]{3,2,1,0:T(8,128)(2,1)} %bitcast.140, s32[1024]{0:T(1024)S(1)} %reshape.241), kind=kCustom, calls=%fused_computation | custom fusion | bytes 16785408 | tf_op jit(solution)/shard_map/gather | solution.py:48
  193.4 14.7 %gather_fusion.1 = bf16[1024,64,64]{2,1,0:T(8,128)(2,1)} fusion(bf16[4,32,64,64]{3,2,1,0:T(8,128)(2,1)S(1)} %bitcast.139, s32[1024]{0:T(1024)S(1)} %reshape.241), kind=kCustom, calls=%fused_computation.1 | custom fusion | bytes 16785408 | tf_op jit(solution)/shard_map/gather | solution.py:48
  208.1 13.1 fusion.40
  229.0 14.1 %convert_bitcast_fusion = bf16[32,64,4,64]{3,1,2,0:T(8,128)(2,1)} fusion(bf16[32,4,512,64]{3,2,1,0:T(8,128)(2,1)} %bitcast.142, f32[32,4,64,512]{3,2,1,0:T(8,128)} %get-tuple-element.170, f32[32,4,64]{2,1,0:T(4,128)S(1)} %fusion, f32[32,4,64]{2,1,0:T(4,128)S(1)} %get-tuple-element.169), kind=kOutput, calls=%fused_computation.65 | convolution fusion | flops 549978112 | bytes 26279936 | tf_op jit(solution)/shard_map/nhqk,nhkd->nhqd/dot_general | solution.py:92
  259.4 67.0 %reduce-scatter.21.cloned.1.call-done = f32[2048,256]{1,0:T(8,128)} async-done(((f32[2048,1024]{1,0:T(8,128)}), f32[2048,256]{1,0:T(8,128)}) %reduce-scatter.21.cloned.1.call-update) | async-done | bytes 2097168 | tf_op jit(solution)/shard_map/reduce_scatter | solution.py:142
  342.9 33.4 %all-gather.9.cloned.1.call-done = bf16[2048,1024]{1,0:T(8,128)(2,1)} async-done(((bf16[2048,256]{1,0:T(8,128)(2,1)}), bf16[2048,1024]{1,0:T(8,128)(2,1)}) %all-gather.9.cloned.1.call-update) | async-done | bytes 4194320 | tf_op jit(solution)/shard_map/all_gather | solution.py:138
  386.9 42.1 %all-gather.13.cloned.1.call-done = bf16[1024,1024]{1,0:T(8,128)(2,1)} async-done(((bf16[1024,128]{1,0:T(8,128)(2,1)}), bf16[1024,1024]{1,0:T(8,128)(2,1)}) %all-gather.13.cloned.1.call-update) | async-done | bytes 2097168 | tf_op jit(solution)/shard_map/all_gather | solution.py:232
  429.0 12.8 fusion.34
  443.5 68.3 %reduce-scatter.23.cloned.1.call-done = f32[2048,256]{1,0:T(8,128)} async-done(((f32[2048,1024]{1,0:T(8,128)}), f32[2048,256]{1,0:T(8,128)}) %reduce-scatter.23.cloned.1.call-update) | async-done | bytes 2097168 | tf_op jit(solution)/shard_map/reduce_scatter | solution.py:142
  544.3 35.8 %all-gather.15.cloned.1.call-done = bf16[2048,1024]{1,0:T(8,128)(2,1)} async-done(((bf16[2048,256]{1,0:T(8,128)(2,1)}), bf16[2048,1024]{1,0:T(8,128)(2,1)}) %all-gather.15.cloned.1.call-update) | async-done | bytes 4194320 | tf_op jit(solution)/shard_map/all_gather | solution.py:138
  580.1 14.4 %convert_reduce_fusion = (f32[1024]{0:T(1024)}, bf16[2048,1024]{1,0:T(8,128)(2,1)S(1)}) fusion(f32[2048,1024]{1,0:T(8,128)} %fusion.42, f32[1024]{0:T(1024)S(1)} %dynamic_slice.34, bf16[2048,1024]{1,0:T(8,128)(2,1)} %all-gather.15.cloned.1.call-done, bf16[1024,1024]{1,0:T(8,128)(2,1)} %all-gather.13.cloned.1.call-done), kind=kOutput, calls=%fused_computation.23 | convolution fusion | flops 4343200768 | bytes 18882560 | tf_op jit(solution)/shard_map/sd,fd->sf/dot_general | solution.py:270
  604.2 71.1 %reduce-scatter.25.cloned.1.call-done = f32[2048,256]{1,0:T(8,128)} async-done(((f32[2048,1024]{1,0:T(8,128)}), f32[2048,256]{1,0:T(8,128)}) %reduce-scatter.25.cloned.1.call-update) | async-done | bytes 2097168 | tf_op jit(solution)/shard_map/reduce_scatter | solution.py:142
  745.9 20.6 %multiply_reduce_fusion = (f32[32,4,64]{2,1,0:T(4,128)S(1)}, f32[32,4,64,512]{3,2,1,0:T(8,128)}) fusion(f32[32,4,64,512]{3,2,1,0:T(8,128)} %get-tuple-element.170, f32[32,4,64]{2,1,0:T(4,128)S(1)} %bitcast.150, bf16[32,4,512,64]{3,2,1,0:T(8,128)(2,1)} %bitcast.143, bf16[32,64,4,64]{1,3,2,0:T(8,128)(2,1)S(1)} %copy.189), kind=kOutput, calls=%fused_computation.5 | convolution fusion | flops 549445632 | bytes 43057152 | tf_op jit(solution)/shard_map/nhqd,nhkd->nhqk/dot_general | solution.py:110
  778.5 13.2 convert_reduce_fusion.2
  804.6 17.7 %fusion.9 = f32[32,4,512,64]{3,2,1,0:T(8,128)} fusion(f32[32,4,64,512]{3,2,1,0:T(8,128)} %get-tuple-element.170, f32[32,4,64]{2,1,0:T(4,128)S(1)} %bitcast.152, bf16[32,64,4,64]{1,3,2,0:T(8,128)(2,1)S(1)} %copy-done.4), kind=kOutput, calls=%fused_computation.22 | convolution fusion | flops 545259520 | bytes 34635776 | tf_op jit(solution)/shard_map/reshape | solution.py:54
  824.7 156.5 %scatter_fusion.1 = f32[128,64,64]{2,1,0:T(8,128)} fusion(f32[128,64,64]{2,1,0:T(8,128)} %broadcast.170.clone.1, s32[1024]{0:T(1024)S(1)} %reshape.253, f32[1024,64,64]{2,1,0:T(8,128)} %bitcast.138), kind=kCustom, calls=%fused_computation.3 | custom fusion | flops 4194304 | bytes 50335744
  1010.5 23.0 %copy.192 = f32[32,4,512,64]{3,2,1,0:T(8,128)} copy(f32[32,4,512,64]{2,3,1,0:T(8,128)} %convolution_multiply_fusion) | data formatting | bytes 33554432 | tf_op jit(solution)/shard_map/reshape | solution.py:54
  1036.0 156.1 %scatter_fusion = f32[128,64,64]{2,1,0:T(8,128)} fusion(f32[128,64,64]{2,1,0:T(8,128)} %broadcast.170.clone, s32[1024]{0:T(1024)S(1)} %reshape.253, f32[1024,64,64]{2,1,0:T(8,128)} %bitcast.141), kind=kCustom, calls=%fused_computation.2 | custom fusion | flops 4194304 | bytes 50335744
  1227.0 40.8 %all-reduce.1 = (f32[1024]{0:T(1024)}, f32[1024]{0:T(1024)}, f32[1024]{0:T(1024)}, f32[1024]{0:T(1024)}, f32[1024]{0:T(1024)}, /*index=5*/f32[4096]{0:T(1024)}, f32[1024]{0:T(1024)}, f32[1024]{0:T(1024)}, f32[1024]{0:T(1024)}) all-reduce(f32[1024]{0:T(1024)S(1)} %dynamic_update_slice.27, ...), channel_id=1, replica_groups=mesh['row'=8,'col'=4] {'row','col'}, use_global_device_ids=true, to_apply=%region_28.29 | all-reduce | flops 12288 | bytes 98304 | tf_op jit(solution)/shard_map/psum | solution.py:321
  1275.4 71.8 %reduce-scatter.27.cloned.1.call-done = f32[2048,256]{1,0:T(8,128)} async-done(((f32[2048,1024]{1,0:T(8,128)}), f32[2048,256]{1,0:T(8,128)}) %reduce-scatter.27.cloned.1.call-update) | async-done | bytes 2097168 | tf_op jit(solution)/shard_map/reduce_scatter | solution.py:142
  (243 shorter events, 313.5 us)
Async XLA Ops:
  8.0 136.0 %all-gather.7.cloned.1.call-start = ((), (), s32[]{:S(2)}) async-start(), calls=%async_computation.10 | async-start | bytes 5242880 | tf_op jit(solution)/shard_map/all_gather | solution.py:138
  8.8 317.6 %reduce-scatter.21.cloned.1.call-start = ((), (), s32[]{:S(2)}) async-start(), calls=%async_computation.11 | async-start | bytes 10485760 | tf_op jit(solution)/shard_map/reduce_scatter | solution.py:142
  81.1 66.4 %copy-start.12 = (bf16[1024,256]{1,0:T(8,128)(2,1)}, bf16[1024,256]{1,0:T(8,128)(2,1)S(1)}, u32[]{:S(2)}) copy-start(bf16[1024,256]{1,0:T(8,128)(2,1)S(1)} %all_gather.33) | copy-start | bytes 1572868
  112.7 52.0 %copy-start.14 = (bf16[1024,256]{1,0:T(8,128)(2,1)}, bf16[1024,256]{1,0:T(8,128)(2,1)S(1)}, u32[]{:S(2)}) copy-start(bf16[1024,256]{1,0:T(8,128)(2,1)S(1)} %all_gather.32) | copy-start | bytes 1572868
  255.2 71.2 %copy-start.11 = (bf16[2048,256]{1,0:T(8,128)(2,1)S(1)}, bf16[2048,256]{1,0:T(8,128)(2,1)}, u32[]{:S(2)}) copy-start(bf16[2048,256]{1,0:T(8,128)(2,1)} %param.20) | copy-start | bytes 3145732
  255.2 87.7 %all-gather.11.cloned.1.call-start = ((), (), s32[]{:S(2)}) async-start(), calls=%async_computation.13 | async-start | bytes 2359296 | tf_op jit(solution)/shard_map/all_gather | solution.py:230
  257.0 119.3 %all-gather.9.cloned.1.call-start = ((), (), s32[]{:S(2)}) async-start(), calls=%async_computation.12 | async-start | bytes 5242880 | tf_op jit(solution)/shard_map/all_gather | solution.py:138
  340.3 88.7 %all-gather.13.cloned.1.call-start = ((), (), s32[]{:S(2)}) async-start(), calls=%async_computation.14 | async-start | bytes 2359296 | tf_op jit(solution)/shard_map/all_gather | solution.py:232
  342.2 169.6 %reduce-scatter.23.cloned.1.call-start = ((), (), s32[]{:S(2)}) async-start(), calls=%async_computation.15 | async-start | bytes 10485760 | tf_op jit(solution)/shard_map/reduce_scatter | solution.py:142
  441.8 83.6 %copy-start.7 = (bf16[2048,256]{1,0:T(8,128)(2,1)S(1)}, bf16[2048,256]{1,0:T(8,128)(2,1)}, u32[]{:S(2)}) copy-start(bf16[2048,256]{1,0:T(8,128)(2,1)} %param.21) | copy-start | bytes 3145732
  441.8 138.2 %all-gather.15.cloned.1.call-start = ((), (), s32[]{:S(2)}) async-start(), calls=%async_computation.16 | async-start | bytes 5242880 | tf_op jit(solution)/shard_map/all_gather | solution.py:138
  544.3 131.0 %reduce-scatter.25.cloned.1.call-start = ((), (), s32[]{:S(2)}) async-start(), calls=%async_computation.17 | async-start | bytes 10485760 | tf_op jit(solution)/shard_map/reduce_scatter | solution.py:142
  580.1 16.3 %copy-start.29 = (bf16[1024,1024]{1,0:T(8,128)(2,1)S(1)}, bf16[1024,1024]{1,0:T(8,128)(2,1)}, u32[]{:S(2)}) copy-start(bf16[1024,1024]{1,0:T(8,128)(2,1)} %all-gather.11.cloned.1.call-done) | copy-start | bytes 6291460
  603.3 129.7 %all-gather.17.cloned.1.call-start = ((), (), s32[]{:S(2)}) async-start(), calls=%async_computation.18 | async-start | bytes 5242880 | tf_op jit(solution)/shard_map/all_gather | solution.py:138
  697.1 524.5 %reduce-scatter.39.cloned.1.call-start = ((), (), s32[]{:S(2)}) async-start(), calls=%async_computation.25 | async-start | bytes 2359296
  710.5 22.5 %copy-start.9 = (bf16[2048,256]{0,1:T(8,128)(2,1)S(1)}, bf16[2048,256]{0,1:T(8,128)(2,1)}, u32[]{:S(2)}) copy-start(bf16[2048,256]{0,1:T(8,128)(2,1)} %copy-done.8) | copy-start | bytes 3145732
  710.5 513.0 %reduce-scatter.29.cloned.1.call-start = ((), (), s32[]{:S(2)}) async-start(), calls=%async_computation.20 | async-start | bytes 2359296 | tf_op jit(solution)/shard_map/reduce_scatter | solution.py:311
  720.2 547.6 %reduce-scatter.37.cloned.1.call-start = ((), (), s32[]{:S(2)}) async-start(), calls=%async_computation.24 | async-start | bytes 589824
  721.1 16.4 %copy-start.17 = (bf16[256,1024]{1,0:T(8,128)(2,1)S(1)}, bf16[256,1024]{1,0:T(8,128)(2,1)}, u32[]{:S(2)}) copy-start(bf16[256,1024]{1,0:T(8,128)(2,1)} %all_gather.34) | copy-start | bytes 1572868
  745.9 20.7 %copy-start.3 = (bf16[32,64,4,64]{1,3,2,0:T(8,128)(2,1)}, bf16[32,64,4,64]{1,3,2,0:T(8,128)(2,1)S(1)}, u32[]{:S(2)}) copy-start(bf16[32,64,4,64]{1,3,2,0:T(8,128)(2,1)S(1)} %copy.189) | copy-start | bytes 3145732
  745.9 523.5 %reduce-scatter.31.cloned.1.call-start = ((), (), s32[]{:S(2)}) async-start(), calls=%async_computation.21 | async-start | bytes 589824
  804.4 466.7 %reduce-scatter.35.cloned.1.call-start = ((), (), s32[]{:S(2)}) async-start(), calls=%async_computation.23 | async-start | bytes 589824
  998.8 274.9 %reduce-scatter.33.cloned.1.call-start = ((), (), s32[]{:S(2)}) async-start(), calls=%async_computation.22 | async-start | bytes 589824
  1211.2 135.9 %reduce-scatter.27.cloned.1.call-start = ((), (), s32[]{:S(2)}) async-start(), calls=%async_computation.19 | async-start | bytes 10485760 | tf_op jit(solution)/shard_map/reduce_scatter | solution.py:142
  (23 other events, 118.7 us)
Sparse Core Ops, SparseCore 0:
  10.4 37.7 all-gather.6
  255.4 70.9 reduce-scatter.20
  544.4 35.6 all-gather.14
  603.5 71.7 reduce-scatter.24
Sparse Core Ops, SparseCore 1:
  258.6 48.6 all-gather.10
  340.4 35.9 all-gather.8
  378.4 50.5 all-gather.12
  441.9 69.8 reduce-scatter.22
  697.1 35.9 all-gather.16
  737.0 68.1 reduce-scatter.38
  809.0 66.6 reduce-scatter.28
  879.3 60.8 reduce-scatter.36
  943.4 61.1 reduce-scatter.30
  1008.2 61.0 reduce-scatter.34
  1211.2 62.3 reduce-scatter.32
  1276.4 70.7 reduce-scatter.26
where the time goes:
time: 1370 us; the launch traced here: 1360 us
  waiting for transfers between devices  403 us (29%)
  other arithmetic  380 us (28%)
  blocking collectives  206 us (15%)
  matrix products  204 us (15%)
  local copies, waits for them, and re-layouts  145 us (11%)
  between operations  17.1 us (1%)
    unnamed x5, other arithmetic  313 us
    reduce_scatter x4, waiting for transfers between devices, reduce_cols(): lax.psum_scatter(partial_value, 'col', scatter_dimension=1, tiled=True)  278 us
    all_gather x4, waiting for transfers between devices, spread(): return lax.all_gather(portion, 'col', axis=1, tiled=True)  81.2 us
    all_gather x1, waiting for transfers between devices, on_device(): lax.all_gather(w_down.astype(jnp.bfloat16), 'row', axis=1, tiled=True)  42.1 us
    psum x1, blocking collectives, on_device(): lax.psum((into_full(jnp.sum(query_grad, axis=0, dtype=jnp.float32), feat_...  40.8 us
    psum x4, blocking collectives, col_totals(): return lax.psum((left_sum, right_sum), 'col')  40.7 us
    all_gather x1, blocking collectives, on_device(): lax.all_gather(w_key.astype(jnp.bfloat16), 'row', axis=0, tiled=True)  31.6 us
    all_gather x1, blocking collectives, on_device(): lax.all_gather(w_value.astype(jnp.bfloat16), 'row', axis=0, tiled=True)  31.4 us
  transfers between devices with their start and end apart: 16, of which 9 were waited for; matrix products, arithmetic and copies ran while one was open for 41% of the time, Pallas kernels for 0%

commit v1 on v0

v1 whole, which is shorter than its diff:
```python
import functools
import math

import jax
import jax.numpy as jnp
from jax import lax
from jax.experimental import pallas as pl
from jax.experimental.pallas import tpu as pltpu
from jax.sharding import PartitionSpec as P

DH = 64
BLK = 64


epsilon = 1e-06


def gelu_tanh(values_in):
    return jax.nn.gelu(values_in, approximate=True)


def lane_heads(rows, width):
    return lax.broadcasted_iota(jnp.int32, (rows, width), 1) // DH


def by_diagonal(rows, width):
    lane_head = lane_heads(BLK, width)
    zero = jnp.zeros_like(rows)
    return jnp.concatenate(
        [jnp.where(lane_head == head, rows, zero) for head in range(width // DH)], axis=0
    )


def from_diagonal(square, width):
    lane_head = lane_heads(BLK, width)
    result = jnp.zeros((BLK, width), jnp.float32)
    for head in range(width // DH):
        result = jnp.where(lane_head == head, square[head * BLK : (head + 1) * BLK, :], result)
    return result


def slot_starts(step, num_blocks, head_count, globals_ref, random_ref):
    shared = [
        jnp.maximum(step - 1, 0),
        step,
        jnp.minimum(step + 1, num_blocks - 1),
        globals_ref[0],
        globals_ref[1],
    ]
    base = step * (head_count * 3)
    apart = [
        [random_ref[base + head * 3 + slot] for head in range(head_count)] for slot in range(3)
    ]
    at = lambda block: pl.multiple_of(block * BLK, BLK)
    return [at(block) for block in shared], [[at(block) for block in row] for row in apart]


def lane_groups(head_count):
    per_group = min(128 // DH, head_count)
    return [
        (first * DH, per_group * DH, list(range(first, first + per_group)))
        for first in range(0, head_count, per_group)
    ]


def picked_rows(rows_ref, shared, apart, head_count):
    pieces = [rows_ref[pl.ds(start, BLK), :] for start in shared]
    for starts in apart:
        groups = []
        for lane, width, heads in lane_groups(head_count):
            lane_head = lane_heads(BLK, width)
            piece = rows_ref[pl.ds(starts[heads[0]], BLK), lane : lane + width]
            for place, head in enumerate(heads[1:], 1):
                other = rows_ref[pl.ds(starts[head], BLK), lane : lane + width]
                piece = jnp.where(lane_head >= place, other, piece)
            groups.append(piece)
        pieces.append(jnp.concatenate(groups, axis=1) if len(groups) > 1 else groups[0])
    return jnp.concatenate(pieces, axis=0)


def put_rows(sums_ref, values_in, shared, apart, head_count):
    for slot, start in enumerate(shared):
        sums_ref[pl.ds(start, BLK), :] += values_in[slot * BLK : (slot + 1) * BLK, :]
    for slot, starts in enumerate(apart, len(shared)):
        rows = values_in[slot * BLK : (slot + 1) * BLK, :]
        for lane, width, heads in lane_groups(head_count):
            lane_head = lane_heads(BLK, width)
            for place, head in enumerate(heads):
                sums_ref[pl.ds(starts[head], BLK), lane : lane + width] += jnp.where(
                    lane_head == place, rows[:, lane : lane + width], 0.0
                )


def masked_scores(picked_keys, grouped, limits_ref, step, width):
    scores = lax.dot_general(
        picked_keys, grouped, (((1,), (1,)), ((), ())), preferred_element_type=jnp.float32
    )
    row = lax.broadcasted_iota(jnp.int32, (BLK, width), 0)
    return [
        jnp.where(
            row < limits_ref[step, slot : slot + 1, :],
            scores[slot * BLK : (slot + 1) * BLK, :],
            -1e30,
        )
        for slot in range(8)
    ]


def attend_kernel(
    head_count,
    unroll,
    globals_ref,
    random_ref,
    limits_ref,
    queries_ref,
    keys_ref,
    values_ref,
    context_ref,
    highest_ref,
    scale_ref,
):
    width = head_count * DH
    num_blocks = queries_ref.shape[0] // BLK

    def one_block(step):
        shared, apart = slot_starts(step, num_blocks, head_count, globals_ref, random_ref)
        own = pl.ds(pl.multiple_of(step * BLK, BLK), BLK)
        grouped = by_diagonal(queries_ref[own, :] * jnp.bfloat16(1.0 / math.sqrt(DH)), width)
        scores = masked_scores(
            picked_rows(keys_ref, shared, apart, head_count), grouped, limits_ref, step, width
        )
        highest = jnp.max(functools.reduce(jnp.maximum, scores), axis=0, keepdims=True)
        exponent = [jnp.exp(piece - highest) for piece in scores]
        denominator = jnp.sum(sum(exponent[1:], exponent[0]), axis=0, keepdims=True)
        scale = 1.0 / denominator
        attn_probs = jnp.concatenate(
            [(piece * scale).astype(jnp.bfloat16) for piece in exponent], axis=0
        )
        square = lax.dot_general(
            attn_probs,
            picked_rows(values_ref, shared, apart, head_count),
            (((0,), (0,)), ((), ())),
            preferred_element_type=jnp.float32,
        )
        context_ref[own, :] = from_diagonal(square, width).astype(jnp.bfloat16)
        highest_ref[step] = highest
        scale_ref[step] = scale

    @pl.loop(0, num_blocks // unroll)
    def _(turn):
        for place in range(unroll):
            one_block(turn * unroll + place)


def attend_back_kernel(
    head_count,
    unroll,
    globals_ref,
    random_ref,
    limits_ref,
    queries_ref,
    keys_ref,
    values_ref,
    grads_ref,
    highest_ref,
    scale_ref,
    query_grad_ref,
    key_grad_ref,
    value_grad_ref,
    key_sums,
    value_sums,
):
    width = head_count * DH
    num_blocks = queries_ref.shape[0] // BLK
    factor = 1.0 / math.sqrt(DH)
    key_sums[...] = jnp.zeros_like(key_sums)
    value_sums[...] = jnp.zeros_like(value_sums)

    def one_block(step):
        shared, apart = slot_starts(step, num_blocks, head_count, globals_ref, random_ref)
        own = pl.ds(pl.multiple_of(step * BLK, BLK), BLK)
        grouped = by_diagonal(queries_ref[own, :] * jnp.bfloat16(factor), width)
        grouped_grad = by_diagonal(grads_ref[own, :], width)
        picked_keys = picked_rows(keys_ref, shared, apart, head_count)
        picked_values = picked_rows(values_ref, shared, apart, head_count)
        scores = masked_scores(picked_keys, grouped, limits_ref, step, width)
        highest = highest_ref[step]
        scale = scale_ref[step]
        attn_probs = [jnp.exp(piece - highest) * scale for piece in scores]
        prob_grad = lax.dot_general(
            picked_values,
            grouped_grad,
            (((1,), (1,)), ((), ())),
            preferred_element_type=jnp.float32,
        )
        prob_grads = [prob_grad[slot * BLK : (slot + 1) * BLK, :] for slot in range(8)]
        products = [left * right for left, right in zip(attn_probs, prob_grads)]
        total = jnp.sum(sum(products[1:], products[0]), axis=0, keepdims=True)
        score_grad = jnp.concatenate(
            [
                (left * (right - total)).astype(jnp.bfloat16)
                for left, right in zip(attn_probs, prob_grads)
            ],
            axis=0,
        )
        probs_low = jnp.concatenate([piece.astype(jnp.bfloat16) for piece in attn_probs], axis=0)
        square = lax.dot_general(
            score_grad, picked_keys, (((0,), (0,)), ((), ())), preferred_element_type=jnp.float32
        )
        query_grad_ref[own, :] = (from_diagonal(square, width) * factor).astype(jnp.bfloat16)
        key_part = jnp.dot(score_grad, grouped, preferred_element_type=jnp.float32)
        value_part = jnp.dot(probs_low, grouped_grad, preferred_element_type=jnp.float32)
        put_rows(key_sums, key_part, shared, apart, head_count)
        put_rows(value_sums, value_part, shared, apart, head_count)

    @pl.loop(0, num_blocks // unroll)
    def _(turn):
        for place in range(unroll):
            one_block(turn * unroll + place)

    key_grad_ref[...] = key_sums[...].astype(jnp.bfloat16)
    value_grad_ref[...] = value_sums[...].astype(jnp.bfloat16)


def limits_of(length, global_ids, random_ids, num_blocks, head_count):
    blocks = jnp.arange(num_blocks, dtype=jnp.int32)
    nearby_raw = blocks[:, None] + jnp.arange(-1, 2, dtype=jnp.int32)[None, :]
    near_ok = (nearby_raw >= 0) & (nearby_raw < num_blocks)
    global_rows = jnp.broadcast_to(global_ids[None, :], (num_blocks, 2))
    global_ok = jnp.all(global_rows[:, :, None] != nearby_raw[:, None, :], axis=2)
    common = jnp.concatenate([nearby_raw, global_rows], axis=1)
    common_ok = jnp.concatenate([near_ok, global_ok], axis=1)
    common_limit = jnp.where(common_ok, length - common * BLK, 0)
    random_limit = jnp.transpose(length - random_ids * BLK, (0, 2, 1))
    return jnp.concatenate(
        [
            jnp.broadcast_to(common_limit[:, :, None], (num_blocks, 5, head_count * DH)),
            jnp.repeat(random_limit, DH, axis=2),
        ],
        axis=1,
    )


VMEM = pl.BlockSpec(memory_space=pltpu.VMEM)
SMEM = pl.BlockSpec(memory_space=pltpu.SMEM)


def attend(queries, key_rows, value_rows, tables):
    seq_len, width = queries.shape
    head_count = width // DH
    num_blocks = seq_len // BLK
    stat = jax.ShapeDtypeStruct((num_blocks, 1, width), jnp.float32)
    return pl.pallas_call(
        functools.partial(attend_kernel, head_count, 2),
        out_shape=(jax.ShapeDtypeStruct((seq_len, width), jnp.bfloat16), stat, stat),
        in_specs=[SMEM] * 2 + [VMEM] * 4,
        out_specs=[VMEM] * 3,
        compiler_params=pltpu.CompilerParams(vmem_limit_bytes=32 * 1024 * 1024),
        cost_estimate=pl.CostEstimate(
            flops=4 * seq_len * 512 * width * head_count,
            bytes_accessed=8 * seq_len * width,
            transcendentals=seq_len * 512 * head_count,
        ),
    )(*tables, queries, key_rows, value_rows)


def attend_back(queries, key_rows, value_rows, tables, stats, context_grad):
    seq_len, width = queries.shape
    head_count = width // DH
    grad = jax.ShapeDtypeStruct((seq_len, width), jnp.bfloat16)
    return pl.pallas_call(
        functools.partial(attend_back_kernel, head_count, 2),
        out_shape=(grad, grad, grad),
        in_specs=[SMEM] * 2 + [VMEM] * 7,
        out_specs=[VMEM] * 3,
        scratch_shapes=[pltpu.VMEM((seq_len, width), jnp.float32)] * 2,
        compiler_params=pltpu.CompilerParams(vmem_limit_bytes=40 * 1024 * 1024),
        cost_estimate=pl.CostEstimate(
            flops=10 * seq_len * 512 * width * head_count,
            bytes_accessed=14 * seq_len * width,
            transcendentals=seq_len * 512 * head_count,
        ),
    )(*tables, queries, key_rows, value_rows, context_grad, *stats)


def spread(portion):
    return lax.all_gather(portion, "col", axis=0, tiled=True)


def reduce_tokens(partial_value):
    return lax.psum_scatter(
        partial_value.astype(jnp.bfloat16), "col", scatter_dimension=0, tiled=True
    ).astype(jnp.float32)


def to_tokens(portion):
    return lax.all_to_all(portion, "col", split_axis=0, concat_axis=1, tiled=True)


def to_features(portion):
    return lax.all_to_all(portion, "col", split_axis=1, concat_axis=0, tiled=True)


def layer_norm(summed, gain_vec, offset_vec):
    average = jnp.mean(summed, axis=1, keepdims=True)
    squares = jnp.mean(summed * summed, axis=1, keepdims=True)
    inv_std = lax.rsqrt(squares - average * average + epsilon)
    normed = (summed - average) * inv_std
    return (normed * gain_vec + offset_vec, normed, inv_std)


def norm_back(upstream, normed, inv_std, gain_vec):
    scaled = upstream * gain_vec
    left = jnp.mean(scaled, axis=1, keepdims=True)
    right = jnp.mean(scaled * normed, axis=1, keepdims=True)
    result = inv_std * (scaled - left - normed * right)
    return (result, jnp.sum(upstream * normed, axis=0), jnp.sum(upstream, axis=0))


def into_full(portion, start_at, full_len):
    return lax.dynamic_update_slice_in_dim(
        jnp.zeros((full_len,), jnp.float32), portion, start_at, 0
    )


def dot(left, right):
    return jnp.dot(left, right, preferred_element_type=jnp.float32)


def dot_nt(left, right):
    return lax.dot_general(
        left, right, (((1,), (1,)), ((), ())), preferred_element_type=jnp.float32
    )


def dot_tn(left, right):
    return lax.dot_general(
        left, right, (((0,), (0,)), ((), ())), preferred_element_type=jnp.float32
    )


def on_device(
    hidden_in,
    out_grad,
    lengths,
    global_blocks,
    rand_blocks,
    w_query,
    b_query,
    w_key,
    w_value,
    b_value,
    w_out,
    b_out,
    ln1_gain,
    ln1_bias,
    w_up,
    b_up,
    w_down,
    b_down,
    ln2_gain,
    ln2_bias,
):
    low = jnp.bfloat16
    seq_len = hidden_in.shape[0]
    feat_cols = hidden_in.shape[1]
    unit_cols = w_up.shape[1]
    cols = lax.axis_size("col")
    features_all = feat_cols * cols
    units_all = unit_cols * cols
    num_blocks = seq_len // BLK
    head_count = feat_cols // DH
    own_len = seq_len // cols
    column = lax.axis_index("col")
    feat_start = column * feat_cols
    unit_start = column * unit_cols
    own_start = column * own_len
    length = lengths[0]
    tables = (
        global_blocks.reshape(-1),
        rand_blocks.reshape(-1),
        limits_of(length, global_blocks[0], rand_blocks[0], num_blocks, head_count),
    )
    full_qkv = lax.all_gather(
        jnp.concatenate([w_query.astype(low), w_key.astype(low), w_value.astype(low)], axis=1),
        "row",
        axis=0,
        tiled=True,
    )
    features = lax.all_gather(hidden_in, "col", axis=1, tiled=True)
    full_out = lax.all_gather(w_out.astype(low).T, "row", axis=0, tiled=True)
    full_up = lax.all_gather(w_up.astype(low), "row", axis=0, tiled=True)
    full_down = lax.all_gather(w_down.astype(low).T, "row", axis=0, tiled=True)
    own_features = lax.dynamic_slice_in_dim(features, own_start, own_len, 0).astype(jnp.float32)
    own_valid = (own_start + jnp.arange(own_len) < length)[:, None]
    upstream = jnp.where(own_valid, to_tokens(out_grad).astype(jnp.float32), 0.0)

    full_query = full_qkv[:, :feat_cols]
    full_key = full_qkv[:, feat_cols : 2 * feat_cols]
    full_value = full_qkv[:, 2 * feat_cols :]
    queries = (
        dot(features, full_query) + lax.dynamic_slice_in_dim(b_query, feat_start, feat_cols)
    ).astype(low)
    key_rows = dot(features, full_key).astype(low)
    value_rows = (
        dot(features, full_value) + lax.dynamic_slice_in_dim(b_value, feat_start, feat_cols)
    ).astype(low)
    context, *stats = attend(queries, key_rows, value_rows, tables)

    summed1 = own_features + reduce_tokens(dot_nt(context, full_out)) + b_out
    normed1, unit1, inv_std1 = layer_norm(summed1, ln1_gain, ln1_bias)
    normed1_full = spread(normed1.astype(low))
    pre_act = dot(normed1_full, full_up) + lax.dynamic_slice_in_dim(b_up, unit_start, unit_cols)
    activated, gelu_back = jax.vjp(gelu_tanh, pre_act)
    hidden = activated.astype(low)
    summed2 = normed1 + reduce_tokens(dot_nt(hidden, full_down)) + b_down
    normed2, unit2, inv_std2 = layer_norm(summed2, ln2_gain, ln2_bias)
    layer_out = to_features(jnp.where(own_valid, normed2, 0.0).astype(low))

    ffn_grad, gain2_grad, shift2_grad = norm_back(upstream, unit2, inv_std2, ln2_gain)
    ffn_low = ffn_grad.astype(low)
    ffn_full = spread(ffn_low)
    pre_grad = gelu_back(dot(ffn_full, full_down))[0].astype(low)
    normed1_grad = ffn_grad + reduce_tokens(dot_nt(pre_grad, full_up))
    grad_down = dot_tn(ffn_full, hidden)
    grad_up = dot_tn(normed1_full, pre_grad)
    attn_grad, gain1_grad, shift1_grad = norm_back(normed1_grad, unit1, inv_std1, ln1_gain)
    attn_low = attn_grad.astype(low)
    attn_full = spread(attn_low)
    context_grad = dot(attn_full, full_out).astype(low)
    grad_out = dot_tn(attn_full, context)
    query_grad, key_grad, value_grad = attend_back(
        queries, key_rows, value_rows, tables, stats, context_grad
    )
    input_part = (
        dot_nt(query_grad, full_query) + dot_nt(key_grad, full_key) + dot_nt(value_grad, full_value)
    )
    own_part = lax.dynamic_slice_in_dim(input_part, own_start, own_len, 0) + attn_grad
    input_part = lax.dynamic_update_slice_in_dim(input_part, own_part, own_start, 0)
    grad_input = lax.psum_scatter(
        input_part.astype(low), "col", scatter_dimension=1, tiled=True
    )
    grad_qkv = dot_tn(features, jnp.concatenate([query_grad, key_grad, value_grad], axis=1))

    def reduce_rows(partial_value):
        return lax.psum_scatter(
            partial_value.astype(low), "row", scatter_dimension=0, tiled=True
        ).astype(jnp.float32)

    down_share = reduce_rows(grad_down).T
    up_share = reduce_rows(grad_up)
    out_share = reduce_rows(grad_out).T
    qkv_share = reduce_rows(grad_qkv)
    small_grads = lax.psum(
        (
            into_full(jnp.sum(query_grad, axis=0, dtype=jnp.float32), feat_start, features_all),
            into_full(jnp.sum(value_grad, axis=0, dtype=jnp.float32), feat_start, features_all),
            jnp.sum(attn_low, axis=0, dtype=jnp.float32),
            gain1_grad,
            shift1_grad,
            into_full(jnp.sum(pre_grad, axis=0, dtype=jnp.float32), unit_start, units_all),
            jnp.sum(ffn_low, axis=0, dtype=jnp.float32),
            gain2_grad,
            shift2_grad,
        ),
        ("row", "col"),
    )
    return (
        layer_out,
        grad_input,
        qkv_share[:, :feat_cols],
        small_grads[0],
        qkv_share[:, feat_cols : 2 * feat_cols],
        qkv_share[:, 2 * feat_cols :],
        small_grads[1],
        out_share,
        small_grads[2],
        small_grads[3],
        small_grads[4],
        up_share,
        small_grads[5],
        down_share,
        small_grads[6],
        small_grads[7],
        small_grads[8],
    )


def solution(mesh):
    placed = (
        P("row", "col"),
        P("row", "col"),
        P("row"),
        P("row", None),
        P("row", None, "col", None),
        P("row", "col"),
        P(),
        P("row", "col"),
        P("row", "col"),
        P(),
        P("col", "row"),
        P(),
        P(),
        P(),
        P("row", "col"),
        P(),
        P("col", "row"),
        P(),
        P(),
        P(),
    )
    return jax.shard_map(
        on_device,
        mesh=mesh,
        in_specs=placed,
        out_specs=(
            P("row", "col"),
            P("row", "col"),
            P("row", "col"),
            P(),
            P("row", "col"),
            P("row", "col"),
            P(),
            P("col", "row"),
            P(),
            P(),
            P(),
            P("row", "col"),
            P(),
            P("col", "row"),
            P(),
            P(),
            P(),
        ),
        check_vma=False,
    )
```

time: 1370 us -> 852 us (0.62)
  other arithmetic: 380 us -> 34.7 us
  waiting for transfers between devices: 403 us -> 554 us
  blocking collectives: 206 us -> 71.9 us
  local copies, waits for them, and re-layouts: 145 us -> 20.5 us
  matrix products: 204 us -> 92.2 us
  Pallas kernels: 0 us -> 46.4 us
    unnamed x5 -> x1, other arithmetic: 313 us -> 0.18 us
    all_gather x6 -> x7, waiting for transfers between devices: 123 us -> 221 us  [the longest x3 83.4 us: spread(): return lax.all_gather(portion, 'col', axis=0, tiled=True)]
    dot_general x23 -> x16, matrix products: 187 us -> 92.2 us  [the longest x6 34.4 us: dot(): return jnp.dot(left, right, preferred_element_type=jnp.float32)]
    all_gather x4 -> x1, blocking collectives: 125 us -> 30.9 us  [on_device(): full_out = lax.all_gather(w_out.astype(low).T, 'row', axis=0, tiled=True)]
    unnamed x21 -> x16, waiting for transfers between devices: 1.73 us -> 66.6 us
    pallas_call x0 -> x2, Pallas kernels: none -> 46.4 us  [the longest x1 26.2 us: attend_back(): pl.pallas_call(functools.partial(attend_back_kernel, head_count, 2), out_...]
    reshape x7 -> x3, local copies, waits for them, and re-layouts: 41.3 us -> 0.45 us  [the longest x2 0.24 us: limits_of(): jnp.repeat(random_limit, DH, axis=2)]
    psum x4 -> x0, blocking collectives: 40.7 us -> none  [col_totals(): return lax.psum((left_sum, right_sum), 'col')]
  transfers between devices with their start and end apart: 16 -> 17, of which waited for: 9 -> 16; matrix products, arithmetic and copies ran while one was open for 41% -> 10% of each run, Pallas kernels for 0% -> 3%
where the time goes in v1:
time: 852 us; the launch traced here: 844 us
  waiting for transfers between devices  554 us (65%)
  matrix products  92.2 us (11%)
  blocking collectives  71.9 us (8%)
  Pallas kernels  46.4 us (5%)
  other arithmetic  34.7 us (4%)
  local copies, waits for them, and re-layouts  20.5 us (2%)
  between operations  15.4 us (2%)
  starting transfers between devices  9.15 us (1%)
    reduce_scatter x3, waiting for transfers between devices, reduce_tokens(): lax.psum_scatter(partial_value.astype(jnp.bfloat16), 'col', scatter_dimen...  110 us
    reduce_scatter x3, waiting for transfers between devices, reduce_rows(): lax.psum_scatter(partial_value.astype(low), 'row', scatter_dimension=0, t...  84.6 us
    all_gather x3, waiting for transfers between devices, spread(): return lax.all_gather(portion, 'col', axis=0, tiled=True)  83.4 us
    unnamed x16, waiting for transfers between devices  66.6 us
    all_gather x1, waiting for transfers between devices, on_device(): full_up = lax.all_gather(w_up.astype(low), 'row', axis=0, tiled=True)  44.9 us
    all_gather x1, waiting for transfers between devices, on_device(): full_down = lax.all_gather(w_down.astype(low).T, 'row', axis=0, tiled=True)  43.2 us
    reduce_scatter x1, waiting for transfers between devices, on_device(): lax.psum_scatter(input_part.astype(low), 'col', scatter_dimension=1, tile...  43.1 us
    psum x1, blocking collectives, on_device(): lax.psum((into_full(jnp.sum(query_grad, axis=0, dtype=jnp.float32), feat_...  40.9 us
  transfers between devices with their start and end apart: 17, of which 16 were waited for; matrix products, arithmetic and copies ran while one was open for 10% of the time, Pallas kernels for 3%

profile of v1, /device:TPU:0, one launch (start us, length us, event | category | flops | bytes accessed | tf_op | source)
XLA Modules:
  0.0 844.3 jit_solution(7403202448228346784)
XLA Ops:
  15.3 30.9 %all_gather.26 = bf16[1024,256]{0,1:T(8,128)(2,1)S(1)} all-gather(bf16[128,256]{0,1:T(8,128)(2,1)S(1)} %convert_bitcast_fusion.4), channel_id=1, replica_groups=mesh['row'=8,'col'=4] {'row'}, dimensions={0}, use_global_device_ids=true | all-gather | bytes 589824 | tf_op jit(solution)/shard_map/all_gather | solution.py:391
  46.2 14.4 %all-gather.10.cloned.1.call-done = bf16[1024,768]{1,0:T(8,128)(2,1)} async-done(((bf16[128,768]{1,0:T(8,128)(2,1)}), bf16[1024,768]{1,0:T(8,128)(2,1)}) %all-gather.10.cloned.1.call-update) | async-done | bytes 1572880 | tf_op jit(solution)/shard_map/all_gather | solution.py:384
  60.6 35.5 %all-gather.8.cloned.1.call-done = bf16[2048,1024]{1,0:T(8,128)(2,1)} async-done(((bf16[2048,256]{1,0:T(8,128)(2,1)}), bf16[2048,1024]{1,0:T(8,128)(2,1)}) %all-gather.8.cloned.1.call-update) | async-done | bytes 4194320 | tf_op jit(solution)/shard_map/all_gather | solution.py:390
  102.5 20.2 %shard_map.323 = (bf16[2048,256]{1,0:T(8,128)(2,1)S(1)}, f32[32,1,256]{2,1,0:T(1,128)S(1)}, f32[32,1,256]{2,1,0:T(1,128)S(1)}) custom-call(s32[2]{0:T(128)S(1)} %bitcast.75, s32[384]{0:T(512)S(1)} %reshape.204.random_ref, s32[32,8,256]{2,1,0:T(8,128)S(1)} %pad_add_fusion.limits_ref, bf16[2048,256]{1,0:T(8,128)(2,1)S(1)} %fusion.17.queries_ref, ...), custom_call_target="tpu_custom_call" | custom-call | flops 4294967296 | bytes 4194304 | tf_op jit(solution)/shard_map/pallas_call | solution.py:253
  127.8 42.8 %reduce-scatter.11.cloned.1.call-done = bf16[512,1024]{1,0:T(8,128)(2,1)} async-done(((bf16[2048,1024]{1,0:T(8,128)(2,1)}), bf16[512,1024]{1,0:T(8,128)(2,1)}) %reduce-scatter.11.cloned.1.call-update) | async-done | bytes 1048592 | tf_op jit(solution)/shard_map/reduce_scatter | solution.py:291
  177.8 44.9 %all-gather.14.cloned.1.call-done = bf16[1024,1024]{1,0:T(8,128)(2,1)} async-done(((bf16[128,1024]{1,0:T(8,128)(2,1)}), bf16[1024,1024]{1,0:T(8,128)(2,1)}) %all-gather.14.cloned.1.call-update) | async-done | bytes 2097168 | tf_op jit(solution)/shard_map/all_gather | solution.py:392
  222.7 35.1 %all-gather.12.cloned.1.call-done = bf16[2048,1024]{1,0:T(8,128)(2,1)} async-done(((bf16[512,1024]{1,0:T(8,128)(2,1)}), bf16[2048,1024]{1,0:T(8,128)(2,1)}) %all-gather.12.cloned.1.call-update) | async-done | bytes 4194320 | tf_op jit(solution)/shard_map/all_gather | solution.py:287
  257.7 10.6 %fusion.45 = f32[2048,1024]{1,0:T(8,128)} fusion(bf16[2048,1024]{1,0:T(8,128)(2,1)} %all-gather.12.cloned.1.call-done, bf16[1024,1024]{1,0:T(8,128)(2,1)} %all-gather.14.cloned.1.call-done), kind=kOutput, calls=%fused_computation.100 | convolution fusion | flops 4294967296 | bytes 14680064 | tf_op jit(solution)/shard_map/dot_general | solution.py:327
  268.3 43.2 %all-gather.16.cloned.1.call-done = bf16[1024,1024]{0,1:T(8,128)(2,1)} async-done(((bf16[128,1024]{0,1:T(8,128)(2,1)}), bf16[1024,1024]{0,1:T(8,128)(2,1)}) %all-gather.16.cloned.1.call-update) | async-done | bytes 2097168 | tf_op jit(solution)/shard_map/all_gather | solution.py:393
  311.5 11.7 %convolution_convert_fusion.2 = bf16[2048,1024]{1,0:T(8,128)(2,1)} fusion(bf16[1024,1024]{0,1:T(8,128)(2,1)} %all-gather.16.cloned.1.call-done, f32[2048,1024]{1,0:T(8,128)} %fusion.45, f32[1024]{0:T(1024)S(1)} %dynamic_slice.18), kind=kOutput, calls=%fused_computation.14 | convolution fusion | flops 4318035968 | bytes 14684160 | tf_op jit(solution)/shard_map/dot_general | solution.py:331
  327.1 14.2 %all-to-all-done.1 = bf16[4,512,256]{2,1,0:T(8,128)(2,1)S(1)} async-done(((bf16[4,512,256]{2,1,0:T(8,128)(2,1)}), bf16[4,512,256]{2,1,0:T(8,128)(2,1)S(1)}, u32[]{:S(2)}, u32[]{:S(2)}) %all-to-all-start.1) | async-done | bytes 1048608 | tf_op jit(solution)/shard_map/all_to_all | solution.py:297
  343.5 22.6 %reduce-scatter.13.cloned.1.call-done = bf16[512,1024]{1,0:T(8,128)(2,1)} async-done(((bf16[2048,1024]{1,0:T(8,128)(2,1)}), bf16[512,1024]{1,0:T(8,128)(2,1)}) %reduce-scatter.13.cloned.1.call-update) | async-done | bytes 1048592 | tf_op jit(solution)/shard_map/reduce_scatter | solution.py:291
  372.6 34.6 %all-gather.18.cloned.1.call-done = bf16[2048,1024]{1,0:T(8,128)(2,1)} async-done(((bf16[512,1024]{1,0:T(8,128)(2,1)}), bf16[2048,1024]{1,0:T(8,128)(2,1)}) %all-gather.18.cloned.1.call-update) | async-done | bytes 4194320 | tf_op jit(solution)/shard_map/all_gather | solution.py:287
  407.2 13.8 %convert_reduce_fusion = (f32[1024]{0:T(1024)S(1)}, bf16[2048,1024]{1,0:T(8,128)(2,1)S(1)}) fusion(f32[2048,1024]{1,0:T(8,128)} %fusion.45, f32[1024]{0:T(1024)S(1)} %dynamic_slice.18, bf16[2048,1024]{1,0:T(8,128)(2,1)} %all-gather.18.cloned.1.call-done, bf16[1024,1024]{0,1:T(8,128)(2,1)} %all-gather.16.cloned.1.call-done), kind=kOutput, calls=%fused_computation.9 | convolution fusion | flops 4343200768 | bytes 18882560 | tf_op jit(solution)/shard_map/dot_general | solution.py:327
  429.5 44.4 %reduce-scatter.15.cloned.1.call-done = bf16[512,1024]{1,0:T(8,128)(2,1)} async-done(((bf16[2048,1024]{1,0:T(8,128)(2,1)}), bf16[512,1024]{1,0:T(8,128)(2,1)}) %reduce-scatter.15.cloned.1.call-update) | async-done | bytes 1048592 | tf_op jit(solution)/shard_map/reduce_scatter | solution.py:291
  481.5 10.9 %convolution_convert_fusion.5 = bf16[1024,1024]{1,0:T(8,128)(2,1)} fusion(bf16[2048,1024]{1,0:T(8,128)(2,1)} %all-gather.18.cloned.1.call-done, f32[2048,1024]{1,0:T(8,128)} %fusion.45, f32[1024]{0:T(1024)S(1)} %dynamic_slice.18), kind=kOutput, calls=%fused_computation.56 | convolution fusion | flops 4316987392 | bytes 14684160 | tf_op jit(solution)/shard_map/dot_general | solution.py:337
  502.3 13.8 %all-gather.20.cloned.1.call-done = bf16[2048,1024]{1,0:T(8,128)(2,1)} async-done(((bf16[512,1024]{1,0:T(8,128)(2,1)}), bf16[2048,1024]{1,0:T(8,128)(2,1)}) %all-gather.20.cloned.1.call-update) | async-done | bytes 4194320 | tf_op jit(solution)/shard_map/all_gather | solution.py:287
  524.2 26.2 %shard_map.324 = (bf16[2048,256]{1,0:T(8,128)(2,1)S(1)}, bf16[2048,256]{1,0:T(8,128)(2,1)S(1)}, bf16[2048,256]{1,0:T(8,128)(2,1)S(1)}) custom-call(s32[2]{0:T(128)S(1)} %bitcast.76, s32[384]{0:T(512)S(1)} %reshape.204.random_ref, s32[32,8,256]{2,1,0:T(8,128)S(1)} %pad_add_fusion.limits_ref, bf16[2048,256]{1,0:T(8,128)(2,1)S(1)} %copy-done.6, ...), custom_call_target="tpu_custom_call" | custom-call | flops 10737418240 | bytes 7340032 | tf_op jit(solution)/shard_map/pallas_call | solution.py:271
  575.9 14.4 %all-to-all-done = bf16[512,4,256]{2,0,1:T(8,128)(2,1)S(1)} async-done(((bf16[512,4,256]{2,0,1:T(8,128)(2,1)}), bf16[512,4,256]{2,0,1:T(8,128)(2,1)S(1)}, u32[]{:S(2)}, u32[]{:S(2)}) %all-to-all-start) | async-done | bytes 1048608 | tf_op jit(solution)/shard_map/all_to_all | solution.py:301
  594.3 63.9 %reduce-scatter.21.cloned.1.call-done = bf16[128,1024]{1,0:T(8,128)(2,1)} async-done(((bf16[1024,1024]{1,0:T(8,128)(2,1)}), bf16[128,1024]{1,0:T(8,128)(2,1)}) %reduce-scatter.21.cloned.1.call-update) | async-done | bytes 262160 | tf_op jit(solution)/shard_map/reduce_scatter | solution.py:446
  661.1 40.9 %all-reduce = (f32[1024]{0:T(1024)}, f32[1024]{0:T(1024)}, f32[1024]{0:T(1024)}, f32[1024]{0:T(1024)}, f32[1024]{0:T(1024)}, /*index=5*/f32[4096]{0:T(1024)}, f32[1024]{0:T(1024)}, f32[1024]{0:T(1024)}, f32[1024]{0:T(1024)}) all-reduce(f32[1024]{0:T(1024)S(1)} %dynamic_update_slice.13, ...), channel_id=1, replica_groups=mesh['row'=8,'col'=4] {'row','col'}, use_global_device_ids=true, to_apply=%region_15.16 | all-reduce | flops 12288 | bytes 98304 | tf_op jit(solution)/shard_map/psum | solution.py:454
  702.0 20.7 %reduce-scatter.19.cloned.1.call-done = bf16[128,256]{1,0:T(8,128)(2,1)} async-done(((bf16[1024,256]{1,0:T(8,128)(2,1)}), bf16[128,256]{1,0:T(8,128)(2,1)}) %reduce-scatter.19.cloned.1.call-update) | async-done | bytes 65552 | tf_op jit(solution)/shard_map/reduce_scatter | solution.py:446
  724.3 65.7 %reduce-scatter.25.cloned.1.call-done = bf16[128,768]{1,0:T(8,128)(2,1)} async-done(((bf16[1024,768]{1,0:T(8,128)(2,1)}), bf16[128,768]{1,0:T(8,128)(2,1)}) %reduce-scatter.25.cloned.1.call-update) | async-done | bytes 196624
  793.4 43.1 %reduce-scatter.17.cloned.1.call-done = bf16[2048,256]{1,0:T(8,128)(2,1)} async-done(((bf16[2048,1024]{1,0:T(8,128)(2,1)}), bf16[2048,256]{1,0:T(8,128)(2,1)}) %reduce-scatter.17.cloned.1.call-update) | async-done | bytes 1048592 | tf_op jit(solution)/shard_map/reduce_scatter | solution.py:440
  (170 shorter events, 110.5 us)
Async XLA Ops:
  7.2 53.4 %all-gather.10.cloned.1.call-start = ((), (), s32[]{:S(2)}) async-start(), calls=%async_computation.11 | async-start | bytes 1769472 | tf_op jit(solution)/shard_map/all_gather | solution.py:384
  10.8 85.3 %all-gather.8.cloned.1.call-start = ((), (), s32[]{:S(2)}) async-start(), calls=%async_computation.10 | async-start | bytes 5242880 | tf_op jit(solution)/shard_map/all_gather | solution.py:390
  11.5 159.1 %reduce-scatter.11.cloned.1.call-start = ((), (), s32[]{:S(2)}) async-start(), calls=%async_computation.12 | async-start | bytes 5242880 | tf_op jit(solution)/shard_map/reduce_scatter | solution.py:291
  46.2 76.5 %copy-start.14 = (bf16[1024,256]{0,1:T(8,128)(2,1)}, bf16[1024,256]{0,1:T(8,128)(2,1)S(1)}, u32[]{:S(2)}) copy-start(bf16[1024,256]{0,1:T(8,128)(2,1)S(1)} %all_gather.26) | copy-start | bytes 1572868
  60.6 39.2 %copy-start.16 = (bf16[1024,768]{1,0:T(8,128)(2,1)S(1)}, bf16[1024,768]{1,0:T(8,128)(2,1)}, u32[]{:S(2)}) copy-start(bf16[1024,768]{1,0:T(8,128)(2,1)} %all-gather.10.cloned.1.call-done) | copy-start | bytes 4718596
  125.9 44.7 %copy-start.20 = (f32[1024]{0:T(1024)S(1)}, f32[1024]{0:T(1024)}, u32[]{:S(2)}) copy-start(f32[1024]{0:T(1024)} %param.31) | copy-start | bytes 12292
  125.9 46.9 %copy-start.21 = (f32[1024]{0:T(1024)S(1)}, f32[1024]{0:T(1024)}, u32[]{:S(2)}) copy-start(f32[1024]{0:T(1024)} %param.32) | copy-start | bytes 12292
  125.9 46.9 %copy-start.24 = (f32[1024]{0:T(1024)S(1)}, f32[1024]{0:T(1024)}, u32[]{:S(2)}) copy-start(f32[1024]{0:T(1024)} %param.33) | copy-start | bytes 12292
  125.9 96.7 %all-gather.14.cloned.1.call-start = ((), (), s32[]{:S(2)}) async-start(), calls=%async_computation.14 | async-start | bytes 2359296 | tf_op jit(solution)/shard_map/all_gather | solution.py:392
  127.7 130.0 %all-gather.12.cloned.1.call-start = ((), (), s32[]{:S(2)}) async-start(), calls=%async_computation.13 | async-start | bytes 5242880 | tf_op jit(solution)/shard_map/all_gather | solution.py:287
  175.7 135.8 %all-gather.16.cloned.1.call-start = ((), (), s32[]{:S(2)}) async-start(), calls=%async_computation.15 | async-start | bytes 2359296 | tf_op jit(solution)/shard_map/all_gather | solution.py:393
  176.5 189.6 %reduce-scatter.13.cloned.1.call-start = ((), (), s32[]{:S(2)}) async-start(), calls=%async_computation.16 | async-start | bytes 5242880 | tf_op jit(solution)/shard_map/reduce_scatter | solution.py:291
  323.3 18.0 %all-to-all-start.1 = ((bf16[4,512,256]{2,1,0:T(8,128)(2,1)}), bf16[4,512,256]{2,1,0:T(8,128)(2,1)S(1)}, u32[]{:S(2)}, u32[]{:S(2)}) async-start(bf16[4,512,256]{2,1,0:T(8,128)(2,1)} %bitcast.82), calls=%async_computation.3 | async-start | bytes 2097152 | tf_op jit(solution)/shard_map/all_to_all | solution.py:297
  326.8 80.3 %all-gather.18.cloned.1.call-start = ((), (), s32[]{:S(2)}) async-start(), calls=%async_computation.17 | async-start | bytes 5242880 | tf_op jit(solution)/shard_map/all_gather | solution.py:287
  341.4 24.7 %copy-start.26 = (f32[1024]{0:T(1024)S(1)}, f32[1024]{0:T(1024)}, u32[]{:S(2)}) copy-start(f32[1024]{0:T(1024)} %param.37) | copy-start | bytes 12292
  372.5 101.4 %reduce-scatter.15.cloned.1.call-start = ((), (), s32[]{:S(2)}) async-start(), calls=%async_computation.18 | async-start | bytes 5242880 | tf_op jit(solution)/shard_map/reduce_scatter | solution.py:291
  429.2 86.9 %all-gather.20.cloned.1.call-start = ((), (), s32[]{:S(2)}) async-start(), calls=%async_computation.19 | async-start | bytes 5242880 | tf_op jit(solution)/shard_map/all_gather | solution.py:287
  481.4 109.0 %reduce-scatter.23.cloned.1.call-start = ((), (), s32[]{:S(2)}) async-start(), calls=%async_computation.23 | async-start | bytes 2359296 | tf_op jit(solution)/shard_map/reduce_scatter | solution.py:446
  492.4 165.8 %reduce-scatter.21.cloned.1.call-start = ((), (), s32[]{:S(2)}) async-start(), calls=%async_computation.22 | async-start | bytes 2359296 | tf_op jit(solution)/shard_map/reduce_scatter | solution.py:446
  501.8 220.9 %reduce-scatter.19.cloned.1.call-start = ((), (), s32[]{:S(2)}) async-start(), calls=%async_computation.21 | async-start | bytes 589824 | tf_op jit(solution)/shard_map/reduce_scatter | solution.py:446
  520.4 269.6 %reduce-scatter.25.cloned.1.call-start = ((), (), s32[]{:S(2)}) async-start(), calls=%async_computation.24 | async-start | bytes 1769472
  524.2 26.2 %copy-start.11 = (bf16[2048,1024]{1,0:T(8,128)(2,1)S(1)}, bf16[2048,1024]{1,0:T(8,128)(2,1)}, u32[]{:S(2)}) copy-start(bf16[2048,1024]{1,0:T(8,128)(2,1)} %all-gather.8.cloned.1.call-done) | copy-start | bytes 12582916
  558.0 278.6 %reduce-scatter.17.cloned.1.call-start = ((), (), s32[]{:S(2)}) async-start(), calls=%async_computation.20 | async-start | bytes 5242880 | tf_op jit(solution)/shard_map/reduce_scatter | solution.py:440
  572.2 18.1 %all-to-all-start = ((bf16[512,4,256]{2,0,1:T(8,128)(2,1)}), bf16[512,4,256]{2,0,1:T(8,128)(2,1)S(1)}, u32[]{:S(2)}, u32[]{:S(2)}) async-start(bf16[512,4,256]{2,0,1:T(8,128)(2,1)} %bitcast.80), calls=%async_computation.2 | async-start | bytes 2097152 | tf_op jit(solution)/shard_map/all_to_all | solution.py:301
  (22 other events, 117.6 us)
Sparse Core Ops, SparseCore 0:
  10.9 49.6 all-gather.9
  62.1 33.8 all-gather.7
  126.0 44.4 reduce-scatter.10
  173.4 49.2 all-gather.13
  224.7 32.9 all-gather.11
  260.4 51.0 all-gather.15
  323.4 42.6 reduce-scatter.12
  372.6 34.4 all-gather.17
  429.3 44.5 reduce-scatter.14
  481.6 34.4 all-gather.19
  520.0 67.5 reduce-scatter.22
  591.4 66.7 reduce-scatter.20
  661.9 60.7 reduce-scatter.18
  726.0 63.9 reduce-scatter.24
  793.1 43.3 reduce-scatter.16

commit v2 on v1

--- a/solution.py
+++ b/solution.py
@@ -10,13 +10,10 @@
 
 DH = 64
 BLK = 64
+MESH = pl.DeviceIdType.MESH
 
 
 epsilon = 1e-06
-
-
-def gelu_tanh(values_in):
-    return jax.nn.gelu(values_in, approximate=True)
 
 
 def lane_heads(rows, width):
@@ -283,59 +280,459 @@
     )(*tables, queries, key_rows, value_rows, context_grad, *stats)
 
 
-def spread(portion):
-    return lax.all_gather(portion, "col", axis=0, tiled=True)
-
-
-def reduce_tokens(partial_value):
-    return lax.psum_scatter(
-        partial_value.astype(jnp.bfloat16), "col", scatter_dimension=0, tiled=True
-    ).astype(jnp.float32)
-
-
-def to_tokens(portion):
-    return lax.all_to_all(portion, "col", split_axis=0, concat_axis=1, tiled=True)
-
-
-def to_features(portion):
-    return lax.all_to_all(portion, "col", split_axis=1, concat_axis=0, tiled=True)
-
-
-def layer_norm(summed, gain_vec, offset_vec):
+def dot(left, right):
+    return jnp.dot(left, right, preferred_element_type=jnp.float32)
+
+
+def dot_nt(left, right):
+    return lax.dot_general(
+        left, right, (((1,), (1,)), ((), ())), preferred_element_type=jnp.float32
+    )
+
+
+def dot_tn(left, right):
+    return lax.dot_general(
+        left, right, (((0,), (0,)), ((), ())), preferred_element_type=jnp.float32
+    )
+
+
+def gelu_parts(values_in):
+    factor = math.sqrt(2.0 / math.pi)
+    square = values_in * values_in
+    bent = jnp.tanh(factor * (values_in + 0.044715 * (values_in * square)))
+    half = 0.5 * (1.0 + bent)
+    slope = half + (0.5 * values_in) * (1.0 - bent * bent) * (
+        factor + (3.0 * 0.044715 * factor) * square
+    )
+    return (values_in * half, slope)
+
+
+def norm_parts(summed):
     average = jnp.mean(summed, axis=1, keepdims=True)
     squares = jnp.mean(summed * summed, axis=1, keepdims=True)
     inv_std = lax.rsqrt(squares - average * average + epsilon)
-    normed = (summed - average) * inv_std
-    return (normed * gain_vec + offset_vec, normed, inv_std)
+    return ((summed - average) * inv_std, inv_std)
 
 
 def norm_back(upstream, normed, inv_std, gain_vec):
     scaled = upstream * gain_vec
     left = jnp.mean(scaled, axis=1, keepdims=True)
     right = jnp.mean(scaled * normed, axis=1, keepdims=True)
-    result = inv_std * (scaled - left - normed * right)
-    return (result, jnp.sum(upstream * normed, axis=0), jnp.sum(upstream, axis=0))
+    return inv_std * (scaled - left - normed * right)
+
+
+CHUNKS = 4
+
+
+def middle_kernel(
+    levels,
+    context_ref,
+    inputs_ref,
+    upstream_ref,
+    out_ref,
+    up_ref,
+    down_ref,
+    vectors_ref,
+    b_up_ref,
+    layer_out_ref,
+    context_grad_ref,
+    attn_full,
+    small_ref,
+    up_small_ref,
+    grad_up_ref,
+    grad_down_ref,
+    grad_out_ref,
+    context_sib,
+    out_sib,
+    up_sib,
+    down_sib,
+    normed_full,
+    ffn_full,
+    hidden,
+    slope,
+    pre_grad,
+    unit1,
+    inv1,
+    ffn_keep,
+    part_own,
+    send_buf,
+    recv_buf,
+    context_send,
+    stage,
+    stage_small,
+    send_sem,
+    recv_sem,
+    core_send,
+    core_recv,
+    stage_sem,
+):
+    low = jnp.bfloat16
+    row, column = lax.axis_index("row"), lax.axis_index("col")
+    core = lax.rem(column, 2)
+    level = lax.div(column, 2)
+    sibling = (row, column + 1 - 2 * core)
+    own_len = inputs_ref.shape[0]
+    step = own_len // CHUNKS
+    b_out, gain1, shift1, b_down, gain2, shift2 = (
+        vectors_ref.at[place : place + 1, :] for place in range(6)
+    )
+
+    def peer_level(offset):
+        return lax.rem(level + offset, levels)
+
+    barrier = pltpu.get_barrier_semaphore()
+    pl.semaphore_signal(barrier, inc=1, device_id=sibling, device_id_type=MESH)
+    for offset in range(1, levels):
+        pl.semaphore_signal(
+            barrier,
+            inc=1,
+            device_id=(row, peer_level(offset) * 2 + core),
+            device_id_type=MESH,
+        )
+    pl.semaphore_wait(barrier, levels)
+
+    def to_sibling(source, target, place):
+        return pltpu.make_async_remote_copy(
+            src_ref=source,
+            dst_ref=target,
+            send_sem=core_send.at[place],
+            recv_sem=core_recv.at[place],
+            device_id=sibling,
+            device_id_type=MESH,
+        )
+
+    def rows_of(place, chunk):
+        return pl.ds(pl.multiple_of(place * own_len + chunk * step, step), step)
+
+    def own_rows(chunk):
+        return pl.ds(pl.multiple_of(chunk * step, step), step)
+
+    def exchange(kind, chunk, offset, source, target):
+        return pltpu.make_async_remote_copy(
+            src_ref=source,
+            dst_ref=target,
+            send_sem=send_sem.at[kind, chunk, offset - 1],
+            recv_sem=recv_sem.at[kind, chunk, levels - offset - 1],
+            device_id=(row, peer_level(offset) * 2 + core),
+            device_id_type=MESH,
+        )
+
+    def sum_copy(kind, chunk, offset):
+        return exchange(
+            kind,
+            chunk,
+            offset,
+            send_buf.at[kind // 2, offset - 1, own_rows(chunk)],
+            recv_buf.at[kind // 2, levels - offset - 1, own_rows(chunk)],
+        )
+
+    def spread_copy(kind, chunk, offset):
+        whole = {1: normed_full, 3: ffn_full, 5: attn_full}[kind]
+        rows = rows_of(level, chunk)
+        return exchange(kind, chunk, offset, whole.at[rows], whole.at[rows])
+
+    def received(kind, chunk):
+        return sum(
+            recv_buf[kind // 2, place, own_rows(chunk), :].astype(jnp.float32)
+            for place in range(levels - 1)
+        )
+
+    offsets = range(1, levels)
+    context_copies = [
+        to_sibling(
+            context_ref.at[
+                pl.ds(pl.multiple_of((place * 2 + 1 - core) * own_len, own_len), own_len)
+            ],
+            context_sib.at[pl.ds(place * own_len, own_len)],
+            place,
+        )
+        for place in range(levels)
+    ]
+    out_copy = to_sibling(out_ref, out_sib, levels)
+    up_copy = to_sibling(up_ref, up_sib, levels + 1)
+    down_copy = to_sibling(down_ref, down_sib, levels + 2)
+    for copy in context_copies + [out_copy, up_copy, down_copy]:
+        copy.start()
+    small_ref[...] = jnp.zeros_like(small_ref)
+    up_small_ref[...] = jnp.zeros_like(up_small_ref)
+    for copy in context_copies:
+        copy.wait()
+    out_copy.wait()
+
+    def context_rows(place, chunk):
+        start = (place * 2 + core) * own_len + chunk * step
+        return pl.ds(pl.multiple_of(start, step), step)
+
+    def attn_part(place, chunk):
+        return dot_nt(context_ref[context_rows(place, chunk), :], out_ref[...]) + dot_nt(
+            context_sib[rows_of(place, chunk), :], out_sib[...]
+        )
+
+    @pl.loop(0, CHUNKS)
+    def _(chunk):
+        for offset in offsets:
+            send_buf[0, offset - 1, own_rows(chunk), :] = attn_part(
+                peer_level(offset), chunk
+            ).astype(low)
+            sum_copy(0, chunk, offset).start()
+
+    @pl.loop(0, CHUNKS)
+    def _(chunk):
+        rows = own_rows(chunk)
+        summed = (
+            inputs_ref[rows, :].astype(jnp.float32) + attn_part(level, chunk) + b_out[...]
+        )
+        for offset in offsets:
+            sum_copy(0, chunk, offset).wait_recv()
+        normed, inv_std = norm_parts(summed + received(0, chunk))
+        unit1[rows, :] = normed
+        inv1[rows, :] = inv_std
+        normed_full[rows_of(level, chunk), :] = (normed * gain1[...] + shift1[...]).astype(low)
+        for offset in offsets:
+            spread_copy(1, chunk, offset).start()
+
+    up_copy.wait()
+    down_copy.wait()
+    sides = ((up_ref, down_ref), (up_sib, down_sib))
+
+    def feed_forward(place, chunk):
+        rows = rows_of(place, chunk)
+        normed = normed_full[rows, :]
+        total = None
+        for side, (up_side, down_side) in enumerate(sides):
+            active, bend = gelu_parts(dot(normed, up_side[...]) + b_up_ref[side : side + 1, :])
+            active = active.astype(low)
+            hidden[side, rows, :] = active
+            slope[side, rows, :] = bend
+            part = dot_nt(active, down_side[...])
+            total = part if total is None else total + part
+        return total
+
+    @pl.loop(0, CHUNKS)
+    def _(chunk):
+        part_own[own_rows(chunk), :] = feed_forward(level, chunk)
+        for offset in offsets:
+            spread_copy(1, chunk, levels - offset).wait_recv()
+            send_buf[1, offset - 1, own_rows(chunk), :] = feed_forward(
+                peer_level(offset), chunk
+            ).astype(low)
+            sum_copy(2, chunk, offset).start()
+
+    @pl.loop(0, CHUNKS)
+    def _(chunk):
+        rows = own_rows(chunk)
+        normed1 = unit1[rows, :] * gain1[...] + shift1[...]
+        summed = normed1 + part_own[rows, :] + b_down[...]
+        for offset in offsets:
+            sum_copy(2, chunk, offset).wait_recv()
+        normed, inv_std = norm_parts(summed + received(2, chunk))
+        layer_out_ref[rows, :] = (normed * gain2[...] + shift2[...]).astype(low)
+        upstream = upstream_ref[rows, :].astype(jnp.float32)
+        grad = norm_back(upstream, normed, inv_std, gain2[...])
+        ffn_keep[rows, :] = grad
+        grad_low = grad.astype(low)
+        ffn_full[rows_of(level, chunk), :] = grad_low
+        for offset in offsets:
+            spread_copy(3, chunk, offset).start()
+        small_ref[0:1, :] += jnp.sum(upstream * normed, axis=0, keepdims=True)
+        small_ref[1:2, :] += jnp.sum(upstream, axis=0, keepdims=True)
+        small_ref[2:3, :] += jnp.sum(grad_low.astype(jnp.float32), axis=0, keepdims=True)
+
+    def feed_back(place, chunk):
+        rows = rows_of(place, chunk)
+        upstream = ffn_full[rows, :]
+        total = None
+        for side, (up_side, down_side) in enumerate(sides):
+            grad = (dot(upstream, down_side[...]) * slope[side, rows, :]).astype(low)
+            pre_grad[side, rows, :] = grad
+            up_small_ref[side : side + 1, :] += jnp.sum(
+                grad.astype(jnp.float32), axis=0, keepdims=True
+            )
+            part = dot_nt(grad, up_side[...])
+            total = part if total is None else total + part
+        return total
+
+    @pl.loop(0, CHUNKS)
+    def _(chunk):
+        part_own[own_rows(chunk), :] = feed_back(level, chunk)
+        for offset in offsets:
+            spread_copy(3, chunk, levels - offset).wait_recv()
+            send_buf[2, offset - 1, own_rows(chunk), :] = feed_back(
+                peer_level(offset), chunk
+            ).astype(low)
+            sum_copy(4, chunk, offset).start()
+
+    def weight_grad(left_ref, right_of, target_ref, buffer):
+        tile = buffer.shape[1]
+        tiles = left_ref.shape[1] // tile
+
+        def put(side, turn):
+            return pltpu.make_async_copy(
+                buffer.at[lax.rem(turn, 2)],
+                target_ref.at[side, pl.ds(pl.multiple_of(turn * tile, tile), tile)],
+                stage_sem.at[lax.rem(turn, 2)],
+            )
+
+        for side in range(2):
+
+            @pl.loop(0, tiles)
+            def _(turn):
+                @pl.when(turn >= 2)
+                def _():
+                    put(side, turn - 2).wait()
+
+                left = left_ref[:, pl.ds(pl.multiple_of(turn * tile, tile), tile)]
+                buffer[lax.rem(turn, 2)] = dot_tn(left, right_of(side)).astype(low)
+                put(side, turn).start()
+
+            for turn in range(max(tiles - 2, 0), tiles):
+                put(side, turn).wait()
+
+    weight_grad(ffn_full, lambda side: hidden[side], grad_down_ref, stage)
+
+    @pl.loop(0, CHUNKS)
+    def _(chunk):
+        rows = own_rows(chunk)
+        upstream = ffn_keep[rows, :] + part_own[rows, :]
+        for offset in offsets:
+            sum_copy(4, chunk, offset).wait_recv()
+        upstream = upstream + received(4, chunk)
+        normed = unit1[rows, :]
+        grad_low = norm_back(upstream, normed, inv1[rows, :], gain1[...]).astype(low)
+        attn_full[rows_of(level, chunk), :] = grad_low
+        for offset in offsets:
+            spread_copy(5, chunk, offset).start()
+        small_ref[3:4, :] += jnp.sum(upstream * normed, axis=0, keepdims=True)
+        small_ref[4:5, :] += jnp.sum(upstream, axis=0, keepdims=True)
+        small_ref[5:6, :] += jnp.sum(grad_low.astype(jnp.float32), axis=0, keepdims=True)
+
+    weight_grad(normed_full, lambda side: pre_grad[side], grad_up_ref, stage)
+
+    def context_back(place, chunk):
+        rows = rows_of(place, chunk)
+        upstream = attn_full[rows, :]
+        context_grad_ref[context_rows(place, chunk), :] = dot(upstream, out_ref[...]).astype(low)
+        context_send[rows, :] = dot(upstream, out_sib[...]).astype(low)
+
+    @pl.loop(0, CHUNKS)
+    def _(chunk):
+        context_back(level, chunk)
+        for offset in offsets:
+            spread_copy(5, chunk, levels - offset).wait_recv()
+            context_back(peer_level(offset), chunk)
+
+    back_copies = [
+        to_sibling(
+            context_send.at[pl.ds(place * own_len, own_len)],
+            context_grad_ref.at[
+                pl.ds(pl.multiple_of((place * 2 + core) * own_len, own_len), own_len)
+            ],
+            levels + 3 + place,
+        )
+        for place in range(levels)
+    ]
+    for copy in back_copies:
+        copy.start()
+
+    own_context = jnp.concatenate(
+        [
+            context_ref[
+                pl.ds(pl.multiple_of((place * 2 + core) * own_len, own_len), own_len), :
+            ]
+            for place in range(levels)
+        ],
+        axis=0,
+    )
+    weight_grad(
+        attn_full,
+        lambda side: context_sib[...] if side else own_context,
+        grad_out_ref,
+        stage_small,
+    )
+    for copy in back_copies:
+        copy.wait()
+    for kind in range(6):
+
+        @pl.loop(0, CHUNKS)
+        def _(chunk):
+            for offset in offsets:
+                if kind % 2:
+                    spread_copy(kind, chunk, offset).wait_send()
+                else:
+                    sum_copy(kind, chunk, offset).wait_send()
+
+
+def middle(levels, context, inputs, upstream, out_own, up_own, down_own, vectors, b_up_pair):
+    low, full = jnp.bfloat16, jnp.float32
+    own_len, features = inputs.shape
+    seq_len, width = context.shape
+    units = up_own.shape[1]
+    tokens = levels * own_len
+    others = levels - 1
+    tile = 256
+    shape = jax.ShapeDtypeStruct
+    hbm = pl.BlockSpec(memory_space=pl.ANY)
+    return pl.pallas_call(
+        functools.partial(middle_kernel, levels),
+        out_shape=(
+            shape((own_len, features), low),
+            shape((seq_len, width), low),
+            shape((tokens, features), low),
+            shape((8, features), full),
+            shape((2, units), full),
+            shape((2, features, units), low),
+            shape((2, features, units), low),
+            shape((2, features, width), low),
+        ),
+        in_specs=[VMEM] * 8,
+        out_specs=[VMEM] * 5 + [hbm] * 3,
+        scratch_shapes=[
+            pltpu.VMEM((tokens, width), low),
+            pltpu.VMEM((features, width), low),
+            pltpu.VMEM((features, units), low),
+            pltpu.VMEM((features, units), low),
+            pltpu.VMEM((tokens, features), low),
+            pltpu.VMEM((tokens, features), low),
+            pltpu.VMEM((2, tokens, units), low),
+            pltpu.VMEM((2, tokens, units), full),
+            pltpu.VMEM((2, tokens, units), low),
+            pltpu.VMEM((own_len, features), full),
+            pltpu.VMEM((own_len, 1), full),
+            pltpu.VMEM((own_len, features), full),
+            pltpu.VMEM((own_len, features), full),
+            pltpu.VMEM((3, others, own_len, features), low),
+            pltpu.VMEM((3, others, own_len, features), low),
+            pltpu.VMEM((tokens, width), low),
+            pltpu.VMEM((2, tile, units), low),
+            pltpu.VMEM((2, tile, width), low),
+            pltpu.SemaphoreType.DMA((6, CHUNKS, others)),
+            pltpu.SemaphoreType.DMA((6, CHUNKS, others)),
+            pltpu.SemaphoreType.DMA((2 * levels + 3,)),
+            pltpu.SemaphoreType.DMA((2 * levels + 3,)),
+            pltpu.SemaphoreType.DMA((2,)),
+        ],
+        compiler_params=pltpu.CompilerParams(
+            collective_id=1, has_side_effects=True, vmem_limit_bytes=60 * 1024 * 1024
+        ),
+        cost_estimate=pl.CostEstimate(
+            flops=2 * tokens * features * (12 * units + 6 * width),
+            bytes_accessed=40 * 1024 * 1024,
+            transcendentals=2 * tokens * units,
+        ),
+    )(context, inputs, upstream, out_own, up_own, down_own, vectors, b_up_pair)
+
+
+def to_tokens(portion):
+    return lax.all_to_all(portion, "col", split_axis=0, concat_axis=1, tiled=True)
+
+
+def to_features(portion):
+    return lax.all_to_all(portion, "col", split_axis=1, concat_axis=0, tiled=True)
 
 
 def into_full(portion, start_at, full_len):
     return lax.dynamic_update_slice_in_dim(
         jnp.zeros((full_len,), jnp.float32), portion, start_at, 0
-    )
-
-
-def dot(left, right):
-    return jnp.dot(left, right, preferred_element_type=jnp.float32)
-
-
-def dot_nt(left, right):
-    return lax.dot_general(
-        left, right, (((1,), (1,)), ((), ())), preferred_element_type=jnp.float32
-    )
-
-
-def dot_tn(left, right):
-    return lax.dot_general(
-        left, right, (((0,), (0,)), ((), ())), preferred_element_type=jnp.float32
     )
 
 
@@ -391,9 +788,9 @@
     full_out = lax.all_gather(w_out.astype(low).T, "row", axis=0, tiled=True)
     full_up = lax.all_gather(w_up.astype(low), "row", axis=0, tiled=True)
     full_down = lax.all_gather(w_down.astype(low).T, "row", axis=0, tiled=True)
-    own_features = lax.dynamic_slice_in_dim(features, own_start, own_len, 0).astype(jnp.float32)
-    own_valid = (own_start + jnp.arange(own_len) < length)[:, None]
-    upstream = jnp.where(own_valid, to_tokens(out_grad).astype(jnp.float32), 0.0)
+    own_features = lax.dynamic_slice_in_dim(features, own_start, own_len, 0)
+    valid = (jnp.arange(seq_len) < length)[:, None]
+    upstream = to_tokens(jnp.where(valid, out_grad, 0))
 
     full_query = full_qkv[:, :feat_cols]
     full_key = full_qkv[:, feat_cols : 2 * feat_cols]
@@ -407,35 +804,33 @@
     ).astype(low)
     context, *stats = attend(queries, key_rows, value_rows, tables)
 
-    summed1 = own_features + reduce_tokens(dot_nt(context, full_out)) + b_out
-    normed1, unit1, inv_std1 = layer_norm(summed1, ln1_gain, ln1_bias)
-    normed1_full = spread(normed1.astype(low))
-    pre_act = dot(normed1_full, full_up) + lax.dynamic_slice_in_dim(b_up, unit_start, unit_cols)
-    activated, gelu_back = jax.vjp(gelu_tanh, pre_act)
-    hidden = activated.astype(low)
-    summed2 = normed1 + reduce_tokens(dot_nt(hidden, full_down)) + b_down
-    normed2, unit2, inv_std2 = layer_norm(summed2, ln2_gain, ln2_bias)
-    layer_out = to_features(jnp.where(own_valid, normed2, 0.0).astype(low))
-
-    ffn_grad, gain2_grad, shift2_grad = norm_back(upstream, unit2, inv_std2, ln2_gain)
-    ffn_low = ffn_grad.astype(low)
-    ffn_full = spread(ffn_low)
-    pre_grad = gelu_back(dot(ffn_full, full_down))[0].astype(low)
-    normed1_grad = ffn_grad + reduce_tokens(dot_nt(pre_grad, full_up))
-    grad_down = dot_tn(ffn_full, hidden)
-    grad_up = dot_tn(normed1_full, pre_grad)
-    attn_grad, gain1_grad, shift1_grad = norm_back(normed1_grad, unit1, inv_std1, ln1_gain)
-    attn_low = attn_grad.astype(low)
-    attn_full = spread(attn_low)
-    context_grad = dot(attn_full, full_out).astype(low)
-    grad_out = dot_tn(attn_full, context)
+    sibling = column + 1 - 2 * lax.rem(column, 2)
+    layer_own, context_grad, attn_full, small, up_small, grad_up, grad_down, grad_out = middle(
+        cols // 2,
+        context,
+        own_features,
+        upstream,
+        full_out,
+        full_up,
+        full_down,
+        jnp.stack([b_out, ln1_gain, ln1_bias, b_down, ln2_gain, ln2_bias, b_out, b_out]),
+        jnp.stack(
+            [
+                lax.dynamic_slice_in_dim(b_up, unit_start, unit_cols),
+                lax.dynamic_slice_in_dim(b_up, sibling * unit_cols, unit_cols),
+            ]
+        ),
+    )
+    layer_out = jnp.where(valid, to_features(layer_own), 0)
     query_grad, key_grad, value_grad = attend_back(
         queries, key_rows, value_rows, tables, stats, context_grad
     )
     input_part = (
         dot_nt(query_grad, full_query) + dot_nt(key_grad, full_key) + dot_nt(value_grad, full_value)
     )
-    own_part = lax.dynamic_slice_in_dim(input_part, own_start, own_len, 0) + attn_grad
+    own_part = lax.dynamic_slice_in_dim(input_part, own_start, own_len, 0) + (
+        lax.dynamic_slice_in_dim(attn_full, lax.div(column, 2) * own_len, own_len, 0)
+    )
     input_part = lax.dynamic_update_slice_in_dim(input_part, own_part, own_start, 0)
     grad_input = lax.psum_scatter(
         input_part.astype(low), "col", scatter_dimension=1, tiled=True
@@ -447,21 +842,22 @@
             partial_value.astype(low), "row", scatter_dimension=0, tiled=True
         ).astype(jnp.float32)
 
-    down_share = reduce_rows(grad_down).T
-    up_share = reduce_rows(grad_up)
-    out_share = reduce_rows(grad_out).T
+    swap = [(place, place + 1 - 2 * (place % 2)) for place in range(cols)]
+
+    def both_cores(pair):
+        return pair[0].astype(jnp.float32) + lax.ppermute(pair[1], "col", swap)
+
+    down_share = reduce_rows(both_cores(grad_down)).T
+    up_share = reduce_rows(both_cores(grad_up))
+    out_share = reduce_rows(both_cores(grad_out)).T
     qkv_share = reduce_rows(grad_qkv)
     small_grads = lax.psum(
         (
             into_full(jnp.sum(query_grad, axis=0, dtype=jnp.float32), feat_start, features_all),
             into_full(jnp.sum(value_grad, axis=0, dtype=jnp.float32), feat_start, features_all),
-            jnp.sum(attn_low, axis=0, dtype=jnp.float32),
-            gain1_grad,
-            shift1_grad,
-            into_full(jnp.sum(pre_grad, axis=0, dtype=jnp.float32), unit_start, units_all),
-            jnp.sum(ffn_low, axis=0, dtype=jnp.float32),
-            gain2_grad,
-            shift2_grad,
+            small,
+            into_full(up_small[0], unit_start, units_all)
+            + into_full(up_small[1], sibling * unit_cols, units_all),
         ),
         ("row", "col"),
     )
@@ -474,15 +870,15 @@
         qkv_share[:, 2 * feat_cols :],
         small_grads[1],
         out_share,
-        small_grads[2],
+        small_grads[2][5],
+        small_grads[2][3],
+        small_grads[2][4],
+        up_share,
         small_grads[3],
-        small_grads[4],
-        up_share,
-        small_grads[5],
         down_share,
-        small_grads[6],
-        small_grads[7],
-        small_grads[8],
+        small_grads[2][2],
+        small_grads[2][0],
+        small_grads[2][1],
     )
 
 

time: 852 us -> 687 us (0.81)
  waiting for transfers between devices: 554 us -> 310 us
  Pallas kernels: 46.4 us -> 199 us
  matrix products: 92.2 us -> 18.4 us
  other arithmetic: 34.7 us -> 23.6 us
  local copies, waits for them, and re-layouts: 20.5 us -> 31.3 us
    pallas_call x0 -> x1, Pallas kernels: none -> 152 us  [middle(): pl.pallas_call(functools.partial(middle_kernel, levels), out_shape=(shape...]
    reduce_scatter x3 -> x0, waiting for transfers between devices: 110 us -> none  [reduce_tokens(): lax.psum_scatter(partial_value.astype(jnp.bfloat16), 'col', scatter_dimen...]
    all_gather x3 -> x0, waiting for transfers between devices: 83.4 us -> none  [spread(): return lax.all_gather(portion, 'col', axis=0, tiled=True)]
    unnamed x16 -> x10, waiting for transfers between devices: 66.6 us -> 5.13 us
    reduce_scatter x3, waiting for transfers between devices: 84.6 us -> 135 us  [reduce_rows(): lax.psum_scatter(partial_value.astype(low), 'row', scatter_dimension=0, t...]
    all_gather x1, waiting for transfers between devices: 35.5 us -> 0.01 us  [on_device(): features = lax.all_gather(hidden_in, 'col', axis=1, tiled=True)]
    dot_general x6 -> x3, matrix products: 34.4 us -> 6.33 us  [dot(): return jnp.dot(left, right, preferred_element_type=jnp.float32)]
    all_gather x1, waiting for transfers between devices: 14.4 us -> 42.2 us  [on_device(): lax.all_gather(jnp.concatenate([w_query.astype(low), w_key.astype(low), w...]
  transfers between devices with their start and end apart: 17 -> 14, of which waited for: 16 -> 10; matrix products, arithmetic and copies ran while one was open for 10% -> 9% of each run, Pallas kernels for 3% -> 7%
where the time goes in v2:
time: 687 us; the launch traced here: 686 us
  waiting for transfers between devices  310 us (45%)
  Pallas kernels  199 us (29%)
  blocking collectives  80.1 us (12%)
  local copies, waits for them, and re-layouts  31.3 us (5%)
  other arithmetic  23.6 us (3%)
  matrix products  18.4 us (3%)
  between operations  15 us (2%)
  starting transfers between devices  8.81 us (1%)
    pallas_call x1, Pallas kernels, middle(): pl.pallas_call(functools.partial(middle_kernel, levels), out_shape=(shape...  152 us
    reduce_scatter x3, waiting for transfers between devices, reduce_rows(): lax.psum_scatter(partial_value.astype(low), 'row', scatter_dimension=0, t...  135 us
    all_gather x1, waiting for transfers between devices, on_device(): full_down = lax.all_gather(w_down.astype(low).T, 'row', axis=0, tiled=True)  50.4 us
    psum x1, blocking collectives, on_device(): lax.psum((into_full(jnp.sum(query_grad, axis=0, dtype=jnp.float32), feat_...  45.8 us
    reduce_scatter x1, waiting for transfers between devices, on_device(): lax.psum_scatter(input_part.astype(low), 'col', scatter_dimension=1, tile...  44.9 us
    all_gather x1, waiting for transfers between devices, on_device(): lax.all_gather(jnp.concatenate([w_query.astype(low), w_key.astype(low), w...  42.2 us
    all_gather x1, blocking collectives, on_device(): full_out = lax.all_gather(w_out.astype(low).T, 'row', axis=0, tiled=True)  34.4 us
    pallas_call x1, Pallas kernels, attend_back(): pl.pallas_call(functools.partial(attend_back_kernel, head_count, 2), out_...  26.2 us
  transfers between devices with their start and end apart: 14, of which 10 were waited for; matrix products, arithmetic and copies ran while one was open for 9% of the time, Pallas kernels for 7%

profile of v2, /device:TPU:0, one launch (start us, length us, event | category | flops | bytes accessed | tf_op | source)
XLA Modules:
  0.0 685.5 jit_solution(17783967465108669243)
XLA Ops:
  16.3 4.2 all-to-all-start
  25.0 34.4 %all_gather.17.out_ref = bf16[1024,256]{1,0:T(8,128)(2,1)} all-gather(bf16[128,256]{1,0:T(8,128)(2,1)S(1)} %bitcast.89), channel_id=1, replica_groups=mesh['row'=8,'col'=4] {'row'}, dimensions={0}, use_global_device_ids=true | all-gather | bytes 589824 | tf_op jit(solution)/shard_map/all_gather | solution.py:788
  62.8 42.2 %all-gather.5.cloned.1.call-done = bf16[1024,768]{1,0:T(8,128)(2,1)} async-done(((bf16[128,768]{1,0:T(8,128)(2,1)}), bf16[1024,768]{1,0:T(8,128)(2,1)}) %all-gather.5.cloned.1.call-update) | async-done | bytes 1572880 | tf_op jit(solution)/shard_map/all_gather | solution.py:781
  105.0 3.7 fusion.10.keys_ref
  111.8 20.3 %shard_map.323 = (bf16[2048,256]{1,0:T(8,128)(2,1)S(1)}, f32[32,1,256]{2,1,0:T(1,128)S(1)}, f32[32,1,256]{2,1,0:T(1,128)S(1)}) custom-call(s32[2]{0:T(128)S(1)} %bitcast.82, s32[384]{0:T(512)S(1)} %reshape.133.random_ref, s32[32,8,256]{2,1,0:T(8,128)S(1)} %pad_add_fusion.limits_ref, bf16[2048,256]{1,0:T(8,128)(2,1)S(1)} %fusion.12.queries_ref, ...), custom_call_target="tpu_custom_call" | custom-call | flops 4294967296 | bytes 4194304 | tf_op jit(solution)/shard_map/pallas_call | solution.py:250
  134.1 22.0 %all-gather.9.cloned.1.call-done.up_ref = bf16[1024,1024]{1,0:T(8,128)(2,1)} async-done(((bf16[128,1024]{1,0:T(8,128)(2,1)}), bf16[1024,1024]{1,0:T(8,128)(2,1)}) %all-gather.9.cloned.1.call-update) | async-done | bytes 2097168 | tf_op jit(solution)/shard_map/all_gather | solution.py:789
  156.0 50.4 %all-gather.11.cloned.1.call-done.down_ref = bf16[1024,1024]{1,0:T(8,128)(2,1)} async-done(((bf16[128,1024]{1,0:T(8,128)(2,1)}), bf16[1024,1024]{1,0:T(8,128)(2,1)}) %all-gather.11.cloned.1.call-update) | async-done | bytes 2097168 | tf_op jit(solution)/shard_map/all_gather | solution.py:790
  206.4 152.1 %shard_map.324 = (bf16[512,1024]{1,0:T(8,128)(2,1)}, bf16[2048,256]{1,0:T(8,128)(2,1)}, bf16[1024,1024]{1,0:T(8,128)(2,1)}, f32[8,1024]{1,0:T(8,128)}, f32[2,102...) custom-call(bf16[2048,256]{1,0:T(8,128)(2,1)} %copy-done.7, ...), custom_call_target="tpu_custom_call" | custom-call | flops 28991029248 | bytes 41943040 | tf_op jit(solution)/shard_map/pallas_call | solution.py:675
  368.5 26.2 %shard_map.325 = (bf16[2048,256]{1,0:T(8,128)(2,1)S(1)}, bf16[2048,256]{1,0:T(8,128)(2,1)S(1)}, bf16[2048,256]{1,0:T(8,128)(2,1)S(1)}) custom-call(s32[2]{0:T(128)S(1)} %bitcast.83, s32[384]{0:T(512)S(1)} %reshape.133.random_ref, s32[32,8,256]{2,1,0:T(8,128)S(1)} %pad_add_fusion.limits_ref, bf16[2048,256]{1,0:T(8,128)(2,1)S(1)} %copy-done.6, ...), custom_call_target="tpu_custom_call" | custom-call | flops 10737418240 | bytes 7340032 | tf_op jit(solution)/shard_map/pallas_call | solution.py:268
  394.8 4.9 fusion.16
  399.7 2.6 copy.101
  404.5 4.0 collective-permute-done.2
  413.1 4.0 collective-permute-done.1
  417.1 2.3 fusion.1
  419.8 2.3 fusion.25
  422.1 2.3 fusion.22
  424.5 2.4 add_add_fusion
  428.6 2.6 convert_element_type.111
  433.5 3.5 all-to-all-start.1
  438.2 45.8 %all-reduce = (f32[1024]{0:T(1024)}, f32[1024]{0:T(1024)}, f32[8,1024]{1,0:T(8,128)S(1)}, f32[4096]{0:T(1024)}) all-reduce(f32[1024]{0:T(1024)S(1)} %dynamic_update_slice.18, f32[1024]{0:T(1024)S(1)} %dynamic_update_slice.19, f32[8,1024]{1,0:T(8,128)S(1)} %copy-done.19, ...), channel_id=1, replica_groups=mesh['row'=8,'col'=4] {'row','col'}, use_global_device_ids=true, to_apply=%region_4.5 | all-reduce | flops 14336 | bytes 114688 | tf_op jit(solution)/shard_map/psum | solution.py:854
  487.5 4.3 reduce-scatter.16.cloned.1.call-done
  495.2 67.0 %reduce-scatter.14.cloned.1.call-done = bf16[128,1024]{1,0:T(8,128)(2,1)} async-done(((bf16[1024,1024]{1,0:T(8,128)(2,1)}), bf16[128,1024]{1,0:T(8,128)(2,1)}) %reduce-scatter.14.cloned.1.call-update) | async-done | bytes 262160 | tf_op jit(solution)/shard_map/reduce_scatter | solution.py:841
  564.2 68.1 %reduce-scatter.12.cloned.1.call-done = bf16[128,1024]{1,0:T(8,128)(2,1)} async-done(((bf16[1024,1024]{1,0:T(8,128)(2,1)}), bf16[128,1024]{1,0:T(8,128)(2,1)}) %reduce-scatter.12.cloned.1.call-update) | async-done | bytes 262160 | tf_op jit(solution)/shard_map/reduce_scatter | solution.py:841
  634.0 44.9 %reduce-scatter.8.cloned.1.call-done = bf16[2048,256]{1,0:T(8,128)(2,1)} async-done(((bf16[2048,1024]{1,0:T(8,128)(2,1)}), bf16[2048,256]{1,0:T(8,128)(2,1)}) %reduce-scatter.8.cloned.1.call-update) | async-done | bytes 1048592 | tf_op jit(solution)/shard_map/reduce_scatter | solution.py:835
  (144 shorter events, 53.8 us)
Async XLA Ops:
  7.2 53.4 %all-gather.7.cloned.1.call-start = ((), (), s32[]{:S(2)}) async-start(), calls=%async_computation.8 | async-start | bytes 5242880 | tf_op jit(solution)/shard_map/all_gather | solution.py:787
  7.9 97.0 %all-gather.5.cloned.1.call-start = ((), (), s32[]{:S(2)}) async-start(), calls=%async_computation.7 | async-start | bytes 1769472 | tf_op jit(solution)/shard_map/all_gather | solution.py:781
  11.5 11.1 %copy-start.20 = (s32[1,32,4,3]{1,2,3,0:T(4,128)S(1)}, s32[1,32,4,3]{1,2,3,0:T(4,128)}, u32[]{:S(2)}) copy-start(s32[1,32,4,3]{1,2,3,0:T(4,128)} %param.24) | copy-start | bytes 4612
  11.5 11.3 %copy-start.17 = (f32[256,128]{1,0:T(8,128)S(1)}, f32[256,128]{1,0:T(8,128)}, u32[]{:S(2)}) copy-start(f32[256,128]{1,0:T(8,128)} %param.30) | copy-start | bytes 393220
  11.5 144.5 %all-gather.9.cloned.1.call-start = ((), (), s32[]{:S(2)}) async-start(), calls=%async_computation.9 | async-start | bytes 2359296 | tf_op jit(solution)/shard_map/all_gather | solution.py:789
  13.4 10.1 %copy-start.18 = (f32[1024]{0:T(1024)S(1)}, f32[1024]{0:T(1024)}, u32[]{:S(2)}) copy-start(f32[1024]{0:T(1024)} %param.31) | copy-start | bytes 12292
  13.4 10.1 %copy-start.22 = (f32[1024]{0:T(1024)S(1)}, f32[1024]{0:T(1024)}, u32[]{:S(2)}) copy-start(f32[1024]{0:T(1024)} %param.32) | copy-start | bytes 12292
  13.4 10.1 %copy-start.23 = (f32[1024]{0:T(1024)S(1)}, f32[1024]{0:T(1024)}, u32[]{:S(2)}) copy-start(f32[1024]{0:T(1024)} %param.33) | copy-start | bytes 12292
  13.4 10.1 %copy-start.24 = (f32[1024]{0:T(1024)S(1)}, f32[1024]{0:T(1024)}, u32[]{:S(2)}) copy-start(f32[1024]{0:T(1024)} %param.37) | copy-start | bytes 12292
  13.4 10.1 %copy-start.25 = (f32[1024]{0:T(1024)S(1)}, f32[1024]{0:T(1024)}, u32[]{:S(2)}) copy-start(f32[1024]{0:T(1024)} %param.38) | copy-start | bytes 12292
  13.4 10.1 %copy-start.26 = (f32[1024]{0:T(1024)S(1)}, f32[1024]{0:T(1024)}, u32[]{:S(2)}) copy-start(f32[1024]{0:T(1024)} %param.39) | copy-start | bytes 12292
  13.4 10.8 %copy-start.27 = (f32[4096]{0:T(1024)S(1)}, f32[4096]{0:T(1024)}, u32[]{:S(2)}) copy-start(f32[4096]{0:T(1024)} %param.35) | copy-start | bytes 49156
  13.4 192.9 %all-gather.11.cloned.1.call-start = ((), (), s32[]{:S(2)}) async-start(), calls=%async_computation.10 | async-start | bytes 2359296 | tf_op jit(solution)/shard_map/all_gather | solution.py:790
  16.3 43.1 %all-to-all-start = ((bf16[4,512,256]{2,1,0:T(8,128)(2,1)}), bf16[4,512,256]{2,1,0:T(8,128)(2,1)S(1)}, u32[]{:S(2)}, u32[]{:S(2)}) async-start(bf16[4,512,256]{2,1,0:T(8,128)(2,1)} %bitcast.7), calls=%async_computation | async-start | bytes 2097152 | tf_op jit(solution)/shard_map/all_to_all | solution.py:726
  20.5 465.3 %reduce-scatter.10.cloned.1.call-start = ((), (), s32[]{:S(2)}) async-start(), calls=%async_computation.12 | async-start | bytes 589824 | tf_op jit(solution)/shard_map/reduce_scatter | solution.py:841
  359.6 2.0 collective-permute-start
  363.6 128.2 %reduce-scatter.16.cloned.1.call-start = ((), (), s32[]{:S(2)}) async-start(), calls=%async_computation.15 | async-start | bytes 1769472
  368.5 26.2 %copy-start.16 = (bf16[2048,1024]{1,0:T(8,128)(2,1)S(1)}, bf16[2048,1024]{1,0:T(8,128)(2,1)}, u32[]{:S(2)}) copy-start(bf16[2048,1024]{1,0:T(8,128)(2,1)} %all-gather.7.cloned.1.call-done) | copy-start | bytes 12582916
  402.3 159.8 %reduce-scatter.14.cloned.1.call-start = ((), (), s32[]{:S(2)}) async-start(), calls=%async_computation.14 | async-start | bytes 2359296 | tf_op jit(solution)/shard_map/reduce_scatter | solution.py:841
  404.3 4.2 collective-permute-start.2
  410.9 221.4 %reduce-scatter.12.cloned.1.call-start = ((), (), s32[]{:S(2)}) async-start(), calls=%async_computation.13 | async-start | bytes 2359296 | tf_op jit(solution)/shard_map/reduce_scatter | solution.py:841
  412.9 4.2 collective-permute-start.1
  419.5 259.5 %reduce-scatter.8.cloned.1.call-start = ((), (), s32[]{:S(2)}) async-start(), calls=%async_computation.11 | async-start | bytes 5242880 | tf_op jit(solution)/shard_map/reduce_scatter | solution.py:835
  433.5 51.0 %all-to-all-start.1 = ((bf16[512,4,256]{2,0,1:T(8,128)(2,1)}), bf16[512,4,256]{2,0,1:T(8,128)(2,1)S(1)}, u32[]{:S(2)}, u32[]{:S(2)}) async-start(bf16[512,4,256]{2,0,1:T(8,128)(2,1)} %bitcast.85), calls=%async_computation.1 | async-start | bytes 2097152 | tf_op jit(solution)/shard_map/all_to_all | solution.py:730
  (18 other events, 66.5 us)
Sparse Core Ops, SparseCore 0:
  9.6 48.9 all-gather.6
  60.8 44.1 all-gather.4
  107.7 48.2 all-gather.8
  158.6 47.7 all-gather.10
  363.7 60.4 reduce-scatter.9
  427.8 63.9 reduce-scatter.15
  495.3 66.8 reduce-scatter.13
  565.7 66.5 reduce-scatter.11
  635.4 43.5 reduce-scatter.7

commit v3 on v2

--- a/solution.py
+++ b/solution.py
@@ -161,17 +161,18 @@
     grads_ref,
     highest_ref,
     scale_ref,
-    query_grad_ref,
-    key_grad_ref,
-    value_grad_ref,
+    grads_out_ref,
+    bias_ref,
     key_sums,
     value_sums,
+    query_total,
 ):
     width = head_count * DH
     num_blocks = queries_ref.shape[0] // BLK
     factor = 1.0 / math.sqrt(DH)
     key_sums[...] = jnp.zeros_like(key_sums)
     value_sums[...] = jnp.zeros_like(value_sums)
+    query_total[...] = jnp.zeros_like(query_total)
 
     def one_block(step):
         shared, apart = slot_starts(step, num_blocks, head_count, globals_ref, random_ref)
@@ -204,7 +205,11 @@
         square = lax.dot_general(
             score_grad, picked_keys, (((0,), (0,)), ((), ())), preferred_element_type=jnp.float32
         )
-        query_grad_ref[own, :] = (from_diagonal(square, width) * factor).astype(jnp.bfloat16)
+        query_grad = (from_diagonal(square, width) * factor).astype(jnp.bfloat16)
+        grads_out_ref[own, :width] = query_grad
+        query_total[...] += jnp.sum(
+            query_grad.astype(jnp.float32).reshape(BLK // 8, 8, width), axis=0
+        )
         key_part = jnp.dot(score_grad, grouped, preferred_element_type=jnp.float32)
         value_part = jnp.dot(probs_low, grouped_grad, preferred_element_type=jnp.float32)
         put_rows(key_sums, key_part, shared, apart, head_count)
@@ -215,8 +220,11 @@
         for place in range(unroll):
             one_block(turn * unroll + place)
 
-    key_grad_ref[...] = key_sums[...].astype(jnp.bfloat16)
-    value_grad_ref[...] = value_sums[...].astype(jnp.bfloat16)
+    value_grad = value_sums[...].astype(jnp.bfloat16)
+    grads_out_ref[:, width : 2 * width] = key_sums[...].astype(jnp.bfloat16)
+    grads_out_ref[:, 2 * width :] = value_grad
+    bias_ref[0:1, :] = jnp.sum(query_total[...], axis=0, keepdims=True)
+    bias_ref[1:2, :] = jnp.sum(value_grad.astype(jnp.float32), axis=0, keepdims=True)
 
 
 def limits_of(length, global_ids, random_ids, num_blocks, head_count):
@@ -264,13 +272,16 @@
 def attend_back(queries, key_rows, value_rows, tables, stats, context_grad):
     seq_len, width = queries.shape
     head_count = width // DH
-    grad = jax.ShapeDtypeStruct((seq_len, width), jnp.bfloat16)
     return pl.pallas_call(
         functools.partial(attend_back_kernel, head_count, 2),
-        out_shape=(grad, grad, grad),
+        out_shape=(
+            jax.ShapeDtypeStruct((seq_len, 3 * width), jnp.bfloat16),
+            jax.ShapeDtypeStruct((2, width), jnp.float32),
+        ),
         in_specs=[SMEM] * 2 + [VMEM] * 7,
-        out_specs=[VMEM] * 3,
-        scratch_shapes=[pltpu.VMEM((seq_len, width), jnp.float32)] * 2,
+        out_specs=[VMEM] * 2,
+        scratch_shapes=[pltpu.VMEM((seq_len, width), jnp.float32)] * 2
+        + [pltpu.VMEM((8, width), jnp.float32)],
         compiler_params=pltpu.CompilerParams(vmem_limit_bytes=40 * 1024 * 1024),
         cost_estimate=pl.CostEstimate(
             flops=10 * seq_len * 512 * width * head_count,
@@ -329,6 +340,7 @@
     context_ref,
     inputs_ref,
     upstream_ref,
+    valid_ref,
     out_ref,
     up_ref,
     down_ref,
@@ -526,7 +538,9 @@
         for offset in offsets:
             sum_copy(2, chunk, offset).wait_recv()
         normed, inv_std = norm_parts(summed + received(2, chunk))
-        layer_out_ref[rows, :] = (normed * gain2[...] + shift2[...]).astype(low)
+        layer_out_ref[rows, :] = jnp.where(
+            valid_ref[rows, :] > 0, normed * gain2[...] + shift2[...], 0.0
+        ).astype(low)
         upstream = upstream_ref[rows, :].astype(jnp.float32)
         grad = norm_back(upstream, normed, inv_std, gain2[...])
         ffn_keep[rows, :] = grad
@@ -662,7 +676,9 @@
                     sum_copy(kind, chunk, offset).wait_send()
 
 
-def middle(levels, context, inputs, upstream, out_own, up_own, down_own, vectors, b_up_pair):
+def middle(
+    levels, context, inputs, upstream, valid, out_own, up_own, down_own, vectors, b_up_pair
+):
     low, full = jnp.bfloat16, jnp.float32
     own_len, features = inputs.shape
     seq_len, width = context.shape
@@ -684,7 +700,7 @@
             shape((2, features, units), low),
             shape((2, features, width), low),
         ),
-        in_specs=[VMEM] * 8,
+        in_specs=[VMEM] * 9,
         out_specs=[VMEM] * 5 + [hbm] * 3,
         scratch_shapes=[
             pltpu.VMEM((tokens, width), low),
@@ -719,15 +735,421 @@
             bytes_accessed=40 * 1024 * 1024,
             transcendentals=2 * tokens * units,
         ),
-    )(context, inputs, upstream, out_own, up_own, down_own, vectors, b_up_pair)
+    )(context, inputs, upstream, valid, out_own, up_own, down_own, vectors, b_up_pair)
+
+
+KINDS = 4
+
+
+def end_kernel(
+    levels,
+    across,
+    along,
+    query_key_value_ref,
+    weights_ref,
+    features_ref,
+    attn_ref,
+    layer_ref,
+    small_ref,
+    down_ref,
+    up_ref,
+    out_ref,
+    grad_input_ref,
+    layer_out_ref,
+    small_out_ref,
+    share_down_ref,
+    share_up_ref,
+    share_out_ref,
+    share_qkv_ref,
+    down_sib,
+    up_sib,
+    out_sib,
+    qkv_sums,
+    down_got,
+    up_got,
+    out_got,
+    qkv_got,
+    down_pass,
+    up_pass,
+    out_pass,
+    qkv_pass,
+    down_in,
+    up_in,
+    out_in,
+    qkv_in,
+    core_out,
+    core_in,
+    level_out,
+    level_in,
+    attn_in,
+    small_sums,
+    small_in,
+    core_send,
+    core_recv,
+    part_send,
+    part_recv,
+    level_send,
+    level_recv,
+    layer_send,
+    layer_recv,
+    across_send,
+    across_recv,
+    along_send,
+    along_recv,
+    small_send,
+    small_recv,
+    keep_sem,
+):
+    low, full = jnp.bfloat16, jnp.float32
+    row, column = lax.axis_index("row"), lax.axis_index("col")
+    core, level = lax.rem(column, 2), lax.div(column, 2)
+    fast, slow = lax.rem(row, across), lax.div(row, across)
+    cols = 2 * levels
+    seq_len = features_ref.shape[0]
+    own_len = seq_len // cols
+    width = grad_input_ref.shape[1]
+    shard = share_qkv_ref.shape[0]
+    other = 1 - core
+    sibling = (row, level * 2 + other)
+    offsets = range(1, levels)
+
+    def peer_level(offset):
+        return lax.rem(level + offset, levels)
+
+    def fast_peer(offset):
+        return slow * across + lax.rem(fast + offset, across)
+
+    def slow_peer(offset):
+        return lax.rem(slow + offset, along) * across + fast
+
+    barrier = pltpu.get_barrier_semaphore()
+    greeted = [sibling]
+    for offset in offsets:
+        greeted += [(row, peer_level(offset) * 2 + core), (row, peer_level(offset) * 2 + other)]
+    greeted += [(fast_peer(offset), column) for offset in range(1, across)]
+    greeted += [(slow_peer(offset), column) for offset in range(1, along)]
+    for device in greeted:
+        pl.semaphore_signal(barrier, inc=1, device_id=device, device_id_type=MESH)
+    pl.semaphore_wait(barrier, len(greeted))
+
+    def remote(source, target, send, recv, device):
+        return pltpu.make_async_remote_copy(
+            src_ref=source,
+            dst_ref=target,
+            send_sem=send,
+            recv_sem=recv,
+            device_id=device,
+            device_id_type=MESH,
+        )
+
+    def block(start, size):
+        return pl.ds(pl.multiple_of(start * size, size), size)
+
+    core_copies = [
+        remote(source.at[1], target, core_send.at[place], core_recv.at[place], sibling)
+        for place, (source, target) in enumerate(
+            [(down_ref, down_sib), (up_ref, up_sib), (out_ref, out_sib)]
+        )
+    ]
+    attn_copy = remote(
+        attn_ref.at[:, block(level * 2 + other, width)],
+        attn_in,
+        core_send.at[3],
+        core_recv.at[3],
+        sibling,
+    )
+
+    partners = [sibling]
+    bit = 1
+    while bit < levels:
+        partners.append((row, (level + bit - 2 * bit * lax.rem(lax.div(level, bit), 2)) * 2 + core))
+        bit *= 2
+    bit = 1
+    while bit < across * along:
+        partners.append((row + bit - 2 * bit * lax.rem(lax.div(row, bit), 2), column))
+        bit *= 2
+
+    def small_copy(turn):
+        return remote(
+            small_sums.at[turn],
+            small_in.at[turn],
+            small_send.at[turn],
+            small_recv.at[turn],
+            partners[turn],
+        )
+
+    small_turn = [0]
+
+    def small_step():
+        turn = small_turn[0]
+        if turn > len(partners):
+            return
+        if turn > 0:
+            small_copy(turn - 1).wait()
+            small_sums[turn] = small_sums[turn - 1] + small_in[turn - 1]
+        if turn < len(partners):
+            small_copy(turn).start()
+        small_turn[0] += 1
+
+    def layer_copy(target, place_out, place_in):
+        return remote(
+            layer_ref.at[:, block(target, width)],
+            layer_out_ref.at[block(column, own_len)],
+            layer_send.at[place_out],
+            layer_recv.at[place_in],
+            (row, target),
+        )
+
+    layer_copies = [layer_copy(level * 2 + other, 0, 0)]
+    for offset in offsets:
+        back = levels - offset
+        layer_copies.append(
+            layer_copy(peer_level(offset) * 2 + core, 2 * offset - 1, 2 * back - 1)
+        )
+        layer_copies.append(layer_copy(peer_level(offset) * 2 + other, 2 * offset, 2 * back))
+    layer_keep = pltpu.make_async_copy(
+        layer_ref.at[:, block(column, width)], layer_out_ref.at[block(column, own_len)], keep_sem
+    )
+
+    small_sums[0] = small_ref[...]
+    core_copies[0].start()
+    small_step()
+    for copy in core_copies[1:] + [attn_copy]:
+        copy.start()
+    layer_keep.start()
+    for copy in layer_copies:
+        copy.start()
+
+    def input_part(turn, target):
+        return dot_nt(
+            query_key_value_ref[block(turn, own_len), :], weights_ref[block(target, width), :]
+        )
+
+    def part_copy(turn, place):
+        rows = block(turn, own_len)
+        return remote(
+            core_out.at[place, rows],
+            core_in.at[place, rows],
+            part_send.at[turn, place],
+            part_recv.at[turn, place],
+            sibling,
+        )
+
+    @pl.loop(0, cols)
+    def _(turn):
+        for place in range(levels):
+            core_out[place, block(turn, own_len), :] = input_part(turn, place * 2 + other).astype(
+                low
+            )
+            part_copy(turn, place).start()
+
+    sums = (down_sib, up_sib, out_sib, qkv_sums)
+    firsts = (down_ref, up_ref, out_ref)
+    got = (down_got, up_got, out_got, qkv_got)
+    passed = (down_pass, up_pass, out_pass, qkv_pass)
+    landed = (down_in, up_in, out_in, qkv_in)
+    shares = (share_down_ref, share_up_ref, share_out_ref, share_qkv_ref)
+
+    def across_copy(kind, turn, offset):
+        return remote(
+            sums[kind].at[block(turn * across + lax.rem(fast + offset, across), shard)],
+            got[kind].at[across - offset - 1, block(turn, shard)],
+            across_send.at[kind, turn, offset - 1],
+            across_recv.at[kind, turn, across - offset - 1],
+            (fast_peer(offset), column),
+        )
+
+    def along_copy(kind, offset):
+        return remote(
+            passed[kind].at[offset - 1],
+            landed[kind].at[along - offset - 1],
+            along_send.at[kind, offset - 1],
+            along_recv.at[kind, along - offset - 1],
+            (slow_peer(offset), column),
+        )
+
+    def give_across(kind, turn):
+        for offset in range(1, across):
+            across_copy(kind, turn, offset).start()
+
+    for kind in range(3):
+        core_copies[kind].wait()
+
+        @pl.loop(0, along)
+        def _(turn):
+            rows = block(turn, across * shard)
+            sums[kind][rows, :] = (
+                firsts[kind][0, rows, :].astype(full) + sums[kind][rows, :].astype(full)
+            ).astype(low)
+            give_across(kind, turn)
+
+        small_step()
+
+    @pl.loop(0, along)
+    def _(turn):
+        rows = block(turn, across * shard)
+        qkv_sums[rows, :] = dot_tn(features_ref[:, rows], query_key_value_ref[...]).astype(low)
+        give_across(3, turn)
+
+    small_step()
+
+    def level_copy(turn, offset):
+        rows = block(turn, own_len)
+        return remote(
+            level_out.at[offset - 1, rows],
+            level_in.at[levels - offset - 1, rows],
+            level_send.at[turn, offset - 1],
+            level_recv.at[turn, levels - offset - 1],
+            (row, peer_level(offset) * 2 + core),
+        )
+
+    @pl.loop(0, cols)
+    def _(turn):
+        rows = block(turn, own_len)
+        for offset in offsets:
+            place = peer_level(offset)
+            part = input_part(turn, place * 2 + core)
+            part_copy(turn, place).wait_recv()
+            level_out[offset - 1, rows, :] = (part + core_in[place, rows, :].astype(full)).astype(
+                low
+            )
+            level_copy(turn, offset).start()
+
+    small_step()
+
+    def own_shard(kind, turn):
+        for offset in range(1, across):
+            across_copy(kind, turn, offset).wait_recv()
+        total = sums[kind][block(turn * across + fast, shard), :].astype(full)
+        for place in range(across - 1):
+            total += got[kind][place, block(turn, shard), :].astype(full)
+        return total
+
+    for kind in range(KINDS):
+        for offset in range(1, along):
+            turn = lax.rem(slow + offset, along)
+            passed[kind][offset - 1] = own_shard(kind, turn).astype(low)
+            along_copy(kind, offset).start()
+        shares[kind][...] = own_shard(kind, slow)
+
+    while small_turn[0] <= len(partners):
+        small_step()
+    small_out_ref[...] = small_sums[len(partners)]
+
+    attn_copy.wait()
+
+    def finish_input(turn, attn_part):
+        rows = block(turn, own_len)
+        total = input_part(turn, column) + attn_part.astype(full)
+        part_copy(turn, level).wait_recv()
+        total += core_in[level, rows, :].astype(full)
+        for offset in offsets:
+            level_copy(turn, offset).wait_recv()
+        for place in range(levels - 1):
+            total += level_in[place, rows, :].astype(full)
+        grad_input_ref[rows, :] = total.astype(low)
+
+    @pl.loop(0, levels)
+    def _(place):
+        rows = block(place, own_len)
+        finish_input(place * 2 + core, attn_ref[rows, block(column, width)])
+        finish_input(place * 2 + other, attn_in[rows, :])
+
+    for kind in range(KINDS):
+        total = shares[kind][...]
+        for offset in range(1, along):
+            along_copy(kind, offset).wait_recv()
+        for place in range(along - 1):
+            total += landed[kind][place].astype(full)
+        shares[kind][...] = total
+
+    layer_keep.wait()
+    for copy in layer_copies:
+        copy.wait()
+    for kind in range(KINDS):
+        for offset in range(1, along):
+            along_copy(kind, offset).wait_send()
+
+        @pl.loop(0, along)
+        def _(turn):
+            for offset in range(1, across):
+                across_copy(kind, turn, offset).wait_send()
+
+    @pl.loop(0, cols)
+    def _(turn):
+        for place in range(levels):
+            part_copy(turn, place).wait_send()
+        for offset in offsets:
+            level_copy(turn, offset).wait_send()
+
+
+def finish(
+    levels, rows, query_key_value, weights, features, attn_full, layer_own, small, down, up, out
+):
+    low, full = jnp.bfloat16, jnp.float32
+    shape = jax.ShapeDtypeStruct
+    across = 2 if rows <= 8 else rows // 4
+    along = rows // across
+    seq_len, features_all = features.shape
+    width = query_key_value.shape[1] // 3
+    own_len = layer_own.shape[0]
+    shard = features_all // rows
+    widths = [down.shape[2], up.shape[2], out.shape[2], 3 * width]
+    others = levels - 1
+    cols = 2 * levels
+    turns = 1 + (levels - 1).bit_length() + (rows - 1).bit_length()
+    dma = pltpu.SemaphoreType.DMA
+    return pl.pallas_call(
+        functools.partial(end_kernel, levels, across, along),
+        out_shape=(
+            shape((seq_len, width), low),
+            shape((seq_len, width), low),
+            shape(small.shape, full),
+            *(shape((shard, each), full) for each in widths),
+        ),
+        in_specs=[VMEM] * 9,
+        out_specs=[VMEM] * 7,
+        scratch_shapes=[
+            *(pltpu.VMEM((features_all, each), low) for each in widths),
+            *(pltpu.VMEM((across - 1, along * shard, each), low) for each in widths),
+            *(pltpu.VMEM((along - 1, shard, each), low) for each in widths),
+            *(pltpu.VMEM((along - 1, shard, each), low) for each in widths),
+            pltpu.VMEM((levels, seq_len, width), low),
+            pltpu.VMEM((levels, seq_len, width), low),
+            pltpu.VMEM((others, seq_len, width), low),
+            pltpu.VMEM((others, seq_len, width), low),
+            pltpu.VMEM((levels * own_len, width), low),
+            pltpu.VMEM((turns + 1, *small.shape), full),
+            pltpu.VMEM((turns, *small.shape), full),
+            dma((4,)),
+            dma((4,)),
+            dma((cols, levels)),
+            dma((cols, levels)),
+            dma((cols, others)),
+            dma((cols, others)),
+            dma((cols,)),
+            dma((cols,)),
+            dma((KINDS, along, across - 1)),
+            dma((KINDS, along, across - 1)),
+            dma((KINDS, along - 1)),
+            dma((KINDS, along - 1)),
+            dma((turns,)),
+            dma((turns,)),
+            dma,
+        ],
+        compiler_params=pltpu.CompilerParams(
+            collective_id=2, has_side_effects=True, vmem_limit_bytes=60 * 1024 * 1024
+        ),
+        cost_estimate=pl.CostEstimate(
+            flops=4 * seq_len * features_all * 3 * width,
+            bytes_accessed=40 * 1024 * 1024,
+            transcendentals=0,
+        ),
+    )(query_key_value, weights, features, attn_full, layer_own, small, down, up, out)
 
 
 def to_tokens(portion):
     return lax.all_to_all(portion, "col", split_axis=0, concat_axis=1, tiled=True)
-
-
-def to_features(portion):
-    return lax.all_to_all(portion, "col", split_axis=1, concat_axis=0, tiled=True)
 
 
 def into_full(portion, start_at, full_len):
@@ -791,6 +1213,7 @@
     own_features = lax.dynamic_slice_in_dim(features, own_start, own_len, 0)
     valid = (jnp.arange(seq_len) < length)[:, None]
     upstream = to_tokens(jnp.where(valid, out_grad, 0))
+    own_valid = (own_start + jnp.arange(own_len) < length).astype(jnp.float32)[:, None]
 
     full_query = full_qkv[:, :feat_cols]
     full_key = full_qkv[:, feat_cols : 2 * feat_cols]
@@ -810,6 +1233,7 @@
         context,
         own_features,
         upstream,
+        own_valid,
         full_out,
         full_up,
         full_down,
@@ -821,64 +1245,46 @@
             ]
         ),
     )
-    layer_out = jnp.where(valid, to_features(layer_own), 0)
-    query_grad, key_grad, value_grad = attend_back(
+    query_key_value, bias_sums = attend_back(
         queries, key_rows, value_rows, tables, stats, context_grad
     )
-    input_part = (
-        dot_nt(query_grad, full_query) + dot_nt(key_grad, full_key) + dot_nt(value_grad, full_value)
-    )
-    own_part = lax.dynamic_slice_in_dim(input_part, own_start, own_len, 0) + (
-        lax.dynamic_slice_in_dim(attn_full, lax.div(column, 2) * own_len, own_len, 0)
-    )
-    input_part = lax.dynamic_update_slice_in_dim(input_part, own_part, own_start, 0)
-    grad_input = lax.psum_scatter(
-        input_part.astype(low), "col", scatter_dimension=1, tiled=True
-    )
-    grad_qkv = dot_tn(features, jnp.concatenate([query_grad, key_grad, value_grad], axis=1))
-
-    def reduce_rows(partial_value):
-        return lax.psum_scatter(
-            partial_value.astype(low), "row", scatter_dimension=0, tiled=True
-        ).astype(jnp.float32)
-
-    swap = [(place, place + 1 - 2 * (place % 2)) for place in range(cols)]
-
-    def both_cores(pair):
-        return pair[0].astype(jnp.float32) + lax.ppermute(pair[1], "col", swap)
-
-    down_share = reduce_rows(both_cores(grad_down)).T
-    up_share = reduce_rows(both_cores(grad_up))
-    out_share = reduce_rows(both_cores(grad_out)).T
-    qkv_share = reduce_rows(grad_qkv)
-    small_grads = lax.psum(
-        (
-            into_full(jnp.sum(query_grad, axis=0, dtype=jnp.float32), feat_start, features_all),
-            into_full(jnp.sum(value_grad, axis=0, dtype=jnp.float32), feat_start, features_all),
-            small,
-            into_full(up_small[0], unit_start, units_all)
-            + into_full(up_small[1], sibling * unit_cols, units_all),
-        ),
-        ("row", "col"),
+    up_sums = into_full(up_small[0], unit_start, units_all) + into_full(
+        up_small[1], sibling * unit_cols, units_all
+    )
+    bias_full = lax.dynamic_update_slice(
+        jnp.zeros((4, features_all), jnp.float32), bias_sums, (0, feat_start)
+    )
+    grad_input, layer_out, small, down_share, up_share, out_share, qkv_share = finish(
+        cols // 2,
+        lax.axis_size("row"),
+        query_key_value,
+        full_qkv,
+        features,
+        attn_full,
+        layer_own,
+        jnp.concatenate([small, up_sums.reshape(-1, features_all), bias_full], axis=0),
+        grad_down,
+        grad_up,
+        grad_out,
     )
     return (
         layer_out,
         grad_input,
         qkv_share[:, :feat_cols],
-        small_grads[0],
+        small[-4],
         qkv_share[:, feat_cols : 2 * feat_cols],
         qkv_share[:, 2 * feat_cols :],
-        small_grads[1],
-        out_share,
-        small_grads[2][5],
-        small_grads[2][3],
-        small_grads[2][4],
+        small[-3],
+        out_share.T,
+        small[5],
+        small[3],
+        small[4],
         up_share,
-        small_grads[3],
-        down_share,
-        small_grads[2][2],
-        small_grads[2][0],
-        small_grads[2][1],
+        small[8:-4].reshape(-1),
+        down_share.T,
+        small[2],
+        small[0],
+        small[1],
     )
 
 

time: 687 us -> 546 us (0.79)
  waiting for transfers between devices: 310 us -> 116 us
  Pallas kernels: 199 us -> 337 us
  blocking collectives: 80.1 us -> 34.3 us
  other arithmetic: 23.6 us -> 7.78 us
  matrix products: 18.4 us -> 6.34 us
  local copies, waits for them, and re-layouts: 31.3 us -> 24.3 us
    reduce_scatter x4 -> x0, waiting for transfers between devices: 180 us -> none  [the longest x3 135 us: reduce_rows(): lax.psum_scatter(partial_value.astype(low), 'row', scatter_dimension=0, t...]
    pallas_call x0 -> x1, Pallas kernels: none -> 138 us  [finish(): pl.pallas_call(functools.partial(end_kernel, levels, across, along), out_...]
    psum x1 -> x0, blocking collectives: 45.8 us -> none  [on_device(): lax.psum((into_full(jnp.sum(query_grad, axis=0, dtype=jnp.float32), feat_...]
    all_gather x1, waiting for transfers between devices: 22 us -> 50.4 us  [on_device(): full_up = lax.all_gather(w_up.astype(low), 'row', axis=0, tiled=True)]
    all_gather x1, waiting for transfers between devices: 50.4 us -> 22.2 us  [on_device(): full_down = lax.all_gather(w_down.astype(low).T, 'row', axis=0, tiled=True)]
    dot_general x4 -> x0, matrix products: 12 us -> none  [the longest x3 7.09 us: dot_nt(): lax.dot_general(left, right, (((1,), (1,)), ((), ())), preferred_element_...]
    convert_element_type x5 -> x1, other arithmetic: 11 us -> 0.74 us  [on_device(): (own_start + jnp.arange(own_len) < length).astype(jnp.float32)[:, None]]
    ppermute x3 -> x0, waiting for transfers between devices: 9.95 us -> none  [both_cores(): return pair[0].astype(jnp.float32) + lax.ppermute(pair[1], 'col', swap)]
  transfers between devices with their start and end apart: 14 -> 5, of which waited for: 10 -> 3; matrix products, arithmetic and copies ran while one was open for 9% -> 4% of each run, Pallas kernels for 7% -> 4%
where the time goes in v3:
time: 546 us; the launch traced here: 545 us
  Pallas kernels  337 us (62%)
  waiting for transfers between devices  116 us (21%)
  blocking collectives  34.3 us (6%)
  local copies, waits for them, and re-layouts  24.3 us (4%)
  between operations  14.8 us (3%)
  other arithmetic  7.78 us (1%)
  matrix products  6.34 us (1%)
    pallas_call x1, Pallas kernels, middle(): pl.pallas_call(functools.partial(middle_kernel, levels), out_shape=(shape...  152 us
    pallas_call x1, Pallas kernels, finish(): pl.pallas_call(functools.partial(end_kernel, levels, across, along), out_...  138 us
    all_gather x1, waiting for transfers between devices, on_device(): full_up = lax.all_gather(w_up.astype(low), 'row', axis=0, tiled=True)  50.4 us
    all_gather x1, waiting for transfers between devices, on_device(): lax.all_gather(jnp.concatenate([w_query.astype(low), w_key.astype(low), w...  42.5 us
    all_gather x1, blocking collectives, on_device(): full_out = lax.all_gather(w_out.astype(low).T, 'row', axis=0, tiled=True)  34.3 us
    pallas_call x1, Pallas kernels, attend_back(): pl.pallas_call(functools.partial(attend_back_kernel, head_count, 2), out_...  26.4 us
    all_gather x1, waiting for transfers between devices, on_device(): full_down = lax.all_gather(w_down.astype(low).T, 'row', axis=0, tiled=True)  22.2 us
    pallas_call x1, Pallas kernels, attend(): pl.pallas_call(functools.partial(attend_kernel, head_count, 2), out_shape...  20.4 us
  transfers between devices with their start and end apart: 5, of which 3 were waited for; matrix products, arithmetic and copies ran while one was open for 4% of the time, Pallas kernels for 4%

profile of v3, /device:TPU:0, one launch (start us, length us, event | category | flops | bytes accessed | tf_op | source)
XLA Modules:
  0.0 545.0 jit_solution(3061327700249263227)
XLA Ops:
  13.9 1.2 broadcast_select_fusion
  15.2 4.4 all-to-all-start
  24.8 34.3 %all_gather.17.out_ref = bf16[1024,256]{1,0:T(8,128)(2,1)} all-gather(bf16[128,256]{1,0:T(8,128)(2,1)S(1)} %bitcast.64), channel_id=1, replica_groups=mesh['row'=8,'col'=4] {'row'}, dimensions={0}, use_global_device_ids=true | all-gather | bytes 589824 | tf_op jit(solution)/shard_map/all_gather | solution.py:1210
  59.1 1.1 copy.101
  60.2 2.3 constant_dynamic-slice_fusion.inputs_ref
  62.5 42.5 %all-gather.5.cloned.1.call-done.weights_ref = bf16[1024,768]{1,0:T(8,128)(2,1)} async-done(((bf16[128,768]{1,0:T(8,128)(2,1)}), bf16[1024,768]{1,0:T(8,128)(2,1)}) %all-gather.5.cloned.1.call-update) | async-done | bytes 1572880 | tf_op jit(solution)/shard_map/all_gather | solution.py:1203
  105.0 3.7 fusion.2.keys_ref
  109.1 1.3 fusion.3.values_ref
  110.4 1.3 fusion.4.queries_ref
  111.7 20.4 %shard_map.323 = (bf16[2048,256]{1,0:T(8,128)(2,1)S(1)}, f32[32,1,256]{2,1,0:T(1,128)S(1)}, f32[32,1,256]{2,1,0:T(1,128)S(1)}) custom-call(s32[2]{0:T(128)S(1)} %bitcast.58, s32[384]{0:T(512)S(1)} %reshape.143.random_ref, s32[32,8,256]{2,1,0:T(8,128)S(1)} %pad_add_fusion.limits_ref, bf16[2048,256]{1,0:T(8,128)(2,1)S(1)} %fusion.4.queries_ref, ...), custom_call_target="tpu_custom_call" | custom-call | flops 4294967296 | bytes 4194304 | tf_op jit(solution)/shard_map/pallas_call | solution.py:258
  132.1 1.0 copy-done.2
  133.1 22.2 %all-gather.11.cloned.1.call-done.down_ref = bf16[1024,1024]{1,0:T(8,128)(2,1)} async-done(((bf16[128,1024]{1,0:T(8,128)(2,1)}), bf16[1024,1024]{1,0:T(8,128)(2,1)}) %all-gather.11.cloned.1.call-update) | async-done | bytes 2097168 | tf_op jit(solution)/shard_map/all_gather | solution.py:1212
  155.3 50.4 %all-gather.9.cloned.1.call-done.up_ref = bf16[1024,1024]{1,0:T(8,128)(2,1)} async-done(((bf16[128,1024]{1,0:T(8,128)(2,1)}), bf16[1024,1024]{1,0:T(8,128)(2,1)}) %all-gather.9.cloned.1.call-update) | async-done | bytes 2097168 | tf_op jit(solution)/shard_map/all_gather | solution.py:1211
  205.6 152.2 %shard_map.324 = (bf16[512,1024]{1,0:T(8,128)(2,1)}, bf16[2048,256]{1,0:T(8,128)(2,1)}, bf16[1024,1024]{1,0:T(8,128)(2,1)}, f32[8,1024]{1,0:T(8,128)}, f32[2,102...) custom-call(bf16[2048,256]{1,0:T(8,128)(2,1)} %copy-done.2, ...), custom_call_target="tpu_custom_call" | custom-call | flops 28991029248 | bytes 41943040 | tf_op jit(solution)/shard_map/pallas_call | solution.py:691
  359.0 1.2 copy-done.3
  360.2 26.4 %shard_map.325 = (bf16[2048,768]{1,0:T(8,128)(2,1)S(1)}, f32[2,256]{1,0:T(2,128)S(1)}) custom-call(s32[2]{0:T(128)S(1)} %bitcast.59, s32[384]{0:T(512)S(1)} %reshape.143.random_ref, s32[32,8,256]{2,1,0:T(8,128)S(1)} %pad_add_fusion.limits_ref, bf16[2048,256]{1,0:T(8,128)(2,1)S(1)} %fusion.4.queries_ref, bf16[2048,256]{1,0:T(8,128)(2,1)S(1)} %fusion.2.keys_ref, ...), custom_call_target="tpu_custom_call" | custom-call | flops 10737418240 | bytes 7340032 | tf_op jit(solution)/shard_map/pallas_call | solution.py:275
  386.7 1.6 copy-done.1
  389.0 138.2 %shard_map.326 = (bf16[2048,256]{1,0:T(8,128)(2,1)}, bf16[2048,256]{1,0:T(8,128)(2,1)}, f32[16,1024]{1,0:T(8,128)}, f32[128,1024]{1,0:T(8,128)}, f32[128,1024]{1...) custom-call(bf16[2048,768]{1,0:T(8,128)(2,1)} %copy-done.1, ...), custom_call_target="tpu_custom_call" | custom-call | flops 6442450944 | bytes 41943040 | tf_op jit(solution)/shard_map/pallas_call | solution.py:1102
  527.2 1.6 fusion.12
  529.5 2.1 copy.94
  531.7 1.8 fusion.11
  533.4 1.7 copy.93
  535.7 1.0 copy.112
  536.7 1.0 copy.113
  (92 shorter events, 15.4 us)
Async XLA Ops:
  7.2 4.3 copy-start.7
  7.2 5.2 copy-start.8
  7.2 6.6 %copy-start.4 = (bf16[2048,256]{1,0:T(8,128)(2,1)S(1)}, bf16[2048,256]{1,0:T(8,128)(2,1)}, u32[]{:S(2)}) copy-start(bf16[2048,256]{1,0:T(8,128)(2,1)} %param.21) | copy-start | bytes 3145732
  7.2 53.0 %all-gather.7.cloned.1.call-start = ((), (), s32[]{:S(2)}) async-start(), calls=%async_computation.2 | async-start | bytes 5242880 | tf_op jit(solution)/shard_map/all_gather | solution.py:1209
  8.0 97.0 %all-gather.5.cloned.1.call-start = ((), (), s32[]{:S(2)}) async-start(), calls=%async_computation.1 | async-start | bytes 1769472 | tf_op jit(solution)/shard_map/all_gather | solution.py:1203
  11.5 143.8 %all-gather.11.cloned.1.call-start = ((), (), s32[]{:S(2)}) async-start(), calls=%async_computation.4 | async-start | bytes 2359296 | tf_op jit(solution)/shard_map/all_gather | solution.py:1212
  12.4 193.3 %all-gather.9.cloned.1.call-start = ((), (), s32[]{:S(2)}) async-start(), calls=%async_computation.3 | async-start | bytes 2359296 | tf_op jit(solution)/shard_map/all_gather | solution.py:1211
  13.9 5.7 %copy-start = (s32[1,2]{1,0:T(1,128)S(1)}, s32[1,2]{1,0:T(1,128)}, u32[]{:S(2)}) copy-start(s32[1,2]{1,0:T(1,128)} %param.23) | copy-start | bytes 28
  13.9 6.0 %copy-start.14 = (s32[1,32,4,3]{1,2,3,0:T(4,128)S(1)}, s32[1,32,4,3]{1,2,3,0:T(4,128)}, u32[]{:S(2)}) copy-start(s32[1,32,4,3]{1,2,3,0:T(4,128)} %param.24) | copy-start | bytes 4612
  15.1 7.3 %copy-start.11 = (f32[256,128]{1,0:T(8,128)S(1)}, f32[256,128]{1,0:T(8,128)}, u32[]{:S(2)}) copy-start(f32[256,128]{1,0:T(8,128)} %param.30) | copy-start | bytes 393220
  15.1 7.4 %copy-start.12 = (f32[1024]{0:T(1024)S(1)}, f32[1024]{0:T(1024)}, u32[]{:S(2)}) copy-start(f32[1024]{0:T(1024)} %param.31) | copy-start | bytes 12292
  15.1 7.4 %copy-start.15 = (f32[1024]{0:T(1024)S(1)}, f32[1024]{0:T(1024)}, u32[]{:S(2)}) copy-start(f32[1024]{0:T(1024)} %param.32) | copy-start | bytes 12292
  15.1 7.4 %copy-start.16 = (f32[1024]{0:T(1024)S(1)}, f32[1024]{0:T(1024)}, u32[]{:S(2)}) copy-start(f32[1024]{0:T(1024)} %param.33) | copy-start | bytes 12292
  15.1 7.5 %copy-start.17 = (f32[1024]{0:T(1024)S(1)}, f32[1024]{0:T(1024)}, u32[]{:S(2)}) copy-start(f32[1024]{0:T(1024)} %param.37) | copy-start | bytes 12292
  15.1 7.4 %copy-start.18 = (f32[1024]{0:T(1024)S(1)}, f32[1024]{0:T(1024)}, u32[]{:S(2)}) copy-start(f32[1024]{0:T(1024)} %param.38) | copy-start | bytes 12292
  15.2 7.4 %copy-start.19 = (f32[1024]{0:T(1024)S(1)}, f32[1024]{0:T(1024)}, u32[]{:S(2)}) copy-start(f32[1024]{0:T(1024)} %param.39) | copy-start | bytes 12292
  15.2 8.1 %copy-start.20 = (f32[4096]{0:T(1024)S(1)}, f32[4096]{0:T(1024)}, u32[]{:S(2)}) copy-start(f32[4096]{0:T(1024)} %param.35) | copy-start | bytes 49156
  15.2 43.9 %all-to-all-start = ((bf16[4,512,256]{2,1,0:T(8,128)(2,1)}), bf16[4,512,256]{2,1,0:T(8,128)(2,1)S(1)}, u32[]{:S(2)}, u32[]{:S(2)}) async-start(bf16[4,512,256]{2,1,0:T(8,128)(2,1)} %bitcast.7), calls=%async_computation | async-start | bytes 2097152 | tf_op jit(solution)/shard_map/all_to_all | solution.py:1152
  105.0 3.7 copy-start.10
  105.0 4.1 copy-start.21
  360.2 28.1 %copy-start.13 = (f32[8,1024]{1,0:T(8,128)S(1)}, f32[8,1024]{1,0:T(8,128)}, u32[]{:S(2)}) copy-start(f32[8,1024]{1,0:T(8,128)} %get-tuple-element.44) | copy-start | bytes 98308
  527.1 8.6 %copy-start.6 = (bf16[2048,256]{1,0:T(8,128)(2,1)S(1)}, bf16[2048,256]{1,0:T(8,128)(2,1)}, u32[]{:S(2)}) copy-start(bf16[2048,256]{1,0:T(8,128)(2,1)} %get-tuple-element.174) | copy-start | bytes 3145732
  529.5 7.2 %copy-start.5 = (bf16[2048,256]{1,0:T(8,128)(2,1)S(1)}, bf16[2048,256]{1,0:T(8,128)(2,1)}, u32[]{:S(2)}) copy-start(bf16[2048,256]{1,0:T(8,128)(2,1)} %get-tuple-element.175) | copy-start | bytes 3145732
  535.7 1.9 copy-start.9
  (3 other events, 3.8 us)
Sparse Core Ops, SparseCore 0:
  9.6 48.9 all-gather.6
  60.8 44.1 all-gather.4
  107.1 48.0 all-gather.10
  157.8 47.7 all-gather.8

commit v4 on v3

--- a/solution.py
+++ b/solution.py
@@ -11,6 +11,7 @@
 DH = 64
 BLK = 64
 MESH = pl.DeviceIdType.MESH
+KINDS = 4
 
 
 epsilon = 1e-06
@@ -48,8 +49,7 @@
     apart = [
         [random_ref[base + head * 3 + slot] for head in range(head_count)] for slot in range(3)
     ]
-    at = lambda block: pl.multiple_of(block * BLK, BLK)
-    return [at(block) for block in shared], [[at(block) for block in row] for row in apart]
+    return shared, apart
 
 
 def lane_groups(head_count):
@@ -61,14 +61,14 @@
 
 
 def picked_rows(rows_ref, shared, apart, head_count):
-    pieces = [rows_ref[pl.ds(start, BLK), :] for start in shared]
-    for starts in apart:
+    pieces = [rows_ref[block] for block in shared]
+    for blocks in apart:
         groups = []
         for lane, width, heads in lane_groups(head_count):
             lane_head = lane_heads(BLK, width)
-            piece = rows_ref[pl.ds(starts[heads[0]], BLK), lane : lane + width]
+            piece = rows_ref[blocks[heads[0]], :, lane : lane + width]
             for place, head in enumerate(heads[1:], 1):
-                other = rows_ref[pl.ds(starts[head], BLK), lane : lane + width]
+                other = rows_ref[blocks[head], :, lane : lane + width]
                 piece = jnp.where(lane_head >= place, other, piece)
             groups.append(piece)
         pieces.append(jnp.concatenate(groups, axis=1) if len(groups) > 1 else groups[0])
@@ -76,14 +76,14 @@
 
 
 def put_rows(sums_ref, values_in, shared, apart, head_count):
-    for slot, start in enumerate(shared):
-        sums_ref[pl.ds(start, BLK), :] += values_in[slot * BLK : (slot + 1) * BLK, :]
-    for slot, starts in enumerate(apart, len(shared)):
+    for slot, block in enumerate(shared):
+        sums_ref[block] += values_in[slot * BLK : (slot + 1) * BLK, :]
+    for slot, blocks in enumerate(apart, len(shared)):
         rows = values_in[slot * BLK : (slot + 1) * BLK, :]
         for lane, width, heads in lane_groups(head_count):
             lane_head = lane_heads(BLK, width)
             for place, head in enumerate(heads):
-                sums_ref[pl.ds(starts[head], BLK), lane : lane + width] += jnp.where(
+                sums_ref[blocks[head], :, lane : lane + width] += jnp.where(
                     lane_head == place, rows[:, lane : lane + width], 0.0
                 )
 
@@ -103,21 +103,14 @@
     ]
 
 
-def attend_kernel(
-    head_count,
-    unroll,
-    globals_ref,
-    random_ref,
-    limits_ref,
-    queries_ref,
-    keys_ref,
-    values_ref,
-    context_ref,
-    highest_ref,
-    scale_ref,
+def attend_blocks(
+    first, count, unroll, globals_ref, random_ref, limits_ref, refs, context_ref, stat_refs
 ):
-    width = head_count * DH
-    num_blocks = queries_ref.shape[0] // BLK
+    queries_ref, keys_ref, values_ref = refs
+    highest_ref, scale_ref = stat_refs
+    seq_len, width = queries_ref.shape
+    head_count = width // DH
+    num_blocks = seq_len // BLK
 
     def one_block(step):
         shared, apart = slot_starts(step, num_blocks, head_count, globals_ref, random_ref)
@@ -143,10 +136,10 @@
         highest_ref[step] = highest
         scale_ref[step] = scale
 
-    @pl.loop(0, num_blocks // unroll)
+    @pl.loop(0, count // unroll)
     def _(turn):
         for place in range(unroll):
-            one_block(turn * unroll + place)
+            one_block(first + turn * unroll + place)
 
 
 def attend_back_kernel(
@@ -220,8 +213,9 @@
         for place in range(unroll):
             one_block(turn * unroll + place)
 
-    value_grad = value_sums[...].astype(jnp.bfloat16)
-    grads_out_ref[:, width : 2 * width] = key_sums[...].astype(jnp.bfloat16)
+    value_grad = value_sums[...].reshape(queries_ref.shape).astype(jnp.bfloat16)
+    seq_len = queries_ref.shape[0]
+    grads_out_ref[:, width : 2 * width] = key_sums[...].reshape(seq_len, width).astype(jnp.bfloat16)
     grads_out_ref[:, 2 * width :] = value_grad
     bias_ref[0:1, :] = jnp.sum(query_total[...], axis=0, keepdims=True)
     bias_ref[1:2, :] = jnp.sum(value_grad.astype(jnp.float32), axis=0, keepdims=True)
@@ -250,25 +244,6 @@
 SMEM = pl.BlockSpec(memory_space=pltpu.SMEM)
 
 
-def attend(queries, key_rows, value_rows, tables):
-    seq_len, width = queries.shape
-    head_count = width // DH
-    num_blocks = seq_len // BLK
-    stat = jax.ShapeDtypeStruct((num_blocks, 1, width), jnp.float32)
-    return pl.pallas_call(
-        functools.partial(attend_kernel, head_count, 2),
-        out_shape=(jax.ShapeDtypeStruct((seq_len, width), jnp.bfloat16), stat, stat),
-        in_specs=[SMEM] * 2 + [VMEM] * 4,
-        out_specs=[VMEM] * 3,
-        compiler_params=pltpu.CompilerParams(vmem_limit_bytes=32 * 1024 * 1024),
-        cost_estimate=pl.CostEstimate(
-            flops=4 * seq_len * 512 * width * head_count,
-            bytes_accessed=8 * seq_len * width,
-            transcendentals=seq_len * 512 * head_count,
-        ),
-    )(*tables, queries, key_rows, value_rows)
-
-
 def attend_back(queries, key_rows, value_rows, tables, stats, context_grad):
     seq_len, width = queries.shape
     head_count = width // DH
@@ -280,7 +255,7 @@
         ),
         in_specs=[SMEM] * 2 + [VMEM] * 7,
         out_specs=[VMEM] * 2,
-        scratch_shapes=[pltpu.VMEM((seq_len, width), jnp.float32)] * 2
+        scratch_shapes=[pltpu.VMEM((seq_len // BLK, BLK, width), jnp.float32)] * 2
         + [pltpu.VMEM((8, width), jnp.float32)],
         compiler_params=pltpu.CompilerParams(vmem_limit_bytes=40 * 1024 * 1024),
         cost_estimate=pl.CostEstimate(
@@ -738,7 +713,294 @@
     )(context, inputs, upstream, valid, out_own, up_own, down_own, vectors, b_up_pair)
 
 
-KINDS = 4
+def front_kernel(
+    levels,
+    across,
+    along,
+    globals_ref,
+    random_ref,
+    limits_ref,
+    hidden_ref,
+    grads_ref,
+    b_query_ref,
+    b_value_ref,
+    part_qkv_ref,
+    part_out_ref,
+    part_up_ref,
+    part_down_ref,
+    features_ref,
+    own_ref,
+    upstream_ref,
+    queries_ref,
+    keys_ref,
+    values_ref,
+    context_ref,
+    highest_ref,
+    scale_ref,
+    full_qkv_ref,
+    full_out_ref,
+    full_up_ref,
+    full_down_ref,
+    level_send,
+    level_recv,
+    core_send,
+    core_recv,
+    swap_send,
+    swap_recv,
+    along_send,
+    along_recv,
+    across_send,
+    across_recv,
+):
+    low, full = jnp.bfloat16, jnp.float32
+    row, column = lax.axis_index("row"), lax.axis_index("col")
+    core, level = lax.rem(column, 2), lax.div(column, 2)
+    fast, slow = lax.rem(row, across), lax.div(row, across)
+    cols = 2 * levels
+    seq_len, width = hidden_ref.shape
+    own_len = seq_len // cols
+    shard = part_qkv_ref.shape[0]
+    other = 1 - core
+    sibling = (row, level * 2 + other)
+    offsets = range(1, levels)
+
+    def peer_level(offset):
+        return lax.rem(level + offset, levels)
+
+    def fast_peer(offset):
+        return slow * across + lax.rem(fast + offset, across)
+
+    def slow_peer(offset):
+        return lax.rem(slow + offset, along) * across + fast
+
+    barrier = pltpu.get_barrier_semaphore()
+    greeted = [sibling]
+    for offset in offsets:
+        greeted += [(row, peer_level(offset) * 2 + core), (row, peer_level(offset) * 2 + other)]
+    greeted += [(fast_peer(offset), column) for offset in range(1, across)]
+    greeted += [(slow_peer(offset), column) for offset in range(1, along)]
+    for device in greeted:
+        pl.semaphore_signal(barrier, inc=1, device_id=device, device_id_type=MESH)
+    pl.semaphore_wait(barrier, len(greeted))
+
+    def remote(source, target, send, recv, device):
+        return pltpu.make_async_remote_copy(
+            src_ref=source,
+            dst_ref=target,
+            send_sem=send,
+            recv_sem=recv,
+            device_id=device,
+            device_id_type=MESH,
+        )
+
+    def block(start, size):
+        return pl.ds(pl.multiple_of(start * size, size), size)
+
+    def level_copy(turn, offset):
+        rows = block(turn, own_len)
+        return remote(
+            hidden_ref.at[rows],
+            features_ref.at[rows, block(column, width)],
+            level_send.at[turn, offset - 1],
+            level_recv.at[turn, levels - offset - 1],
+            (row, peer_level(offset) * 2 + core),
+        )
+
+    def core_copy(turn, offset):
+        view = features_ref.at[block(turn, own_len), block(peer_level(offset) * 2 + core, width)]
+        return remote(
+            view, view, core_send.at[turn, offset], core_recv.at[turn, offset], sibling
+        )
+
+    @pl.loop(0, cols)
+    def _(turn):
+        for offset in offsets:
+            level_copy(turn, offset).start()
+        rows = block(turn, own_len)
+        features_ref[rows, block(column, width)] = hidden_ref[rows, :]
+        core_copy(turn, 0).start()
+
+    parts = (part_qkv_ref, part_out_ref, part_up_ref, part_down_ref)
+    fulls = (full_qkv_ref, full_out_ref, full_up_ref, full_down_ref)
+
+    def shard_rows(place):
+        return block(place * across + fast, shard)
+
+    def along_copy(kind, offset):
+        view = fulls[kind].at[shard_rows(slow)]
+        return remote(
+            view,
+            view,
+            along_send.at[kind, offset - 1],
+            along_recv.at[kind, along - offset - 1],
+            (slow_peer(offset), column),
+        )
+
+    def across_copy(kind, place, offset):
+        view = fulls[kind].at[shard_rows(place)]
+        return remote(
+            view,
+            view,
+            across_send.at[kind, place, offset - 1],
+            across_recv.at[kind, place, across - offset - 1],
+            (fast_peer(offset), column),
+        )
+
+    for kind in range(KINDS):
+        fulls[kind][shard_rows(slow), :] = parts[kind][...]
+        for offset in range(1, along):
+            along_copy(kind, offset).start()
+        for offset in range(1, across):
+            across_copy(kind, slow, offset).start()
+
+    def swap_copy(target, place_out, place_in):
+        return remote(
+            grads_ref.at[block(target, own_len)],
+            upstream_ref.at[:, block(column, width)],
+            swap_send.at[place_out],
+            swap_recv.at[place_in],
+            (row, target),
+        )
+
+    swaps = [swap_copy(level * 2 + other, 0, 0)]
+    for offset in offsets:
+        back = levels - offset
+        swaps.append(swap_copy(peer_level(offset) * 2 + core, 2 * offset - 1, 2 * back - 1))
+        swaps.append(swap_copy(peer_level(offset) * 2 + other, 2 * offset, 2 * back))
+    for copy in swaps:
+        copy.start()
+    upstream_ref[:, block(column, width)] = grads_ref[block(column, own_len), :]
+
+    def pass_on(kind):
+        for offset in range(1, along):
+            along_copy(kind, along - offset).wait_recv()
+            for step in range(1, across):
+                across_copy(kind, lax.rem(slow + offset, along), step).start()
+
+    def await_shards(kind):
+        @pl.loop(0, along)
+        def _(place):
+            for offset in range(1, across):
+                across_copy(kind, place, offset).wait_recv()
+
+    pass_on(0)
+    await_shards(0)
+
+    @pl.loop(0, cols)
+    def _(turn):
+        rows = block(turn, own_len)
+        for offset in offsets:
+            level_copy(turn, levels - offset).wait_recv()
+            core_copy(turn, offset).start()
+        for offset in range(levels):
+            core_copy(turn, offset).wait_recv()
+        values_in = features_ref[rows, :]
+        queries_ref[rows, :] = (
+            dot(values_in, full_qkv_ref[:, :width]) + b_query_ref[...]
+        ).astype(low)
+        blocks = pl.ds(turn * (own_len // BLK), own_len // BLK)
+        by_block = (own_len // BLK, BLK, width)
+        keys_ref[blocks] = (
+            dot(values_in, full_qkv_ref[:, width : 2 * width]).astype(low).reshape(by_block)
+        )
+        values_ref[blocks] = (
+            (dot(values_in, full_qkv_ref[:, 2 * width :]) + b_value_ref[...])
+            .astype(low)
+            .reshape(by_block)
+        )
+
+    own_ref[...] = features_ref[block(column, own_len), :]
+    pass_on(1)
+    count = seq_len // BLK // 4
+    for part in range(4):
+        attend_blocks(
+            part * count,
+            count,
+            2,
+            globals_ref,
+            random_ref,
+            limits_ref,
+            (queries_ref, keys_ref, values_ref),
+            context_ref,
+            (highest_ref, scale_ref),
+        )
+        if part == 1:
+            pass_on(2)
+    pass_on(3)
+    for kind in range(1, KINDS):
+        await_shards(kind)
+    for copy in swaps:
+        copy.wait()
+    for kind in range(KINDS):
+        for offset in range(1, along):
+            along_copy(kind, offset).wait_send()
+
+        @pl.loop(0, along)
+        def _(place):
+            for offset in range(1, across):
+                across_copy(kind, place, offset).wait_send()
+
+    @pl.loop(0, cols)
+    def _(turn):
+        for offset in offsets:
+            level_copy(turn, offset).wait_send()
+        for offset in range(levels):
+            core_copy(turn, offset).wait_send()
+
+
+def across_of(rows):
+    return 2 if rows <= 8 else rows // 4
+
+
+def front(levels, rows, tables, hidden_in, grads, biases, parts):
+    low, full = jnp.bfloat16, jnp.float32
+    shape = jax.ShapeDtypeStruct
+    across = across_of(rows)
+    along = rows // across
+    seq_len, width = hidden_in.shape
+    cols = 2 * levels
+    own_len = seq_len // cols
+    features_all = width * cols
+    others = levels - 1
+    stat = shape((seq_len // BLK, 1, width), full)
+    dma = pltpu.SemaphoreType.DMA
+    return pl.pallas_call(
+        functools.partial(front_kernel, levels, across, along),
+        out_shape=(
+            shape((seq_len, features_all), low),
+            shape((own_len, features_all), low),
+            shape((own_len, features_all), low),
+            shape((seq_len, width), low),
+            shape((seq_len // BLK, BLK, width), low),
+            shape((seq_len // BLK, BLK, width), low),
+            shape((seq_len, width), low),
+            stat,
+            stat,
+            *(shape((part.shape[0] * rows, part.shape[1]), low) for part in parts),
+        ),
+        in_specs=[SMEM] * 2 + [VMEM] * 9,
+        out_specs=[VMEM] * 13,
+        scratch_shapes=[
+            dma((cols, others)),
+            dma((cols, others)),
+            dma((cols, levels)),
+            dma((cols, levels)),
+            dma((cols,)),
+            dma((cols,)),
+            dma((KINDS, along - 1)),
+            dma((KINDS, along - 1)),
+            dma((KINDS, along, across - 1)),
+            dma((KINDS, along, across - 1)),
+        ],
+        compiler_params=pltpu.CompilerParams(
+            collective_id=3, has_side_effects=True, vmem_limit_bytes=48 * 1024 * 1024
+        ),
+        cost_estimate=pl.CostEstimate(
+            flops=2 * seq_len * features_all * 3 * width,
+            bytes_accessed=20 * 1024 * 1024,
+            transcendentals=seq_len * 512 * (width // DH),
+        ),
+    )(*tables, hidden_in, grads, *biases, *parts)
 
 
 def end_kernel(
@@ -1088,7 +1350,7 @@
 ):
     low, full = jnp.bfloat16, jnp.float32
     shape = jax.ShapeDtypeStruct
-    across = 2 if rows <= 8 else rows // 4
+    across = across_of(rows)
     along = rows // across
     seq_len, features_all = features.shape
     width = query_key_value.shape[1] // 3
@@ -1148,10 +1410,6 @@
     )(query_key_value, weights, features, attn_full, layer_own, small, down, up, out)
 
 
-def to_tokens(portion):
-    return lax.all_to_all(portion, "col", split_axis=0, concat_axis=1, tiled=True)
-
-
 def into_full(portion, start_at, full_len):
     return lax.dynamic_update_slice_in_dim(
         jnp.zeros((full_len,), jnp.float32), portion, start_at, 0
@@ -1200,32 +1458,38 @@
         rand_blocks.reshape(-1),
         limits_of(length, global_blocks[0], rand_blocks[0], num_blocks, head_count),
     )
-    full_qkv = lax.all_gather(
-        jnp.concatenate([w_query.astype(low), w_key.astype(low), w_value.astype(low)], axis=1),
-        "row",
-        axis=0,
-        tiled=True,
-    )
-    features = lax.all_gather(hidden_in, "col", axis=1, tiled=True)
-    full_out = lax.all_gather(w_out.astype(low).T, "row", axis=0, tiled=True)
-    full_up = lax.all_gather(w_up.astype(low), "row", axis=0, tiled=True)
-    full_down = lax.all_gather(w_down.astype(low).T, "row", axis=0, tiled=True)
-    own_features = lax.dynamic_slice_in_dim(features, own_start, own_len, 0)
     valid = (jnp.arange(seq_len) < length)[:, None]
-    upstream = to_tokens(jnp.where(valid, out_grad, 0))
     own_valid = (own_start + jnp.arange(own_len) < length).astype(jnp.float32)[:, None]
-
-    full_query = full_qkv[:, :feat_cols]
-    full_key = full_qkv[:, feat_cols : 2 * feat_cols]
-    full_value = full_qkv[:, 2 * feat_cols :]
-    queries = (
-        dot(features, full_query) + lax.dynamic_slice_in_dim(b_query, feat_start, feat_cols)
-    ).astype(low)
-    key_rows = dot(features, full_key).astype(low)
-    value_rows = (
-        dot(features, full_value) + lax.dynamic_slice_in_dim(b_value, feat_start, feat_cols)
-    ).astype(low)
-    context, *stats = attend(queries, key_rows, value_rows, tables)
+    (
+        features,
+        own_features,
+        upstream,
+        queries,
+        key_rows,
+        value_rows,
+        context,
+        *stats,
+        full_qkv,
+        full_out,
+        full_up,
+        full_down,
+    ) = front(
+        cols // 2,
+        lax.axis_size("row"),
+        tables,
+        hidden_in,
+        jnp.where(valid, out_grad, 0),
+        (
+            lax.dynamic_slice_in_dim(b_query, feat_start, feat_cols)[None, :],
+            lax.dynamic_slice_in_dim(b_value, feat_start, feat_cols)[None, :],
+        ),
+        (
+            jnp.concatenate([w_query, w_key, w_value], axis=1).astype(low),
+            w_out.T.astype(low),
+            w_up.astype(low),
+            w_down.T.astype(low),
+        ),
+    )
 
     sibling = column + 1 - 2 * lax.rem(column, 2)
     layer_own, context_grad, attn_full, small, up_small, grad_up, grad_down, grad_out = middle(

time: 546 us -> 464 us (0.85)
  waiting for transfers between devices: 116 us -> 0 us
  Pallas kernels: 337 us -> 429 us
  blocking collectives: 34.3 us -> 0 us
  between operations: 14.8 us -> 1.69 us
  matrix products: 6.34 us -> 0 us
    all_gather x4 -> x0, waiting for transfers between devices: 115 us -> none  [the longest x1 50.4 us: on_device(): full_up = lax.all_gather(w_up.astype(low), 'row', axis=0, tiled=True)]
    pallas_call x1, Pallas kernels: 20.4 us -> 96.5 us  [front(): pl.pallas_call(functools.partial(front_kernel, levels, across, along), ou...]
    all_gather x1 -> x0, blocking collectives: 34.3 us -> none  [on_device(): full_out = lax.all_gather(w_out.astype(low).T, 'row', axis=0, tiled=True)]
    pallas_call x1, Pallas kernels: 138 us -> 154 us  [finish(): pl.pallas_call(functools.partial(end_kernel, levels, across, along), out_...]
    dot_general x3 -> x0, matrix products: 6.34 us -> none  [dot(): return jnp.dot(left, right, preferred_element_type=jnp.float32)]
    unnamed x54 -> x56, local copies, waits for them, and re-layouts: 13.2 us -> 16.5 us
  transfers between devices with their start and end apart: 5 -> 0, of which waited for: 3 -> 0; matrix products, arithmetic and copies ran while one was open for 4% -> 0% of each run, Pallas kernels for 4% -> 0%
where the time goes in v4:
time: 464 us; the launch traced here: 462 us
  Pallas kernels  429 us (92%)
  local copies, waits for them, and re-layouts  25.7 us (6%)
  other arithmetic  6.11 us (1%)
    pallas_call x1, Pallas kernels, finish(): pl.pallas_call(functools.partial(end_kernel, levels, across, along), out_...  154 us
    pallas_call x1, Pallas kernels, middle(): pl.pallas_call(functools.partial(middle_kernel, levels), out_shape=(shape...  152 us
    pallas_call x1, Pallas kernels, front(): pl.pallas_call(functools.partial(front_kernel, levels, across, along), ou...  96.5 us
    pallas_call x1, Pallas kernels, attend_back(): pl.pallas_call(functools.partial(attend_back_kernel, head_count, 2), out_...  26.4 us
    unnamed x56, local copies, waits for them, and re-layouts  16.5 us

profile of v4, /device:TPU:0, one launch (start us, length us, event | category | flops | bytes accessed | tf_op | source)
XLA Modules:
  0.0 462.4 jit_solution(12128171747305539346)
XLA Ops:
  0.7 0.8 fusion.5
  2.2 0.8 dynamic_slice.12
  2.9 0.8 dynamic_slice.13
  3.8 0.7 compare_reduce_fusion
  7.6 2.3 broadcast_select_fusion.grads_ref
  10.7 96.5 %shard_map.323 = (bf16[2048,1024]{1,0:T(8,128)(2,1)}, bf16[512,1024]{1,0:T(8,128)(2,1)S(1)}, bf16[512,1024]{1,0:T(8,128)(2,1)S(1)}, bf16[2048,256]{1,0:T(8,128)(...) custom-call(s32[2]{0:T(128)S(1)} %bitcast.51, ...), custom_call_target="tpu_custom_call" | custom-call | flops 3221225472 | bytes 20971520 | tf_op jit(solution)/shard_map/pallas_call | solution.py:967
  107.1 1.0 copy-done.3
  108.1 1.0 copy-done.4
  109.1 0.8 copy-done.5
  111.3 152.3 %shard_map.324 = (bf16[512,1024]{1,0:T(8,128)(2,1)}, bf16[2048,256]{1,0:T(8,128)(2,1)}, bf16[1024,1024]{1,0:T(8,128)(2,1)}, f32[8,1024]{1,0:T(8,128)}, f32[2,102...) custom-call(bf16[2048,256]{1,0:T(8,128)(2,1)} %get-tuple-element.50.c, ...), custom_call_target="tpu_custom_call" | custom-call | flops 28991029248 | bytes 41943040 | tf_op jit(solution)/shard_map/pallas_call | solution.py:666
  263.6 0.8 fusion.6
  264.7 1.2 copy-done.2
  266.0 1.2 copy-done.6
  267.2 26.4 %shard_map.325 = (bf16[2048,768]{1,0:T(8,128)(2,1)S(1)}, f32[2,256]{1,0:T(2,128)S(1)}) custom-call(s32[2]{0:T(128)S(1)} %bitcast.52, s32[384]{0:T(512)S(1)} %reshape.138.random_ref, s32[32,8,256]{2,1,0:T(8,128)S(1)} %pad_add_fusion.limits_ref, bf16[2048,256]{1,0:T(8,128)(2,1)S(1)} %get-tuple-element.47.queries_ref, ...), custom_call_target="tpu_custom_call" | custom-call | flops 10737418240 | bytes 7340032 | tf_op jit(solution)/shard_map/pallas_call | solution.py:250
  293.6 1.6 copy-done.1
  295.9 153.7 %shard_map.326 = (bf16[2048,256]{1,0:T(8,128)(2,1)}, bf16[2048,256]{1,0:T(8,128)(2,1)}, f32[16,1024]{1,0:T(8,128)}, f32[128,1024]{1,0:T(8,128)}, f32[128,1024]{1...) custom-call(bf16[2048,768]{1,0:T(8,128)(2,1)} %copy-done.1, bf16[1024,768]{1,0:T(8,128)(2,1)} %get-tuple-element.60.weights_ref, ...), custom_call_target="tpu_custom_call" | custom-call | flops 6442450944 | bytes 41943040 | tf_op jit(solution)/shard_map/pallas_call | solution.py:1364
  449.6 2.2 copy.74
  451.8 1.8 fusion.3
  453.6 1.7 copy.73
  455.2 1.7 fusion.4
  457.0 0.8 slice_bitcast_fusion
  458.3 2.3 copy.85
  460.6 1.0 copy.86
  461.6 0.8 copy.87
  (74 shorter events, 6.8 us)
Async XLA Ops:
  0.7 9.2 %copy-start.17 = (s32[1,32,4,3]{1,2,3,0:T(4,128)S(1)}, s32[1,32,4,3]{1,2,3,0:T(4,128)}, u32[]{:S(2)}) copy-start(s32[1,32,4,3]{1,2,3,0:T(4,128)} %param.24) | copy-start | bytes 4612
  0.7 9.5 %copy-start.11 = (f32[128,256]{1,0:T(8,128)S(1)}, f32[128,256]{1,0:T(8,128)}, u32[]{:S(2)}) copy-start(f32[128,256]{1,0:T(8,128)} %param.27) | copy-start | bytes 393220
  0.7 9.5 %copy-start.12 = (f32[128,256]{1,0:T(8,128)S(1)}, f32[128,256]{1,0:T(8,128)}, u32[]{:S(2)}) copy-start(f32[128,256]{1,0:T(8,128)} %param.28) | copy-start | bytes 393220
  0.7 9.5 %copy-start.13 = (f32[128,256]{1,0:T(8,128)S(1)}, f32[128,256]{1,0:T(8,128)}, u32[]{:S(2)}) copy-start(f32[128,256]{1,0:T(8,128)} %param.25) | copy-start | bytes 393220
  0.7 9.6 %copy-start.8 = (f32[1024,128]{1,0:T(8,128)S(1)}, f32[1024,128]{1,0:T(8,128)}, u32[]{:S(2)}) copy-start(f32[1024,128]{1,0:T(8,128)} %param.36) | copy-start | bytes 1572868
  0.7 9.7 %copy-start.9 = (f32[128,1024]{1,0:T(8,128)S(1)}, f32[128,1024]{1,0:T(8,128)}, u32[]{:S(2)}) copy-start(f32[128,1024]{1,0:T(8,128)} %param.34) | copy-start | bytes 1572868
  6.2 4.3 copy-start.14
  7.2 3.4 copy-start
  10.6 100.0 %copy-start.15 = (f32[1024]{0:T(1024)S(1)}, f32[1024]{0:T(1024)}, u32[]{:S(2)}) copy-start(f32[1024]{0:T(1024)} %param.31) | copy-start | bytes 12292
  10.6 100.0 %copy-start.18 = (f32[1024]{0:T(1024)S(1)}, f32[1024]{0:T(1024)}, u32[]{:S(2)}) copy-start(f32[1024]{0:T(1024)} %param.32) | copy-start | bytes 12292
  10.6 100.0 %copy-start.19 = (f32[1024]{0:T(1024)S(1)}, f32[1024]{0:T(1024)}, u32[]{:S(2)}) copy-start(f32[1024]{0:T(1024)} %param.33) | copy-start | bytes 12292
  10.6 100.0 %copy-start.20 = (f32[1024]{0:T(1024)S(1)}, f32[1024]{0:T(1024)}, u32[]{:S(2)}) copy-start(f32[1024]{0:T(1024)} %param.37) | copy-start | bytes 12292
  10.6 100.0 %copy-start.21 = (f32[1024]{0:T(1024)S(1)}, f32[1024]{0:T(1024)}, u32[]{:S(2)}) copy-start(f32[1024]{0:T(1024)} %param.38) | copy-start | bytes 12292
  10.7 100.0 %copy-start.22 = (f32[1024]{0:T(1024)S(1)}, f32[1024]{0:T(1024)}, u32[]{:S(2)}) copy-start(f32[1024]{0:T(1024)} %param.39) | copy-start | bytes 12292
  107.1 1.0 copy-start.3
  108.1 1.0 copy-start.4
  109.1 0.8 copy-start.5
  264.7 1.2 copy-start.2
  266.0 1.2 copy-start.6
  267.2 28.1 %copy-start.16 = (f32[8,1024]{1,0:T(8,128)S(1)}, f32[8,1024]{1,0:T(8,128)}, u32[]{:S(2)}) copy-start(f32[8,1024]{1,0:T(8,128)} %get-tuple-element.64) | copy-start | bytes 98308
  293.6 1.6 copy-start.1
  449.6 11.0 %copy-start.7 = (bf16[2048,256]{1,0:T(8,128)(2,1)S(1)}, bf16[2048,256]{1,0:T(8,128)(2,1)}, u32[]{:S(2)}) copy-start(bf16[2048,256]{1,0:T(8,128)(2,1)} %get-tuple-element.195) | copy-start | bytes 3145732
  449.6 11.9 %copy-start.10 = (f32[128,1024]{1,0:T(8,128)S(1)}, f32[128,1024]{1,0:T(8,128)}, u32[]{:S(2)}) copy-start(f32[128,1024]{1,0:T(8,128)} %get-tuple-element.205) | copy-start | bytes 1572868

commit v5 on v3

--- a/solution.py
+++ b/solution.py
@@ -48,8 +48,7 @@
     apart = [
         [random_ref[base + head * 3 + slot] for head in range(head_count)] for slot in range(3)
     ]
-    at = lambda block: pl.multiple_of(block * BLK, BLK)
-    return [at(block) for block in shared], [[at(block) for block in row] for row in apart]
+    return shared, apart
 
 
 def lane_groups(head_count):
@@ -61,14 +60,14 @@
 
 
 def picked_rows(rows_ref, shared, apart, head_count):
-    pieces = [rows_ref[pl.ds(start, BLK), :] for start in shared]
-    for starts in apart:
+    pieces = [rows_ref[block] for block in shared]
+    for blocks in apart:
         groups = []
         for lane, width, heads in lane_groups(head_count):
             lane_head = lane_heads(BLK, width)
-            piece = rows_ref[pl.ds(starts[heads[0]], BLK), lane : lane + width]
+            piece = rows_ref[blocks[heads[0]], :, lane : lane + width]
             for place, head in enumerate(heads[1:], 1):
-                other = rows_ref[pl.ds(starts[head], BLK), lane : lane + width]
+                other = rows_ref[blocks[head], :, lane : lane + width]
                 piece = jnp.where(lane_head >= place, other, piece)
             groups.append(piece)
         pieces.append(jnp.concatenate(groups, axis=1) if len(groups) > 1 else groups[0])
@@ -76,14 +75,14 @@
 
 
 def put_rows(sums_ref, values_in, shared, apart, head_count):
-    for slot, start in enumerate(shared):
-        sums_ref[pl.ds(start, BLK), :] += values_in[slot * BLK : (slot + 1) * BLK, :]
-    for slot, starts in enumerate(apart, len(shared)):
+    for slot, block in enumerate(shared):
+        sums_ref[block] += values_in[slot * BLK : (slot + 1) * BLK, :]
+    for slot, blocks in enumerate(apart, len(shared)):
         rows = values_in[slot * BLK : (slot + 1) * BLK, :]
         for lane, width, heads in lane_groups(head_count):
             lane_head = lane_heads(BLK, width)
             for place, head in enumerate(heads):
-                sums_ref[pl.ds(starts[head], BLK), lane : lane + width] += jnp.where(
+                sums_ref[blocks[head], :, lane : lane + width] += jnp.where(
                     lane_head == place, rows[:, lane : lane + width], 0.0
                 )
 
@@ -103,21 +102,14 @@
     ]
 
 
-def attend_kernel(
-    head_count,
-    unroll,
-    globals_ref,
-    random_ref,
-    limits_ref,
-    queries_ref,
-    keys_ref,
-    values_ref,
-    context_ref,
-    highest_ref,
-    scale_ref,
+def attend_blocks(
+    first, count, unroll, globals_ref, random_ref, limits_ref, refs, context_ref, stat_refs
 ):
-    width = head_count * DH
-    num_blocks = queries_ref.shape[0] // BLK
+    queries_ref, keys_ref, values_ref = refs
+    highest_ref, scale_ref = stat_refs
+    seq_len, width = queries_ref.shape
+    head_count = width // DH
+    num_blocks = seq_len // BLK
 
     def one_block(step):
         shared, apart = slot_starts(step, num_blocks, head_count, globals_ref, random_ref)
@@ -143,10 +135,10 @@
         highest_ref[step] = highest
         scale_ref[step] = scale
 
-    @pl.loop(0, num_blocks // unroll)
+    @pl.loop(0, count // unroll)
     def _(turn):
         for place in range(unroll):
-            one_block(turn * unroll + place)
+            one_block(first + turn * unroll + place)
 
 
 def attend_back_kernel(
@@ -220,8 +212,9 @@
         for place in range(unroll):
             one_block(turn * unroll + place)
 
-    value_grad = value_sums[...].astype(jnp.bfloat16)
-    grads_out_ref[:, width : 2 * width] = key_sums[...].astype(jnp.bfloat16)
+    value_grad = value_sums[...].reshape(queries_ref.shape).astype(jnp.bfloat16)
+    seq_len = queries_ref.shape[0]
+    grads_out_ref[:, width : 2 * width] = key_sums[...].reshape(seq_len, width).astype(jnp.bfloat16)
     grads_out_ref[:, 2 * width :] = value_grad
     bias_ref[0:1, :] = jnp.sum(query_total[...], axis=0, keepdims=True)
     bias_ref[1:2, :] = jnp.sum(value_grad.astype(jnp.float32), axis=0, keepdims=True)
@@ -250,25 +243,6 @@
 SMEM = pl.BlockSpec(memory_space=pltpu.SMEM)
 
 
-def attend(queries, key_rows, value_rows, tables):
-    seq_len, width = queries.shape
-    head_count = width // DH
-    num_blocks = seq_len // BLK
-    stat = jax.ShapeDtypeStruct((num_blocks, 1, width), jnp.float32)
-    return pl.pallas_call(
-        functools.partial(attend_kernel, head_count, 2),
-        out_shape=(jax.ShapeDtypeStruct((seq_len, width), jnp.bfloat16), stat, stat),
-        in_specs=[SMEM] * 2 + [VMEM] * 4,
-        out_specs=[VMEM] * 3,
-        compiler_params=pltpu.CompilerParams(vmem_limit_bytes=32 * 1024 * 1024),
-        cost_estimate=pl.CostEstimate(
-            flops=4 * seq_len * 512 * width * head_count,
-            bytes_accessed=8 * seq_len * width,
-            transcendentals=seq_len * 512 * head_count,
-        ),
-    )(*tables, queries, key_rows, value_rows)
-
-
 def attend_back(queries, key_rows, value_rows, tables, stats, context_grad):
     seq_len, width = queries.shape
     head_count = width // DH
@@ -280,7 +254,7 @@
         ),
         in_specs=[SMEM] * 2 + [VMEM] * 7,
         out_specs=[VMEM] * 2,
-        scratch_shapes=[pltpu.VMEM((seq_len, width), jnp.float32)] * 2
+        scratch_shapes=[pltpu.VMEM((seq_len // BLK, BLK, width), jnp.float32)] * 2
         + [pltpu.VMEM((8, width), jnp.float32)],
         compiler_params=pltpu.CompilerParams(vmem_limit_bytes=40 * 1024 * 1024),
         cost_estimate=pl.CostEstimate(
@@ -291,6 +265,301 @@
     )(*tables, queries, key_rows, value_rows, context_grad, *stats)
 
 
+FRONT_KINDS = 3
+SEGMENTS = 8
+
+
+def front_kernel(
+    levels,
+    across,
+    along,
+    globals_ref,
+    random_ref,
+    limits_ref,
+    hidden_ref,
+    grads_ref,
+    b_query_ref,
+    b_value_ref,
+    part_qkv_ref,
+    part_out_ref,
+    part_up_ref,
+    features_ref,
+    own_ref,
+    upstream_ref,
+    queries_ref,
+    keys_ref,
+    values_ref,
+    context_ref,
+    highest_ref,
+    scale_ref,
+    full_qkv_ref,
+    full_out_ref,
+    full_up_ref,
+    level_send,
+    level_recv,
+    core_send,
+    core_recv,
+    swap_send,
+    swap_recv,
+    along_send,
+    along_recv,
+    across_send,
+    across_recv,
+):
+    low, full = jnp.bfloat16, jnp.float32
+    row, column = lax.axis_index("row"), lax.axis_index("col")
+    core, level = lax.rem(column, 2), lax.div(column, 2)
+    fast, slow = lax.rem(row, across), lax.div(row, across)
+    cols = 2 * levels
+    seq_len, width = hidden_ref.shape
+    own_len = seq_len // cols
+    shard = part_qkv_ref.shape[0]
+    other = 1 - core
+    sibling = (row, level * 2 + other)
+    offsets = range(1, levels)
+
+    def peer_level(offset):
+        return lax.rem(level + offset, levels)
+
+    def fast_peer(offset):
+        return slow * across + lax.rem(fast + offset, across)
+
+    def slow_peer(offset):
+        return lax.rem(slow + offset, along) * across + fast
+
+    barrier = pltpu.get_barrier_semaphore()
+    greeted = [sibling]
+    for offset in offsets:
+        greeted += [(row, peer_level(offset) * 2 + core), (row, peer_level(offset) * 2 + other)]
+    greeted += [(fast_peer(offset), column) for offset in range(1, across)]
+    greeted += [(slow_peer(offset), column) for offset in range(1, along)]
+    for device in greeted:
+        pl.semaphore_signal(barrier, inc=1, device_id=device, device_id_type=MESH)
+    pl.semaphore_wait(barrier, len(greeted))
+
+    def remote(source, target, send, recv, device):
+        return pltpu.make_async_remote_copy(
+            src_ref=source,
+            dst_ref=target,
+            send_sem=send,
+            recv_sem=recv,
+            device_id=device,
+            device_id_type=MESH,
+        )
+
+    def block(start, size):
+        return pl.ds(pl.multiple_of(start * size, size), size)
+
+    def level_copy(turn, offset):
+        rows = block(turn, own_len)
+        return remote(
+            hidden_ref.at[rows],
+            features_ref.at[rows, block(column, width)],
+            level_send.at[turn, offset - 1],
+            level_recv.at[turn, levels - offset - 1],
+            (row, peer_level(offset) * 2 + core),
+        )
+
+    def core_copy(turn, offset):
+        view = features_ref.at[block(turn, own_len), block(peer_level(offset) * 2 + core, width)]
+        return remote(
+            view, view, core_send.at[turn, offset], core_recv.at[turn, offset], sibling
+        )
+
+    @pl.loop(0, cols)
+    def _(turn):
+        for offset in offsets:
+            level_copy(turn, offset).start()
+        rows = block(turn, own_len)
+        features_ref[rows, block(column, width)] = hidden_ref[rows, :]
+        core_copy(turn, 0).start()
+
+    parts = (part_qkv_ref, part_out_ref, part_up_ref)
+    fulls = (full_qkv_ref, full_out_ref, full_up_ref)
+
+    def shard_rows(place):
+        return block(place * across + fast, shard)
+
+    def along_copy(kind, offset):
+        view = fulls[kind].at[shard_rows(slow)]
+        return remote(
+            view,
+            view,
+            along_send.at[kind, offset - 1],
+            along_recv.at[kind, along - offset - 1],
+            (slow_peer(offset), column),
+        )
+
+    def across_copy(kind, place, offset):
+        view = fulls[kind].at[shard_rows(place)]
+        return remote(
+            view,
+            view,
+            across_send.at[kind, place, offset - 1],
+            across_recv.at[kind, place, across - offset - 1],
+            (fast_peer(offset), column),
+        )
+
+    for kind in range(FRONT_KINDS):
+        fulls[kind][shard_rows(slow), :] = parts[kind][...]
+        for offset in range(1, along):
+            along_copy(kind, offset).start()
+        for offset in range(1, across):
+            across_copy(kind, slow, offset).start()
+
+    def swap_copy(target, place_out, place_in):
+        return remote(
+            grads_ref.at[block(target, own_len)],
+            upstream_ref.at[:, block(column, width)],
+            swap_send.at[place_out],
+            swap_recv.at[place_in],
+            (row, target),
+        )
+
+    swaps = [swap_copy(level * 2 + other, 0, 0)]
+    for offset in offsets:
+        back = levels - offset
+        swaps.append(swap_copy(peer_level(offset) * 2 + core, 2 * offset - 1, 2 * back - 1))
+        swaps.append(swap_copy(peer_level(offset) * 2 + other, 2 * offset, 2 * back))
+    for copy in swaps:
+        copy.start()
+    upstream_ref[:, block(column, width)] = grads_ref[block(column, own_len), :]
+
+    waiting = [(kind, offset) for kind in range(FRONT_KINDS) for offset in range(1, along)]
+
+    def pass_on(count):
+        for kind, offset in waiting[:count]:
+            along_copy(kind, along - offset).wait_recv()
+            for step in range(1, across):
+                across_copy(kind, lax.rem(slow + offset, along), step).start()
+        del waiting[:count]
+
+    def await_shards(kind):
+        @pl.loop(0, along)
+        def _(place):
+            for offset in range(1, across):
+                across_copy(kind, place, offset).wait_recv()
+
+    pass_on(along - 1)
+    await_shards(0)
+
+    def project(turn):
+        rows = block(turn, own_len)
+        for offset in offsets:
+            level_copy(turn, levels - offset).wait_recv()
+            core_copy(turn, offset).start()
+        for offset in range(levels):
+            core_copy(turn, offset).wait_recv()
+        values_in = features_ref[rows, :]
+        queries_ref[rows, :] = (
+            dot(values_in, full_qkv_ref[:, :width]) + b_query_ref[...]
+        ).astype(low)
+        blocks = pl.ds(turn * (own_len // BLK), own_len // BLK)
+        by_block = (own_len // BLK, BLK, width)
+        keys_ref[blocks] = (
+            dot(values_in, full_qkv_ref[:, width : 2 * width]).astype(low).reshape(by_block)
+        )
+        values_ref[blocks] = (
+            (dot(values_in, full_qkv_ref[:, 2 * width :]) + b_value_ref[...])
+            .astype(low)
+            .reshape(by_block)
+        )
+
+    for turn in range(cols):
+        project(turn)
+        pass_on(1)
+    own_ref[...] = features_ref[block(column, own_len), :]
+    count = seq_len // BLK // SEGMENTS
+    for part in range(SEGMENTS):
+        attend_blocks(
+            part * count,
+            count,
+            2,
+            globals_ref,
+            random_ref,
+            limits_ref,
+            (queries_ref, keys_ref, values_ref),
+            context_ref,
+            (highest_ref, scale_ref),
+        )
+        pass_on(part % 2)
+    pass_on(len(waiting))
+    for kind in range(1, FRONT_KINDS):
+        await_shards(kind)
+    for copy in swaps:
+        copy.wait()
+    for kind in range(FRONT_KINDS):
+        for offset in range(1, along):
+            along_copy(kind, offset).wait_send()
+
+        @pl.loop(0, along)
+        def _(place):
+            for offset in range(1, across):
+                across_copy(kind, place, offset).wait_send()
+
+    @pl.loop(0, cols)
+    def _(turn):
+        for offset in offsets:
+            level_copy(turn, offset).wait_send()
+        for offset in range(levels):
+            core_copy(turn, offset).wait_send()
+
+
+def across_of(rows):
+    return 2 if rows <= 8 else rows // 4
+
+
+def front(levels, rows, tables, hidden_in, grads, biases, parts):
+    low, full = jnp.bfloat16, jnp.float32
+    shape = jax.ShapeDtypeStruct
+    across = across_of(rows)
+    along = rows // across
+    seq_len, width = hidden_in.shape
+    cols = 2 * levels
+    own_len = seq_len // cols
+    features_all = width * cols
+    others = levels - 1
+    stat = shape((seq_len // BLK, 1, width), full)
+    dma = pltpu.SemaphoreType.DMA
+    return pl.pallas_call(
+        functools.partial(front_kernel, levels, across, along),
+        out_shape=(
+            shape((seq_len, features_all), low),
+            shape((own_len, features_all), low),
+            shape((own_len, features_all), low),
+            shape((seq_len, width), low),
+            shape((seq_len // BLK, BLK, width), low),
+            shape((seq_len // BLK, BLK, width), low),
+            shape((seq_len, width), low),
+            stat,
+            stat,
+            *(shape((part.shape[0] * rows, part.shape[1]), low) for part in parts),
+        ),
+        in_specs=[SMEM] * 2 + [VMEM] * 8,
+        out_specs=[VMEM] * 12,
+        scratch_shapes=[
+            dma((cols, others)),
+            dma((cols, others)),
+            dma((cols, levels)),
+            dma((cols, levels)),
+            dma((cols,)),
+            dma((cols,)),
+            dma((FRONT_KINDS, along - 1)),
+            dma((FRONT_KINDS, along - 1)),
+            dma((FRONT_KINDS, along, across - 1)),
+            dma((FRONT_KINDS, along, across - 1)),
+        ],
+        compiler_params=pltpu.CompilerParams(
+            collective_id=3, has_side_effects=True, vmem_limit_bytes=48 * 1024 * 1024
+        ),
+        cost_estimate=pl.CostEstimate(
+            flops=2 * seq_len * features_all * 3 * width,
+            bytes_accessed=20 * 1024 * 1024,
+            transcendentals=seq_len * 512 * (width // DH),
+        ),
+    )(*tables, hidden_in, grads, *biases, *parts)
+
+
 def dot(left, right):
     return jnp.dot(left, right, preferred_element_type=jnp.float32)
 
@@ -337,13 +606,15 @@
 
 def middle_kernel(
     levels,
+    across,
+    along,
     context_ref,
     inputs_ref,
     upstream_ref,
     valid_ref,
     out_ref,
     up_ref,
-    down_ref,
+    part_down_ref,
     vectors_ref,
     b_up_ref,
     layer_out_ref,
@@ -351,12 +622,13 @@
     attn_full,
     small_ref,
     up_small_ref,
-    grad_up_ref,
-    grad_down_ref,
+    share_down_ref,
+    up_part_ref,
     grad_out_ref,
     context_sib,
     out_sib,
     up_sib,
+    down_full,
     down_sib,
     normed_full,
     ffn_full,
@@ -371,11 +643,22 @@
     recv_buf,
     context_send,
     stage,
-    stage_small,
+    down_sums,
+    up_sums,
+    down_got,
+    up_got,
+    down_pass,
+    down_in,
     send_sem,
     recv_sem,
     core_send,
     core_recv,
+    shard_send,
+    shard_recv,
+    along_send,
+    along_recv,
+    across_send,
+    across_recv,
     stage_sem,
 ):
     low = jnp.bfloat16
@@ -383,6 +666,8 @@
     core = lax.rem(column, 2)
     level = lax.div(column, 2)
     sibling = (row, column + 1 - 2 * core)
+    fast, slow = lax.rem(row, across), lax.div(row, across)
+    shard = part_down_ref.shape[0]
     own_len = inputs_ref.shape[0]
     step = own_len // CHUNKS
     b_out, gain1, shift1, b_down, gain2, shift2 = (
@@ -392,26 +677,74 @@
     def peer_level(offset):
         return lax.rem(level + offset, levels)
 
+    def fast_peer(offset):
+        return slow * across + lax.rem(fast + offset, across)
+
+    def slow_peer(offset):
+        return lax.rem(slow + offset, along) * across + fast
+
     barrier = pltpu.get_barrier_semaphore()
-    pl.semaphore_signal(barrier, inc=1, device_id=sibling, device_id_type=MESH)
-    for offset in range(1, levels):
-        pl.semaphore_signal(
-            barrier,
-            inc=1,
-            device_id=(row, peer_level(offset) * 2 + core),
-            device_id_type=MESH,
-        )
-    pl.semaphore_wait(barrier, levels)
-
-    def to_sibling(source, target, place):
+    greeted = [sibling]
+    greeted += [(row, peer_level(offset) * 2 + core) for offset in range(1, levels)]
+    greeted += [(fast_peer(offset), column) for offset in range(1, across)]
+    greeted += [(slow_peer(offset), column) for offset in range(1, along)]
+    for device in greeted:
+        pl.semaphore_signal(barrier, inc=1, device_id=device, device_id_type=MESH)
+    pl.semaphore_wait(barrier, len(greeted))
+
+    def remote(source, target, send, recv, device):
         return pltpu.make_async_remote_copy(
             src_ref=source,
             dst_ref=target,
-            send_sem=core_send.at[place],
-            recv_sem=core_recv.at[place],
-            device_id=sibling,
+            send_sem=send,
+            recv_sem=recv,
+            device_id=device,
             device_id_type=MESH,
         )
+
+    def block(start, size):
+        return pl.ds(pl.multiple_of(start * size, size), size)
+
+    def to_sibling(source, target, place):
+        return remote(source, target, core_send.at[place], core_recv.at[place], sibling)
+
+    def shard_view(ref, place, position):
+        return ref.at[block(place * across + position, shard)]
+
+    def along_down(offset):
+        view = shard_view(down_full, slow, fast)
+        return remote(
+            view,
+            view,
+            along_send.at[0, offset - 1],
+            along_recv.at[0, along - offset - 1],
+            (slow_peer(offset), column),
+        )
+
+    def across_down(place, offset):
+        view = shard_view(down_full, place, fast)
+        return remote(
+            view,
+            view,
+            across_send.at[0, place, offset - 1],
+            across_recv.at[0, place, across - offset - 1],
+            (fast_peer(offset), column),
+        )
+
+    def core_down(place, offset):
+        position = lax.rem(fast + offset, across)
+        return remote(
+            shard_view(down_full, place, position),
+            shard_view(down_sib, place, position),
+            shard_send.at[place, offset],
+            shard_recv.at[place, offset],
+            sibling,
+        )
+
+    def pass_down(place):
+        for offset in range(1, across):
+            across_down(place, offset).start()
+        core_down(place, 0).start()
 
     def rows_of(place, chunk):
         return pl.ds(pl.multiple_of(place * own_len + chunk * step, step), step)
@@ -462,9 +795,13 @@
     ]
     out_copy = to_sibling(out_ref, out_sib, levels)
     up_copy = to_sibling(up_ref, up_sib, levels + 1)
-    down_copy = to_sibling(down_ref, down_sib, levels + 2)
-    for copy in context_copies + [out_copy, up_copy, down_copy]:
+    for copy in context_copies + [out_copy]:
         copy.start()
+    down_full[block(slow * across + fast, shard), :] = part_down_ref[...]
+    for offset in range(1, along):
+        along_down(offset).start()
+    pass_down(slow)
+    up_copy.start()
     small_ref[...] = jnp.zeros_like(small_ref)
     up_small_ref[...] = jnp.zeros_like(up_small_ref)
     for copy in context_copies:
@@ -488,8 +825,7 @@
             ).astype(low)
             sum_copy(0, chunk, offset).start()
 
-    @pl.loop(0, CHUNKS)
-    def _(chunk):
+    for chunk in range(CHUNKS):
         rows = own_rows(chunk)
         summed = (
             inputs_ref[rows, :].astype(jnp.float32) + attn_part(level, chunk) + b_out[...]
@@ -502,10 +838,24 @@
         normed_full[rows_of(level, chunk), :] = (normed * gain1[...] + shift1[...]).astype(low)
         for offset in offsets:
             spread_copy(1, chunk, offset).start()
-
+        for offset in range(1, along):
+            if min(offset, CHUNKS - 1) == chunk:
+                along_down(along - offset).wait_recv()
+                pass_down(lax.rem(slow + offset, along))
+
+    for turn in range(along):
+        place = lax.rem(slow + turn, along)
+        for offset in range(1, across):
+            across_down(place, across - offset).wait_recv()
+            core_down(place, offset).start()
     up_copy.wait()
-    down_copy.wait()
-    sides = ((up_ref, down_ref), (up_sib, down_sib))
+
+    @pl.loop(0, along)
+    def _(place):
+        for offset in range(across):
+            core_down(place, offset).wait_recv()
+
+    sides = ((up_ref, down_full), (up_sib, down_sib))
 
     def feed_forward(place, chunk):
         rows = rows_of(place, chunk)
@@ -515,7 +865,7 @@
             active, bend = gelu_parts(dot(normed, up_side[...]) + b_up_ref[side : side + 1, :])
             active = active.astype(low)
             hidden[side, rows, :] = active
-            slope[side, rows, :] = bend
+            slope[side, rows, :] = bend.astype(low)
             part = dot_nt(active, down_side[...])
             total = part if total is None else total + part
         return total
@@ -557,7 +907,9 @@
         upstream = ffn_full[rows, :]
         total = None
         for side, (up_side, down_side) in enumerate(sides):
-            grad = (dot(upstream, down_side[...]) * slope[side, rows, :]).astype(low)
+            grad = (
+                dot(upstream, down_side[...]) * slope[side, rows, :].astype(jnp.float32)
+            ).astype(low)
             pre_grad[side, rows, :] = grad
             up_small_ref[side : side + 1, :] += jnp.sum(
                 grad.astype(jnp.float32), axis=0, keepdims=True
@@ -576,33 +928,62 @@
             ).astype(low)
             sum_copy(4, chunk, offset).start()
 
-    def weight_grad(left_ref, right_of, target_ref, buffer):
-        tile = buffer.shape[1]
-        tiles = left_ref.shape[1] // tile
-
-        def put(side, turn):
-            return pltpu.make_async_copy(
-                buffer.at[lax.rem(turn, 2)],
-                target_ref.at[side, pl.ds(pl.multiple_of(turn * tile, tile), tile)],
-                stage_sem.at[lax.rem(turn, 2)],
-            )
-
-        for side in range(2):
-
-            @pl.loop(0, tiles)
-            def _(turn):
-                @pl.when(turn >= 2)
-                def _():
-                    put(side, turn - 2).wait()
-
-                left = left_ref[:, pl.ds(pl.multiple_of(turn * tile, tile), tile)]
-                buffer[lax.rem(turn, 2)] = dot_tn(left, right_of(side)).astype(low)
-                put(side, turn).start()
-
-            for turn in range(max(tiles - 2, 0), tiles):
-                put(side, turn).wait()
-
-    weight_grad(ffn_full, lambda side: hidden[side], grad_down_ref, stage)
+    tile = across * shard
+    lefts, rights = (ffn_full, normed_full), (hidden, pre_grad)
+    sums, got = (down_sums, up_sums), (down_got, up_got)
+
+    def grad_tile(kind, side, turn):
+        return dot_tn(lefts[kind][:, block(turn, tile)], rights[kind][side])
+
+    def core_grad(kind):
+        return to_sibling(
+            slope.at[kind, : sums[kind].shape[0]], sums[kind], 2 * levels + 2 + kind
+        )
+
+    def across_grad(kind, turn, offset):
+        return remote(
+            sums[kind].at[block(turn * across + lax.rem(fast + offset, across), shard)],
+            got[kind].at[across - offset - 1, block(turn, shard)],
+            across_send.at[1 + kind, turn, offset - 1],
+            across_recv.at[1 + kind, turn, across - offset - 1],
+            (fast_peer(offset), column),
+        )
+
+    def along_grad(offset):
+        return remote(
+            down_pass.at[offset - 1],
+            down_in.at[along - offset - 1],
+            along_send.at[1, offset - 1],
+            along_recv.at[1, along - offset - 1],
+            (slow_peer(offset), column),
+        )
+
+    def own_shard(kind, turn):
+        for offset in range(1, across):
+            across_grad(kind, turn, offset).wait_recv()
+        total = sums[kind][block(turn * across + fast, shard), :].astype(jnp.float32)
+        for place in range(across - 1):
+            total += got[kind][place, block(turn, shard), :].astype(jnp.float32)
+        return total
+
+    for kind in range(2):
+
+        @pl.loop(0, along)
+        def _(turn):
+            slope[kind, block(turn, tile), :] = grad_tile(kind, 1, turn).astype(low)
+
+        core_grad(kind).start()
+    for kind in range(2):
+        core_grad(kind).wait_recv()
+
+        @pl.loop(0, along)
+        def _(turn):
+            rows = block(turn, tile)
+            sums[kind][rows, :] = (
+                grad_tile(kind, 0, turn) + sums[kind][rows, :].astype(jnp.float32)
+            ).astype(low)
+            for offset in range(1, across):
+                across_grad(kind, turn, offset).start()
 
     @pl.loop(0, CHUNKS)
     def _(chunk):
@@ -620,7 +1001,10 @@
         small_ref[4:5, :] += jnp.sum(upstream, axis=0, keepdims=True)
         small_ref[5:6, :] += jnp.sum(grad_low.astype(jnp.float32), axis=0, keepdims=True)
 
-    weight_grad(normed_full, lambda side: pre_grad[side], grad_up_ref, stage)
+    for offset in range(1, along):
+        down_pass[offset - 1] = own_shard(0, lax.rem(slow + offset, along)).astype(low)
+        along_grad(offset).start()
+    share_down_ref[...] = own_shard(0, slow)
 
     def context_back(place, chunk):
         rows = rows_of(place, chunk)
@@ -641,7 +1025,7 @@
             context_grad_ref.at[
                 pl.ds(pl.multiple_of((place * 2 + core) * own_len, own_len), own_len)
             ],
-            levels + 3 + place,
+            levels + 2 + place,
         )
         for place in range(levels)
     ]
@@ -657,12 +1041,38 @@
         ],
         axis=0,
     )
-    weight_grad(
-        attn_full,
-        lambda side: context_sib[...] if side else own_context,
-        grad_out_ref,
-        stage_small,
-    )
+
+    def out_put(side):
+        return pltpu.make_async_copy(stage.at[side], grad_out_ref.at[side], stage_sem.at[side])
+
+    for side, right in enumerate((own_context, context_sib[...])):
+        stage[side] = dot_tn(attn_full[...], right).astype(low)
+        out_put(side).start()
+    for turn in range(along):
+        up_part_ref[turn] = own_shard(1, turn).astype(low)
+    total = share_down_ref[...]
+    for offset in range(1, along):
+        along_grad(offset).wait_recv()
+    for place in range(along - 1):
+        total += down_in[place].astype(jnp.float32)
+    share_down_ref[...] = total
+    for side in range(2):
+        out_put(side).wait()
+    for kind in range(2):
+        core_grad(kind).wait_send()
+    for offset in range(1, along):
+        along_down(offset).wait_send()
+        along_grad(offset).wait_send()
+
+    @pl.loop(0, along)
+    def _(place):
+        for offset in range(1, across):
+            across_down(place, offset).wait_send()
+            across_grad(0, place, offset).wait_send()
+            across_grad(1, place, offset).wait_send()
+        for offset in range(across):
+            core_down(place, offset).wait_send()
+
     for copy in back_copies:
         copy.wait()
     for kind in range(6):
@@ -677,68 +1087,80 @@
 
 
 def middle(
-    levels, context, inputs, upstream, valid, out_own, up_own, down_own, vectors, b_up_pair
+    levels, rows, context, inputs, upstream, valid, out_own, up_own, part_down, vectors, b_up_pair
 ):
     low, full = jnp.bfloat16, jnp.float32
+    across = across_of(rows)
+    along = rows // across
     own_len, features = inputs.shape
     seq_len, width = context.shape
-    units = up_own.shape[1]
+    shard, units = part_down.shape
     tokens = levels * own_len
     others = levels - 1
-    tile = 256
     shape = jax.ShapeDtypeStruct
     hbm = pl.BlockSpec(memory_space=pl.ANY)
+    dma = pltpu.SemaphoreType.DMA
+    vmem = pltpu.VMEM
     return pl.pallas_call(
-        functools.partial(middle_kernel, levels),
+        functools.partial(middle_kernel, levels, across, along),
         out_shape=(
             shape((own_len, features), low),
             shape((seq_len, width), low),
             shape((tokens, features), low),
             shape((8, features), full),
             shape((2, units), full),
-            shape((2, features, units), low),
-            shape((2, features, units), low),
+            shape((shard, units), full),
+            shape((along, shard, units), low),
             shape((2, features, width), low),
         ),
         in_specs=[VMEM] * 9,
-        out_specs=[VMEM] * 5 + [hbm] * 3,
+        out_specs=[VMEM] * 7 + [hbm],
         scratch_shapes=[
-            pltpu.VMEM((tokens, width), low),
-            pltpu.VMEM((features, width), low),
-            pltpu.VMEM((features, units), low),
-            pltpu.VMEM((features, units), low),
-            pltpu.VMEM((tokens, features), low),
-            pltpu.VMEM((tokens, features), low),
-            pltpu.VMEM((2, tokens, units), low),
-            pltpu.VMEM((2, tokens, units), full),
-            pltpu.VMEM((2, tokens, units), low),
-            pltpu.VMEM((own_len, features), full),
-            pltpu.VMEM((own_len, 1), full),
-            pltpu.VMEM((own_len, features), full),
-            pltpu.VMEM((own_len, features), full),
-            pltpu.VMEM((3, others, own_len, features), low),
-            pltpu.VMEM((3, others, own_len, features), low),
-            pltpu.VMEM((tokens, width), low),
-            pltpu.VMEM((2, tile, units), low),
-            pltpu.VMEM((2, tile, width), low),
-            pltpu.SemaphoreType.DMA((6, CHUNKS, others)),
-            pltpu.SemaphoreType.DMA((6, CHUNKS, others)),
-            pltpu.SemaphoreType.DMA((2 * levels + 3,)),
-            pltpu.SemaphoreType.DMA((2 * levels + 3,)),
-            pltpu.SemaphoreType.DMA((2,)),
+            vmem((tokens, width), low),
+            vmem((features, width), low),
+            vmem((features, units), low),
+            vmem((features, units), low),
+            vmem((features, units), low),
+            vmem((tokens, features), low),
+            vmem((tokens, features), low),
+            vmem((2, tokens, units), low),
+            vmem((2, max(tokens, features), units), low),
+            vmem((2, tokens, units), low),
+            vmem((own_len, features), full),
+            vmem((own_len, 1), full),
+            vmem((own_len, features), full),
+            vmem((own_len, features), full),
+            vmem((3, others, own_len, features), low),
+            vmem((3, others, own_len, features), low),
+            vmem((tokens, width), low),
+            vmem((2, features, width), low),
+            vmem((features, units), low),
+            vmem((features, units), low),
+            vmem((across - 1, along * shard, units), low),
+            vmem((across - 1, along * shard, units), low),
+            vmem((along - 1, shard, units), low),
+            vmem((along - 1, shard, units), low),
+            dma((6, CHUNKS, others)),
+            dma((6, CHUNKS, others)),
+            dma((2 * levels + 4,)),
+            dma((2 * levels + 4,)),
+            dma((along, across)),
+            dma((along, across)),
+            dma((2, along - 1)),
+            dma((2, along - 1)),
+            dma((3, along, across - 1)),
+            dma((3, along, across - 1)),
+            dma((2,)),
         ],
         compiler_params=pltpu.CompilerParams(
-            collective_id=1, has_side_effects=True, vmem_limit_bytes=60 * 1024 * 1024
+            collective_id=1, has_side_effects=True, vmem_limit_bytes=62 * 1024 * 1024
         ),
         cost_estimate=pl.CostEstimate(
             flops=2 * tokens * features * (12 * units + 6 * width),
-            bytes_accessed=40 * 1024 * 1024,
+            bytes_accessed=20 * 1024 * 1024,
             transcendentals=2 * tokens * units,
         ),
-    )(context, inputs, upstream, valid, out_own, up_own, down_own, vectors, b_up_pair)
-
-
-KINDS = 4
+    )(context, inputs, upstream, valid, out_own, up_own, part_down, vectors, b_up_pair)
 
 
 def end_kernel(
@@ -751,32 +1173,23 @@
     attn_ref,
     layer_ref,
     small_ref,
-    down_ref,
+    out_ref,
     up_ref,
-    out_ref,
     grad_input_ref,
     layer_out_ref,
     small_out_ref,
-    share_down_ref,
-    share_up_ref,
     share_out_ref,
     share_qkv_ref,
-    down_sib,
-    up_sib,
+    share_up_ref,
     out_sib,
     qkv_sums,
-    down_got,
-    up_got,
     out_got,
     qkv_got,
-    down_pass,
-    up_pass,
     out_pass,
     qkv_pass,
-    down_in,
-    up_in,
     out_in,
     qkv_in,
+    up_in,
     core_out,
     core_in,
     level_out,
@@ -845,17 +1258,12 @@
     def block(start, size):
         return pl.ds(pl.multiple_of(start * size, size), size)
 
-    core_copies = [
-        remote(source.at[1], target, core_send.at[place], core_recv.at[place], sibling)
-        for place, (source, target) in enumerate(
-            [(down_ref, down_sib), (up_ref, up_sib), (out_ref, out_sib)]
-        )
-    ]
+    out_copy = remote(out_ref.at[1], out_sib, core_send.at[0], core_recv.at[0], sibling)
     attn_copy = remote(
         attn_ref.at[:, block(level * 2 + other, width)],
         attn_in,
-        core_send.at[3],
-        core_recv.at[3],
+        core_send.at[1],
+        core_recv.at[1],
         sibling,
     )
 
@@ -912,10 +1320,9 @@
     )
 
     small_sums[0] = small_ref[...]
-    core_copies[0].start()
     small_step()
-    for copy in core_copies[1:] + [attn_copy]:
-        copy.start()
+    out_copy.start()
+    attn_copy.start()
     layer_keep.start()
     for copy in layer_copies:
         copy.start()
@@ -935,20 +1342,20 @@
             sibling,
         )
 
-    @pl.loop(0, cols)
-    def _(turn):
-        for place in range(levels):
-            core_out[place, block(turn, own_len), :] = input_part(turn, place * 2 + other).astype(
-                low
-            )
-            part_copy(turn, place).start()
-
-    sums = (down_sib, up_sib, out_sib, qkv_sums)
-    firsts = (down_ref, up_ref, out_ref)
-    got = (down_got, up_got, out_got, qkv_got)
-    passed = (down_pass, up_pass, out_pass, qkv_pass)
-    landed = (down_in, up_in, out_in, qkv_in)
-    shares = (share_down_ref, share_up_ref, share_out_ref, share_qkv_ref)
+    def give_core():
+        @pl.loop(0, cols)
+        def _(turn):
+            for place in range(levels):
+                core_out[place, block(turn, own_len), :] = input_part(
+                    turn, place * 2 + other
+                ).astype(low)
+                part_copy(turn, place).start()
+
+    sums = (out_sib, qkv_sums)
+    got = (out_got, qkv_got)
+    passed = (out_pass, qkv_pass)
+    landed = (out_in, qkv_in, up_in)
+    shares = (share_out_ref, share_qkv_ref, share_up_ref)
 
     def across_copy(kind, turn, offset):
         return remote(
@@ -960,8 +1367,12 @@
         )
 
     def along_copy(kind, offset):
+        if kind == 2:
+            source = up_ref.at[lax.rem(slow + offset, along)]
+        else:
+            source = passed[kind].at[offset - 1]
         return remote(
-            passed[kind].at[offset - 1],
+            source,
             landed[kind].at[along - offset - 1],
             along_send.at[kind, offset - 1],
             along_recv.at[kind, along - offset - 1],
@@ -972,26 +1383,23 @@
         for offset in range(1, across):
             across_copy(kind, turn, offset).start()
 
-    for kind in range(3):
-        core_copies[kind].wait()
+    def sum_cores():
+        out_copy.wait()
 
         @pl.loop(0, along)
         def _(turn):
             rows = block(turn, across * shard)
-            sums[kind][rows, :] = (
-                firsts[kind][0, rows, :].astype(full) + sums[kind][rows, :].astype(full)
+            out_sib[rows, :] = (
+                out_ref[0, rows, :].astype(full) + out_sib[rows, :].astype(full)
             ).astype(low)
-            give_across(kind, turn)
-
-        small_step()
-
-    @pl.loop(0, along)
-    def _(turn):
-        rows = block(turn, across * shard)
-        qkv_sums[rows, :] = dot_tn(features_ref[:, rows], query_key_value_ref[...]).astype(low)
-        give_across(3, turn)
-
-    small_step()
+            give_across(0, turn)
+
+    def weight_grad():
+        @pl.loop(0, along)
+        def _(turn):
+            rows = block(turn, across * shard)
+            qkv_sums[rows, :] = dot_tn(features_ref[:, rows], query_key_value_ref[...]).astype(low)
+            give_across(1, turn)
 
     def level_copy(turn, offset):
         rows = block(turn, own_len)
@@ -1003,19 +1411,18 @@
             (row, peer_level(offset) * 2 + core),
         )
 
-    @pl.loop(0, cols)
-    def _(turn):
-        rows = block(turn, own_len)
-        for offset in offsets:
-            place = peer_level(offset)
-            part = input_part(turn, place * 2 + core)
-            part_copy(turn, place).wait_recv()
-            level_out[offset - 1, rows, :] = (part + core_in[place, rows, :].astype(full)).astype(
-                low
-            )
-            level_copy(turn, offset).start()
-
-    small_step()
+    def give_levels():
+        @pl.loop(0, cols)
+        def _(turn):
+            rows = block(turn, own_len)
+            for offset in offsets:
+                place = peer_level(offset)
+                part = input_part(turn, place * 2 + core)
+                part_copy(turn, place).wait_recv()
+                level_out[offset - 1, rows, :] = (
+                    part + core_in[place, rows, :].astype(full)
+                ).astype(low)
+                level_copy(turn, offset).start()
 
     def own_shard(kind, turn):
         for offset in range(1, across):
@@ -1025,18 +1432,12 @@
             total += got[kind][place, block(turn, shard), :].astype(full)
         return total
 
-    for kind in range(KINDS):
+    def give_along(kind):
         for offset in range(1, along):
             turn = lax.rem(slow + offset, along)
             passed[kind][offset - 1] = own_shard(kind, turn).astype(low)
             along_copy(kind, offset).start()
         shares[kind][...] = own_shard(kind, slow)
-
-    while small_turn[0] <= len(partners):
-        small_step()
-    small_out_ref[...] = small_sums[len(partners)]
-
-    attn_copy.wait()
 
     def finish_input(turn, attn_part):
         rows = block(turn, own_len)
@@ -1049,13 +1450,35 @@
             total += level_in[place, rows, :].astype(full)
         grad_input_ref[rows, :] = total.astype(low)
 
-    @pl.loop(0, levels)
-    def _(place):
-        rows = block(place, own_len)
-        finish_input(place * 2 + core, attn_ref[rows, block(column, width)])
-        finish_input(place * 2 + other, attn_in[rows, :])
-
-    for kind in range(KINDS):
+    def finish_inputs():
+        attn_copy.wait()
+
+        @pl.loop(0, levels)
+        def _(place):
+            rows = block(place, own_len)
+            finish_input(place * 2 + core, attn_ref[rows, block(column, width)])
+            finish_input(place * 2 + other, attn_in[rows, :])
+
+    for offset in range(1, along):
+        along_copy(2, offset).start()
+    share_up_ref[...] = up_ref[slow].astype(full)
+    weight_grad()
+    small_step()
+    give_core()
+    sum_cores()
+    small_step()
+    give_levels()
+    small_step()
+    give_along(1)
+    small_step()
+    give_along(0)
+    small_step()
+    finish_inputs()
+    while small_turn[0] <= len(partners):
+        small_step()
+    small_out_ref[...] = small_sums[len(partners)]
+
+    for kind in range(3):
         total = shares[kind][...]
         for offset in range(1, along):
             along_copy(kind, offset).wait_recv()
@@ -1066,9 +1489,10 @@
     layer_keep.wait()
     for copy in layer_copies:
         copy.wait()
-    for kind in range(KINDS):
+    for kind in range(3):
         for offset in range(1, along):
             along_copy(kind, offset).wait_send()
+    for kind in range(2):
 
         @pl.loop(0, along)
         def _(turn):
@@ -1084,17 +1508,18 @@
 
 
 def finish(
-    levels, rows, query_key_value, weights, features, attn_full, layer_own, small, down, up, out
+    levels, rows, query_key_value, weights, features, attn_full, layer_own, small, out, up
 ):
     low, full = jnp.bfloat16, jnp.float32
     shape = jax.ShapeDtypeStruct
-    across = 2 if rows <= 8 else rows // 4
+    across = across_of(rows)
     along = rows // across
     seq_len, features_all = features.shape
     width = query_key_value.shape[1] // 3
     own_len = layer_own.shape[0]
     shard = features_all // rows
-    widths = [down.shape[2], up.shape[2], out.shape[2], 3 * width]
+    widths = [out.shape[2], 3 * width]
+    units = up.shape[2]
     others = levels - 1
     cols = 2 * levels
     turns = 1 + (levels - 1).bit_length() + (rows - 1).bit_length()
@@ -1105,15 +1530,15 @@
             shape((seq_len, width), low),
             shape((seq_len, width), low),
             shape(small.shape, full),
-            *(shape((shard, each), full) for each in widths),
+            *(shape((shard, each), full) for each in widths + [units]),
         ),
-        in_specs=[VMEM] * 9,
-        out_specs=[VMEM] * 7,
+        in_specs=[VMEM] * 8,
+        out_specs=[VMEM] * 6,
         scratch_shapes=[
             *(pltpu.VMEM((features_all, each), low) for each in widths),
             *(pltpu.VMEM((across - 1, along * shard, each), low) for each in widths),
             *(pltpu.VMEM((along - 1, shard, each), low) for each in widths),
-            *(pltpu.VMEM((along - 1, shard, each), low) for each in widths),
+            *(pltpu.VMEM((along - 1, shard, each), low) for each in widths + [units]),
             pltpu.VMEM((levels, seq_len, width), low),
             pltpu.VMEM((levels, seq_len, width), low),
             pltpu.VMEM((others, seq_len, width), low),
@@ -1121,18 +1546,18 @@
             pltpu.VMEM((levels * own_len, width), low),
             pltpu.VMEM((turns + 1, *small.shape), full),
             pltpu.VMEM((turns, *small.shape), full),
-            dma((4,)),
-            dma((4,)),
+            dma((2,)),
+            dma((2,)),
             dma((cols, levels)),
             dma((cols, levels)),
             dma((cols, others)),
             dma((cols, others)),
             dma((cols,)),
             dma((cols,)),
-            dma((KINDS, along, across - 1)),
-            dma((KINDS, along, across - 1)),
-            dma((KINDS, along - 1)),
-            dma((KINDS, along - 1)),
+            dma((2, along, across - 1)),
+            dma((2, along, across - 1)),
+            dma((3, along - 1)),
+            dma((3, along - 1)),
             dma((turns,)),
             dma((turns,)),
             dma,
@@ -1145,11 +1570,7 @@
             bytes_accessed=40 * 1024 * 1024,
             transcendentals=0,
         ),
-    )(query_key_value, weights, features, attn_full, layer_own, small, down, up, out)
-
-
-def to_tokens(portion):
-    return lax.all_to_all(portion, "col", split_axis=0, concat_axis=1, tiled=True)
+    )(query_key_value, weights, features, attn_full, layer_own, small, out, up)
 
 
 def into_full(portion, start_at, full_len):
@@ -1200,43 +1621,48 @@
         rand_blocks.reshape(-1),
         limits_of(length, global_blocks[0], rand_blocks[0], num_blocks, head_count),
     )
-    full_qkv = lax.all_gather(
-        jnp.concatenate([w_query.astype(low), w_key.astype(low), w_value.astype(low)], axis=1),
-        "row",
-        axis=0,
-        tiled=True,
-    )
-    features = lax.all_gather(hidden_in, "col", axis=1, tiled=True)
-    full_out = lax.all_gather(w_out.astype(low).T, "row", axis=0, tiled=True)
-    full_up = lax.all_gather(w_up.astype(low), "row", axis=0, tiled=True)
-    full_down = lax.all_gather(w_down.astype(low).T, "row", axis=0, tiled=True)
-    own_features = lax.dynamic_slice_in_dim(features, own_start, own_len, 0)
     valid = (jnp.arange(seq_len) < length)[:, None]
-    upstream = to_tokens(jnp.where(valid, out_grad, 0))
     own_valid = (own_start + jnp.arange(own_len) < length).astype(jnp.float32)[:, None]
-
-    full_query = full_qkv[:, :feat_cols]
-    full_key = full_qkv[:, feat_cols : 2 * feat_cols]
-    full_value = full_qkv[:, 2 * feat_cols :]
-    queries = (
-        dot(features, full_query) + lax.dynamic_slice_in_dim(b_query, feat_start, feat_cols)
-    ).astype(low)
-    key_rows = dot(features, full_key).astype(low)
-    value_rows = (
-        dot(features, full_value) + lax.dynamic_slice_in_dim(b_value, feat_start, feat_cols)
-    ).astype(low)
-    context, *stats = attend(queries, key_rows, value_rows, tables)
+    (
+        features,
+        own_features,
+        upstream,
+        queries,
+        key_rows,
+        value_rows,
+        context,
+        *stats,
+        full_qkv,
+        full_out,
+        full_up,
+    ) = front(
+        cols // 2,
+        lax.axis_size("row"),
+        tables,
+        hidden_in,
+        jnp.where(valid, out_grad, 0),
+        (
+            lax.dynamic_slice_in_dim(b_query, feat_start, feat_cols)[None, :],
+            lax.dynamic_slice_in_dim(b_value, feat_start, feat_cols)[None, :],
+        ),
+        (
+            jnp.concatenate([w_query, w_key, w_value], axis=1).astype(low),
+            w_out.T.astype(low),
+            w_up.astype(low),
+        ),
+    )
 
     sibling = column + 1 - 2 * lax.rem(column, 2)
-    layer_own, context_grad, attn_full, small, up_small, grad_up, grad_down, grad_out = middle(
+    layer_own, context_grad, attn_full, small, up_small, down_share, up_part, grad_out = middle(
         cols // 2,
+        lax.axis_size("row"),
         context,
         own_features,
         upstream,
         own_valid,
         full_out,
         full_up,
-        full_down,
+        w_down.T.astype(low),
         jnp.stack([b_out, ln1_gain, ln1_bias, b_down, ln2_gain, ln2_bias, b_out, b_out]),
         jnp.stack(
             [
@@ -1254,7 +1680,7 @@
     bias_full = lax.dynamic_update_slice(
         jnp.zeros((4, features_all), jnp.float32), bias_sums, (0, feat_start)
     )
-    grad_input, layer_out, small, down_share, up_share, out_share, qkv_share = finish(
+    grad_input, layer_out, small, out_share, qkv_share, up_share = finish(
         cols // 2,
         lax.axis_size("row"),
         query_key_value,
@@ -1263,9 +1689,8 @@
         attn_full,
         layer_own,
         jnp.concatenate([small, up_sums.reshape(-1, features_all), bias_full], axis=0),
-        grad_down,
-        grad_up,
         grad_out,
+        up_part,
     )
     return (
         layer_out,

time: 546 us -> 372 us (0.68)
  waiting for transfers between devices: 116 us -> 0 us
  blocking collectives: 34.3 us -> 0 us
  between operations: 14.8 us -> 1.69 us
  matrix products: 6.34 us -> 0 us
    all_gather x4 -> x0, waiting for transfers between devices: 115 us -> none  [the longest x1 50.4 us: on_device(): full_up = lax.all_gather(w_up.astype(low), 'row', axis=0, tiled=True)]
    pallas_call x2, Pallas kernels: 173 us -> 246 us  [the longest x1 175 us: middle(): pl.pallas_call(functools.partial(middle_kernel, levels, across, along), o...]
    pallas_call x1, Pallas kernels: 138 us -> 65.5 us  [finish(): pl.pallas_call(functools.partial(end_kernel, levels, across, along), out_...]
    all_gather x1 -> x0, blocking collectives: 34.3 us -> none  [on_device(): full_out = lax.all_gather(w_out.astype(low).T, 'row', axis=0, tiled=True)]
    dot_general x3 -> x0, matrix products: 6.34 us -> none  [dot(): return jnp.dot(left, right, preferred_element_type=jnp.float32)]
    unnamed x54 -> x66, local copies, waits for them, and re-layouts: 13.2 us -> 17 us
  transfers between devices with their start and end apart: 5 -> 0, of which waited for: 3 -> 0; matrix products, arithmetic and copies ran while one was open for 4% -> 0% of each run, Pallas kernels for 4% -> 0%
where the time goes in v5:
time: 372 us; the launch traced here: 371 us
  Pallas kernels  338 us (91%)
  local copies, waits for them, and re-layouts  26.2 us (7%)
  other arithmetic  5.07 us (1%)
    pallas_call x1, Pallas kernels, middle(): pl.pallas_call(functools.partial(middle_kernel, levels, across, along), o...  175 us
    pallas_call x1, Pallas kernels, front(): pl.pallas_call(functools.partial(front_kernel, levels, across, along), ou...  70.5 us
    pallas_call x1, Pallas kernels, finish(): pl.pallas_call(functools.partial(end_kernel, levels, across, along), out_...  65.5 us
    pallas_call x1, Pallas kernels, attend_back(): pl.pallas_call(functools.partial(attend_back_kernel, head_count, 2), out_...  26.7 us
    unnamed x66, local copies, waits for them, and re-layouts  17 us

profile of v5, /device:TPU:0, one launch (start us, length us, event | category | flops | bytes accessed | tf_op | source)
XLA Modules:
  0.0 371.0 jit_solution(8804887723478531223)
XLA Ops:
  0.7 0.8 fusion.5
  7.6 1.2 broadcast_select_fusion.grads_ref
  9.5 70.5 %shard_map.323 = (bf16[2048,1024]{1,0:T(8,128)(2,1)}, bf16[512,1024]{1,0:T(8,128)(2,1)S(1)}, bf16[512,1024]{1,0:T(8,128)(2,1)S(1)}, bf16[2048,256]{1,0:T(8,128)(...) custom-call(s32[2]{0:T(128)S(1)} %bitcast.50, ...), custom_call_target="tpu_custom_call" | custom-call | flops 3221225472 | bytes 20971520 | tf_op jit(solution)/shard_map/pallas_call | solution.py:524
  80.1 1.0 copy-done.2
  81.0 1.0 copy-done.5
  82.0 1.0 copy-done.6
  83.0 0.8 copy-done.7
  84.5 0.8 copy.72
  86.0 175.2 %shard_map.324 = (bf16[512,1024]{1,0:T(8,128)(2,1)}, bf16[2048,256]{1,0:T(8,128)(2,1)}, bf16[1024,1024]{1,0:T(8,128)(2,1)}, f32[8,1024]{1,0:T(8,128)}, f32[2,102...) custom-call(bf16[2048,256]{1,0:T(8,128)(2,1)} %get-tuple-element.48.context_ref, ...), custom_call_target="tpu_custom_call" | custom-call | flops 28991029248 | bytes 20971520 | tf_op jit(solution)/shard_map/pallas_call | solution.py:1104
  261.2 0.8 fusion.6
  262.4 1.2 copy-done.3
  263.6 1.2 copy-done.4
  264.8 1.2 copy-done.8
  266.0 26.7 %shard_map.325 = (bf16[2048,768]{1,0:T(8,128)(2,1)S(1)}, f32[2,256]{1,0:T(2,128)S(1)}) custom-call(s32[2]{0:T(128)S(1)} %bitcast.51, s32[384]{0:T(512)S(1)} %reshape.138.random_ref, s32[32,8,256]{2,1,0:T(8,128)S(1)} %pad_add_fusion.limits_ref, bf16[2048,256]{1,0:T(8,128)(2,1)S(1)} %get-tuple-element.45.queries_ref, bf16[32,64,256]{2,1,0:T(8,128)(2,1)S(1)} %copy-done.3, ...), custom_call_target="tpu_custom_call" | custom-call | flops 10737418240 | bytes 7340032 | tf_op jit(solution)/shard_map/pallas_call | solution.py:249
  292.8 1.7 copy-done.1
  295.1 65.5 %shard_map.326 = (bf16[2048,256]{1,0:T(8,128)(2,1)}, bf16[2048,256]{1,0:T(8,128)(2,1)}, f32[16,1024]{1,0:T(8,128)}, f32[128,256]{1,0:T(8,128)}, f32[128,768]{1,0:T(8,128)}, /*index=5*/f32[128,1024]{1,0:T(8,128)}) custom-call(bf16[2048,768]{1,0:T(8,128)(2,1)} %copy-done.1, bf16[1024,768]{1,0:T(8,128)(2,1)} %get-tuple-element.57.weights_ref, ...), custom_call_target="tpu_custom_call" | custom-call | flops 6442450944 | bytes 41943040 | tf_op jit(solution)/shard_map/pallas_call | solution.py:1527
  360.7 1.9 fusion.3
  362.6 1.7 copy.73
  364.2 1.6 fusion.4
  365.9 0.8 slice_bitcast_fusion
  367.2 1.0 copy.74
  368.2 1.0 copy.85
  369.2 1.0 copy.86
  370.2 0.8 copy.87
  (84 shorter events, 8.9 us)
Async XLA Ops:
  0.7 8.1 %copy-start.22 = (s32[1,32,4,3]{1,2,3,0:T(4,128)S(1)}, s32[1,32,4,3]{1,2,3,0:T(4,128)}, u32[]{:S(2)}) copy-start(s32[1,32,4,3]{1,2,3,0:T(4,128)} %param.24) | copy-start | bytes 4612
  0.7 6.9 %copy-start.9 = (bf16[2048,256]{1,0:T(8,128)(2,1)S(1)}, bf16[2048,256]{1,0:T(8,128)(2,1)}, u32[]{:S(2)}) copy-start(bf16[2048,256]{1,0:T(8,128)(2,1)} %param.21) | copy-start | bytes 3145732
  0.7 8.4 %copy-start.16 = (f32[128,256]{1,0:T(8,128)S(1)}, f32[128,256]{1,0:T(8,128)}, u32[]{:S(2)}) copy-start(f32[128,256]{1,0:T(8,128)} %param.27) | copy-start | bytes 393220
  6.1 3.1 copy-start.17
  6.2 3.0 copy-start.18
  7.4 1.9 copy-start.12
  7.5 1.8 copy-start.19
  7.5 1.9 copy-start
  9.4 75.1 %copy-start.13 = (f32[1024,128]{1,0:T(8,128)S(1)}, f32[1024,128]{1,0:T(8,128)}, u32[]{:S(2)}) copy-start(f32[1024,128]{1,0:T(8,128)} %param.36) | copy-start | bytes 1572868
  9.4 75.9 %copy-start.20 = (f32[1024]{0:T(1024)S(1)}, f32[1024]{0:T(1024)}, u32[]{:S(2)}) copy-start(f32[1024]{0:T(1024)} %param.31) | copy-start | bytes 12292
  9.4 75.9 %copy-start.23 = (f32[1024]{0:T(1024)S(1)}, f32[1024]{0:T(1024)}, u32[]{:S(2)}) copy-start(f32[1024]{0:T(1024)} %param.32) | copy-start | bytes 12292
  9.4 75.9 %copy-start.24 = (f32[1024]{0:T(1024)S(1)}, f32[1024]{0:T(1024)}, u32[]{:S(2)}) copy-start(f32[1024]{0:T(1024)} %param.33) | copy-start | bytes 12292
  9.5 75.9 %copy-start.25 = (f32[1024]{0:T(1024)S(1)}, f32[1024]{0:T(1024)}, u32[]{:S(2)}) copy-start(f32[1024]{0:T(1024)} %param.37) | copy-start | bytes 12292
  9.5 75.9 %copy-start.26 = (f32[1024]{0:T(1024)S(1)}, f32[1024]{0:T(1024)}, u32[]{:S(2)}) copy-start(f32[1024]{0:T(1024)} %param.38) | copy-start | bytes 12292
  9.5 75.9 %copy-start.27 = (f32[1024]{0:T(1024)S(1)}, f32[1024]{0:T(1024)}, u32[]{:S(2)}) copy-start(f32[1024]{0:T(1024)} %param.39) | copy-start | bytes 12292
  262.4 1.2 copy-start.3
  263.6 1.2 copy-start.4
  264.8 1.2 copy-start.8
  266.0 28.4 %copy-start.21 = (f32[8,1024]{1,0:T(8,128)S(1)}, f32[8,1024]{1,0:T(8,128)}, u32[]{:S(2)}) copy-start(f32[8,1024]{1,0:T(8,128)} %get-tuple-element.61) | copy-start | bytes 98308
  292.7 1.7 copy-start.1
  295.1 72.1 %copy-start.14 = (f32[128,1024]{1,0:T(8,128)S(1)}, f32[128,1024]{1,0:T(8,128)}, u32[]{:S(2)}) copy-start(f32[128,1024]{1,0:T(8,128)} %get-tuple-element.72) | copy-start | bytes 1572868
  360.6 7.6 %copy-start.11 = (bf16[2048,256]{1,0:T(8,128)(2,1)S(1)}, bf16[2048,256]{1,0:T(8,128)(2,1)}, u32[]{:S(2)}) copy-start(bf16[2048,256]{1,0:T(8,128)(2,1)} %get-tuple-element.190) | copy-start | bytes 3145732
  360.6 8.6 %copy-start.10 = (bf16[2048,256]{1,0:T(8,128)(2,1)S(1)}, bf16[2048,256]{1,0:T(8,128)(2,1)}, u32[]{:S(2)}) copy-start(bf16[2048,256]{1,0:T(8,128)(2,1)} %get-tuple-element.191) | copy-start | bytes 3145732
  368.2 1.9 copy-start.15
  (4 other events, 3.7 us)

commit v6 on v5

--- a/solution.py
+++ b/solution.py
@@ -247,7 +247,7 @@
     seq_len, width = queries.shape
     head_count = width // DH
     return pl.pallas_call(
-        functools.partial(attend_back_kernel, head_count, 2),
+        functools.partial(attend_back_kernel, head_count, 8),
         out_shape=(
             jax.ShapeDtypeStruct((seq_len, 3 * width), jnp.bfloat16),
             jax.ShapeDtypeStruct((2, width), jnp.float32),
@@ -265,8 +265,8 @@
     )(*tables, queries, key_rows, value_rows, context_grad, *stats)
 
 
-FRONT_KINDS = 3
-SEGMENTS = 8
+KINDS = 4
+CHUNKS = 4
 
 
 def front_kernel(
@@ -283,6 +283,8 @@
     part_qkv_ref,
     part_out_ref,
     part_up_ref,
+    part_down_ref,
+    vectors_ref,
     features_ref,
     own_ref,
     upstream_ref,
@@ -295,6 +297,16 @@
     full_qkv_ref,
     full_out_ref,
     full_up_ref,
+    full_down_ref,
+    out_sib,
+    up_sib,
+    down_sib,
+    context_sib,
+    normed_full,
+    unit1,
+    inv1,
+    sum_out,
+    sum_in,
     level_send,
     level_recv,
     core_send,
@@ -305,6 +317,14 @@
     along_recv,
     across_send,
     across_recv,
+    shard_send,
+    shard_recv,
+    context_send,
+    context_recv,
+    sum_send,
+    sum_recv,
+    normed_send,
+    normed_recv,
 ):
     low, full = jnp.bfloat16, jnp.float32
     row, column = lax.axis_index("row"), lax.axis_index("col")
@@ -374,8 +394,9 @@
         features_ref[rows, block(column, width)] = hidden_ref[rows, :]
         core_copy(turn, 0).start()
 
-    parts = (part_qkv_ref, part_out_ref, part_up_ref)
-    fulls = (full_qkv_ref, full_out_ref, full_up_ref)
+    parts = (part_qkv_ref, part_out_ref, part_up_ref, part_down_ref)
+    fulls = (full_qkv_ref, full_out_ref, full_up_ref, full_down_ref)
+    sibs = (None, out_sib, up_sib, down_sib)
 
     def shard_rows(place):
         return block(place * across + fast, shard)
@@ -400,12 +421,24 @@
             (fast_peer(offset), column),
         )
 
-    for kind in range(FRONT_KINDS):
+    def core_shard(kind, place, offset):
+        rows = block(place * across + lax.rem(fast + offset, across), shard)
+        return remote(
+            fulls[kind].at[rows],
+            sibs[kind].at[rows],
+            shard_send.at[kind - 1, place, offset],
+            shard_recv.at[kind - 1, place, offset],
+            sibling,
+        )
+
+    for kind in range(KINDS):
         fulls[kind][shard_rows(slow), :] = parts[kind][...]
         for offset in range(1, along):
             along_copy(kind, offset).start()
         for offset in range(1, across):
             across_copy(kind, slow, offset).start()
+        if kind > 0:
+            core_shard(kind, slow, 0).start()
 
     def swap_copy(target, place_out, place_in):
         return remote(
@@ -425,20 +458,30 @@
         copy.start()
     upstream_ref[:, block(column, width)] = grads_ref[block(column, own_len), :]
 
-    waiting = [(kind, offset) for kind in range(FRONT_KINDS) for offset in range(1, along)]
+    waiting = [(kind, offset) for kind in range(KINDS) for offset in range(1, along)]
 
     def pass_on(count):
         for kind, offset in waiting[:count]:
             along_copy(kind, along - offset).wait_recv()
             for step in range(1, across):
                 across_copy(kind, lax.rem(slow + offset, along), step).start()
+            if kind > 0:
+                core_shard(kind, lax.rem(slow + offset, along), 0).start()
         del waiting[:count]
 
     def await_shards(kind):
         @pl.loop(0, along)
         def _(place):
             for offset in range(1, across):
-                across_copy(kind, place, offset).wait_recv()
+                across_copy(kind, place, across - offset).wait_recv()
+                if kind > 0:
+                    core_shard(kind, place, offset).start()
+
+    def await_sibling(kind):
+        @pl.loop(0, along)
+        def _(place):
+            for offset in range(across):
+                core_shard(kind, place, offset).wait_recv()
 
     pass_on(along - 1)
     await_shards(0)
@@ -469,12 +512,16 @@
         project(turn)
         pass_on(1)
     own_ref[...] = features_ref[block(column, own_len), :]
-    count = seq_len // BLK // SEGMENTS
-    for part in range(SEGMENTS):
+    step = own_len // CHUNKS
+    halves = 2
+    count = own_len // BLK // halves
+    b_out, gain1, shift1 = (vectors_ref.at[place : place + 1, :] for place in range(3))
+
+    def attend_half(quarter, half):
         attend_blocks(
-            part * count,
+            (quarter * halves + half) * count,
             count,
-            2,
+            min(count, 4),
             globals_ref,
             random_ref,
             limits_ref,
@@ -482,13 +529,96 @@
             context_ref,
             (highest_ref, scale_ref),
         )
-        pass_on(part % 2)
+
+    def context_copy(place, half):
+        rows = own_len // halves
+        return remote(
+            context_ref.at[block((place * 2 + other) * halves + half, rows)],
+            context_sib.at[block(place * halves + half, rows)],
+            context_send.at[place, half],
+            context_recv.at[place, half],
+            sibling,
+        )
+
+    def chunk_rows(place, chunk):
+        return block(place * CHUNKS + chunk, step)
+
+    def attn_part(place, chunk):
+        return dot_nt(
+            context_ref[chunk_rows(place * 2 + core, chunk), :], full_out_ref[...]
+        ) + dot_nt(context_sib[chunk_rows(place, chunk), :], out_sib[...])
+
+    def sum_copy(chunk, offset):
+        rows = block(chunk, step)
+        return remote(
+            sum_out.at[offset - 1, rows],
+            sum_in.at[levels - offset - 1, rows],
+            sum_send.at[chunk, offset - 1],
+            sum_recv.at[chunk, levels - offset - 1],
+            (row, peer_level(offset) * 2 + core),
+        )
+
+    def normed_copy(chunk, offset):
+        view = normed_full.at[chunk_rows(level, chunk)]
+        return remote(
+            view,
+            view,
+            normed_send.at[chunk, offset - 1],
+            normed_recv.at[chunk, levels - offset - 1],
+            (row, peer_level(offset) * 2 + core),
+        )
+
+    for offset in list(offsets) + [0]:
+        place = peer_level(offset)
+        for half in range(halves):
+            attend_half(place * 2 + other, half)
+            context_copy(place, half).start()
+            pass_on(half if len(waiting) > along - 1 else 0)
+        if offset == 1:
+            await_shards(1)
+        for half in range(halves):
+            attend_half(place * 2 + core, half)
+            if offset == 1 and half == 0:
+                await_sibling(1)
+            context_copy(place, half).wait_recv()
+            per_half = CHUNKS // halves
+            for chunk in range(half * per_half, (half + 1) * per_half):
+                if offset:
+                    sum_out[offset - 1, block(chunk, step), :] = attn_part(place, chunk).astype(
+                        low
+                    )
+                    sum_copy(chunk, offset).start()
+        pass_on(1 if len(waiting) > along - 1 else 0)
+    pass_on(max(len(waiting) - (along - 1), 0))
+    await_shards(2)
+    for chunk in range(CHUNKS):
+        rows = block(chunk, step)
+        summed = own_ref[rows, :].astype(full) + attn_part(level, chunk) + b_out[...]
+        for offset in offsets:
+            sum_copy(chunk, offset).wait_recv()
+        for place in range(levels - 1):
+            summed += sum_in[place, rows, :].astype(full)
+        normed, inv_std = norm_parts(summed)
+        unit1[rows, :] = normed
+        inv1[rows, :] = inv_std
+        normed_full[chunk_rows(level, chunk), :] = (normed * gain1[...] + shift1[...]).astype(low)
+        for offset in offsets:
+            normed_copy(chunk, offset).start()
+        pass_on(1 if chunk else 0)
     pass_on(len(waiting))
-    for kind in range(1, FRONT_KINDS):
-        await_shards(kind)
+    await_shards(3)
+    for chunk in range(CHUNKS):
+        for offset in offsets:
+            normed_copy(chunk, offset).wait()
+            sum_copy(chunk, offset).wait_send()
+    for kind in range(2, KINDS):
+        await_sibling(kind)
+    for place in range(levels):
+        for half in range(halves):
+            context_copy(place, half).wait_send()
     for copy in swaps:
         copy.wait()
-    for kind in range(FRONT_KINDS):
+    for kind in range(KINDS):
         for offset in range(1, along):
             along_copy(kind, offset).wait_send()
 
@@ -496,6 +626,9 @@
         def _(place):
             for offset in range(1, across):
                 across_copy(kind, place, offset).wait_send()
+            if kind > 0:
+                for offset in range(across):
+                    core_shard(kind, place, offset).wait_send()
 
     @pl.loop(0, cols)
     def _(turn):
@@ -509,7 +642,7 @@
     return 2 if rows <= 8 else rows // 4
 
 
-def front(levels, rows, tables, hidden_in, grads, biases, parts):
+def front(levels, rows, tables, hidden_in, grads, biases, parts, vectors):
     low, full = jnp.bfloat16, jnp.float32
     shape = jax.ShapeDtypeStruct
     across = across_of(rows)
@@ -534,30 +667,42 @@
             stat,
             stat,
             *(shape((part.shape[0] * rows, part.shape[1]), low) for part in parts),
+            *(shape((part.shape[0] * rows, part.shape[1]), low) for part in parts[1:]),
+            shape((levels * own_len, width), low),
+            shape((levels * own_len, features_all), low),
+            shape((own_len, features_all), full),
+            shape((own_len, 1), full),
         ),
-        in_specs=[SMEM] * 2 + [VMEM] * 8,
-        out_specs=[VMEM] * 12,
+        in_specs=[SMEM] * 2 + [VMEM] * 10,
+        out_specs=[VMEM] * 20,
         scratch_shapes=[
+            pltpu.VMEM((others, own_len, features_all), low),
+            pltpu.VMEM((others, own_len, features_all), low),
             dma((cols, others)),
             dma((cols, others)),
             dma((cols, levels)),
             dma((cols, levels)),
             dma((cols,)),
             dma((cols,)),
-            dma((FRONT_KINDS, along - 1)),
-            dma((FRONT_KINDS, along - 1)),
-            dma((FRONT_KINDS, along, across - 1)),
-            dma((FRONT_KINDS, along, across - 1)),
+            dma((KINDS, along - 1)),
+            dma((KINDS, along - 1)),
+            dma((KINDS, along, across - 1)),
+            dma((KINDS, along, across - 1)),
+            dma((KINDS - 1, along, across)),
+            dma((KINDS - 1, along, across)),
+            dma((levels, 2)),
+            dma((levels, 2)),
+            *(dma((CHUNKS, others)) for _ in range(4)),
         ],
         compiler_params=pltpu.CompilerParams(
-            collective_id=3, has_side_effects=True, vmem_limit_bytes=48 * 1024 * 1024
+            collective_id=3, has_side_effects=True, vmem_limit_bytes=56 * 1024 * 1024
         ),
         cost_estimate=pl.CostEstimate(
             flops=2 * seq_len * features_all * 3 * width,
             bytes_accessed=20 * 1024 * 1024,
             transcendentals=seq_len * 512 * (width // DH),
         ),
-    )(*tables, hidden_in, grads, *biases, *parts)
+    )(*tables, hidden_in, grads, *biases, *parts, vectors)
 
 
 def dot(left, right):
@@ -601,20 +746,23 @@
     return inv_std * (scaled - left - normed * right)
 
 
-CHUNKS = 4
-
-
 def middle_kernel(
     levels,
     across,
     along,
     context_ref,
-    inputs_ref,
+    context_sib,
     upstream_ref,
     valid_ref,
     out_ref,
+    out_sib,
     up_ref,
-    part_down_ref,
+    up_sib,
+    down_full,
+    down_sib,
+    normed_full,
+    unit1,
+    inv1,
     vectors_ref,
     b_up_ref,
     layer_out_ref,
@@ -625,18 +773,10 @@
     share_down_ref,
     up_part_ref,
     grad_out_ref,
-    context_sib,
-    out_sib,
-    up_sib,
-    down_full,
-    down_sib,
-    normed_full,
     ffn_full,
     hidden,
     slope,
     pre_grad,
-    unit1,
-    inv1,
     ffn_keep,
     part_own,
     send_buf,
@@ -653,8 +793,6 @@
     recv_sem,
     core_send,
     core_recv,
-    shard_send,
-    shard_recv,
     along_send,
     along_recv,
     across_send,
@@ -667,8 +805,8 @@
     level = lax.div(column, 2)
     sibling = (row, column + 1 - 2 * core)
     fast, slow = lax.rem(row, across), lax.div(row, across)
-    shard = part_down_ref.shape[0]
-    own_len = inputs_ref.shape[0]
+    shard = share_down_ref.shape[0]
+    own_len = upstream_ref.shape[0]
     step = own_len // CHUNKS
     b_out, gain1, shift1, b_down, gain2, shift2 = (
         vectors_ref.at[place : place + 1, :] for place in range(6)
@@ -708,44 +846,6 @@
     def to_sibling(source, target, place):
         return remote(source, target, core_send.at[place], core_recv.at[place], sibling)
 
-    def shard_view(ref, place, position):
-        return ref.at[block(place * across + position, shard)]
-
-    def along_down(offset):
-        view = shard_view(down_full, slow, fast)
-        return remote(
-            view,
-            view,
-            along_send.at[0, offset - 1],
-            along_recv.at[0, along - offset - 1],
-            (slow_peer(offset), column),
-        )
-
-    def across_down(place, offset):
-        view = shard_view(down_full, place, fast)
-        return remote(
-            view,
-            view,
-            across_send.at[0, place, offset - 1],
-            across_recv.at[0, place, across - offset - 1],
-            (fast_peer(offset), column),
-        )
-
-    def core_down(place, offset):
-        position = lax.rem(fast + offset, across)
-        return remote(
-            shard_view(down_full, place, position),
-            shard_view(down_sib, place, position),
-            shard_send.at[place, offset],
-            shard_recv.at[place, offset],
-            sibling,
-        )
-
-    def pass_down(place):
-        for offset in range(1, across):
-            across_down(place, offset).start()
-        core_down(place, 0).start()
-
     def rows_of(place, chunk):
         return pl.ds(pl.multiple_of(place * own_len + chunk * step, step), step)
 
@@ -756,8 +856,8 @@
         return pltpu.make_async_remote_copy(
             src_ref=source,
             dst_ref=target,
-            send_sem=send_sem.at[kind, chunk, offset - 1],
-            recv_sem=recv_sem.at[kind, chunk, levels - offset - 1],
+            send_sem=send_sem.at[kind - 2, chunk, offset - 1],
+            recv_sem=recv_sem.at[kind - 2, chunk, levels - offset - 1],
             device_id=(row, peer_level(offset) * 2 + core),
             device_id_type=MESH,
         )
@@ -767,93 +867,27 @@
             kind,
             chunk,
             offset,
-            send_buf.at[kind // 2, offset - 1, own_rows(chunk)],
-            recv_buf.at[kind // 2, levels - offset - 1, own_rows(chunk)],
+            send_buf.at[kind // 2 - 1, offset - 1, own_rows(chunk)],
+            recv_buf.at[kind // 2 - 1, levels - offset - 1, own_rows(chunk)],
         )
 
     def spread_copy(kind, chunk, offset):
-        whole = {1: normed_full, 3: ffn_full, 5: attn_full}[kind]
+        whole = {3: ffn_full, 5: attn_full}[kind]
         rows = rows_of(level, chunk)
         return exchange(kind, chunk, offset, whole.at[rows], whole.at[rows])
 
     def received(kind, chunk):
         return sum(
-            recv_buf[kind // 2, place, own_rows(chunk), :].astype(jnp.float32)
+            recv_buf[kind // 2 - 1, place, own_rows(chunk), :].astype(jnp.float32)
             for place in range(levels - 1)
         )
 
     offsets = range(1, levels)
-    context_copies = [
-        to_sibling(
-            context_ref.at[
-                pl.ds(pl.multiple_of((place * 2 + 1 - core) * own_len, own_len), own_len)
-            ],
-            context_sib.at[pl.ds(place * own_len, own_len)],
-            place,
-        )
-        for place in range(levels)
-    ]
-    out_copy = to_sibling(out_ref, out_sib, levels)
-    up_copy = to_sibling(up_ref, up_sib, levels + 1)
-    for copy in context_copies + [out_copy]:
-        copy.start()
-    down_full[block(slow * across + fast, shard), :] = part_down_ref[...]
-    for offset in range(1, along):
-        along_down(offset).start()
-    pass_down(slow)
-    up_copy.start()
     small_ref[...] = jnp.zeros_like(small_ref)
     up_small_ref[...] = jnp.zeros_like(up_small_ref)
-    for copy in context_copies:
-        copy.wait()
-    out_copy.wait()
-
     def context_rows(place, chunk):
         start = (place * 2 + core) * own_len + chunk * step
         return pl.ds(pl.multiple_of(start, step), step)
-
-    def attn_part(place, chunk):
-        return dot_nt(context_ref[context_rows(place, chunk), :], out_ref[...]) + dot_nt(
-            context_sib[rows_of(place, chunk), :], out_sib[...]
-        )
-
-    @pl.loop(0, CHUNKS)
-    def _(chunk):
-        for offset in offsets:
-            send_buf[0, offset - 1, own_rows(chunk), :] = attn_part(
-                peer_level(offset), chunk
-            ).astype(low)
-            sum_copy(0, chunk, offset).start()
-
-    for chunk in range(CHUNKS):
-        rows = own_rows(chunk)
-        summed = (
-            inputs_ref[rows, :].astype(jnp.float32) + attn_part(level, chunk) + b_out[...]
-        )
-        for offset in offsets:
-            sum_copy(0, chunk, offset).wait_recv()
-        normed, inv_std = norm_parts(summed + received(0, chunk))
-        unit1[rows, :] = normed
-        inv1[rows, :] = inv_std
-        normed_full[rows_of(level, chunk), :] = (normed * gain1[...] + shift1[...]).astype(low)
-        for offset in offsets:
-            spread_copy(1, chunk, offset).start()
-        for offset in range(1, along):
-            if min(offset, CHUNKS - 1) == chunk:
-                along_down(along - offset).wait_recv()
-                pass_down(lax.rem(slow + offset, along))
-
-    for turn in range(along):
-        place = lax.rem(slow + turn, along)
-        for offset in range(1, across):
-            across_down(place, across - offset).wait_recv()
-            core_down(place, offset).start()
-    up_copy.wait()
-
-    @pl.loop(0, along)
-    def _(place):
-        for offset in range(across):
-            core_down(place, offset).wait_recv()
 
     sides = ((up_ref, down_full), (up_sib, down_sib))
 
@@ -872,10 +906,8 @@
 
     @pl.loop(0, CHUNKS)
     def _(chunk):
-        part_own[own_rows(chunk), :] = feed_forward(level, chunk)
         for offset in offsets:
-            spread_copy(1, chunk, levels - offset).wait_recv()
-            send_buf[1, offset - 1, own_rows(chunk), :] = feed_forward(
+            send_buf[0, offset - 1, own_rows(chunk), :] = feed_forward(
                 peer_level(offset), chunk
             ).astype(low)
             sum_copy(2, chunk, offset).start()
@@ -883,6 +915,7 @@
     @pl.loop(0, CHUNKS)
     def _(chunk):
         rows = own_rows(chunk)
+        part_own[rows, :] = feed_forward(level, chunk)
         normed1 = unit1[rows, :] * gain1[...] + shift1[...]
         summed = normed1 + part_own[rows, :] + b_down[...]
         for offset in offsets:
@@ -923,7 +956,7 @@
         part_own[own_rows(chunk), :] = feed_back(level, chunk)
         for offset in offsets:
             spread_copy(3, chunk, levels - offset).wait_recv()
-            send_buf[2, offset - 1, own_rows(chunk), :] = feed_back(
+            send_buf[1, offset - 1, own_rows(chunk), :] = feed_back(
                 peer_level(offset), chunk
             ).astype(low)
             sum_copy(4, chunk, offset).start()
@@ -937,15 +970,15 @@
 
     def core_grad(kind):
         return to_sibling(
-            slope.at[kind, : sums[kind].shape[0]], sums[kind], 2 * levels + 2 + kind
+            slope.at[kind, : sums[kind].shape[0]], sums[kind], levels + kind
         )
 
     def across_grad(kind, turn, offset):
         return remote(
             sums[kind].at[block(turn * across + lax.rem(fast + offset, across), shard)],
             got[kind].at[across - offset - 1, block(turn, shard)],
-            across_send.at[1 + kind, turn, offset - 1],
-            across_recv.at[1 + kind, turn, across - offset - 1],
+            across_send.at[kind, turn, offset - 1],
+            across_recv.at[kind, turn, across - offset - 1],
             (fast_peer(offset), column),
         )
 
@@ -953,8 +986,8 @@
         return remote(
             down_pass.at[offset - 1],
             down_in.at[along - offset - 1],
-            along_send.at[1, offset - 1],
-            along_recv.at[1, along - offset - 1],
+            along_send.at[offset - 1],
+            along_recv.at[along - offset - 1],
             (slow_peer(offset), column),
         )
 
@@ -1025,7 +1058,7 @@
             context_grad_ref.at[
                 pl.ds(pl.multiple_of((place * 2 + core) * own_len, own_len), own_len)
             ],
-            levels + 2 + place,
+            place,
         )
         for place in range(levels)
     ]
@@ -1061,21 +1094,17 @@
     for kind in range(2):
         core_grad(kind).wait_send()
     for offset in range(1, along):
-        along_down(offset).wait_send()
         along_grad(offset).wait_send()
 
     @pl.loop(0, along)
     def _(place):
         for offset in range(1, across):
-            across_down(place, offset).wait_send()
             across_grad(0, place, offset).wait_send()
             across_grad(1, place, offset).wait_send()
-        for offset in range(across):
-            core_down(place, offset).wait_send()
 
     for copy in back_copies:
         copy.wait()
-    for kind in range(6):
+    for kind in range(2, 6):
 
         @pl.loop(0, CHUNKS)
         def _(chunk):
@@ -1087,14 +1116,26 @@
 
 
 def middle(
-    levels, rows, context, inputs, upstream, valid, out_own, up_own, part_down, vectors, b_up_pair
+    levels,
+    rows,
+    context,
+    context_sib,
+    upstream,
+    valid,
+    weights,
+    normed_full,
+    unit1,
+    inv1,
+    vectors,
+    b_up_pair,
 ):
     low, full = jnp.bfloat16, jnp.float32
     across = across_of(rows)
     along = rows // across
-    own_len, features = inputs.shape
+    own_len, features = upstream.shape
     seq_len, width = context.shape
-    shard, units = part_down.shape
+    units = weights[2].shape[1]
+    shard = features // rows
     tokens = levels * own_len
     others = levels - 1
     shape = jax.ShapeDtypeStruct
@@ -1113,25 +1154,17 @@
             shape((along, shard, units), low),
             shape((2, features, width), low),
         ),
-        in_specs=[VMEM] * 9,
+        in_specs=[VMEM] * 15,
         out_specs=[VMEM] * 7 + [hbm],
         scratch_shapes=[
-            vmem((tokens, width), low),
-            vmem((features, width), low),
-            vmem((features, units), low),
-            vmem((features, units), low),
-            vmem((features, units), low),
-            vmem((tokens, features), low),
             vmem((tokens, features), low),
             vmem((2, tokens, units), low),
             vmem((2, max(tokens, features), units), low),
             vmem((2, tokens, units), low),
             vmem((own_len, features), full),
-            vmem((own_len, 1), full),
             vmem((own_len, features), full),
-            vmem((own_len, features), full),
-            vmem((3, others, own_len, features), low),
-            vmem((3, others, own_len, features), low),
+            vmem((2, others, own_len, features), low),
+            vmem((2, others, own_len, features), low),
             vmem((tokens, width), low),
             vmem((2, features, width), low),
             vmem((features, units), low),
@@ -1140,16 +1173,14 @@
             vmem((across - 1, along * shard, units), low),
             vmem((along - 1, shard, units), low),
             vmem((along - 1, shard, units), low),
-            dma((6, CHUNKS, others)),
-            dma((6, CHUNKS, others)),
-            dma((2 * levels + 4,)),
-            dma((2 * levels + 4,)),
-            dma((along, across)),
-            dma((along, across)),
-            dma((2, along - 1)),
-            dma((2, along - 1)),
-            dma((3, along, across - 1)),
-            dma((3, along, across - 1)),
+            dma((4, CHUNKS, others)),
+            dma((4, CHUNKS, others)),
+            dma((levels + 2,)),
+            dma((levels + 2,)),
+            dma((along - 1,)),
+            dma((along - 1,)),
+            dma((2, along, across - 1)),
+            dma((2, along, across - 1)),
             dma((2,)),
         ],
         compiler_params=pltpu.CompilerParams(
@@ -1160,7 +1191,18 @@
             bytes_accessed=20 * 1024 * 1024,
             transcendentals=2 * tokens * units,
         ),
-    )(context, inputs, upstream, valid, out_own, up_own, part_down, vectors, b_up_pair)
+    )(
+        context,
+        context_sib,
+        upstream,
+        valid,
+        *weights,
+        normed_full,
+        unit1,
+        inv1,
+        vectors,
+        b_up_pair,
+    )
 
 
 def end_kernel(
@@ -1621,6 +1663,7 @@
         rand_blocks.reshape(-1),
         limits_of(length, global_blocks[0], rand_blocks[0], num_blocks, head_count),
     )
+    vectors = jnp.stack([b_out, ln1_gain, ln1_bias, b_down, ln2_gain, ln2_bias, b_out, b_out])
     valid = (jnp.arange(seq_len) < length)[:, None]
     own_valid = (own_start + jnp.arange(own_len) < length).astype(jnp.float32)[:, None]
     (
@@ -1631,10 +1674,19 @@
         key_rows,
         value_rows,
         context,
-        *stats,
+        highest,
+        scale,
         full_qkv,
         full_out,
         full_up,
+        full_down,
+        out_sib,
+        up_sib,
+        down_sib,
+        context_sib,
+        normed_full,
+        unit1,
+        inv1,
     ) = front(
         cols // 2,
         lax.axis_size("row"),
@@ -1649,7 +1701,9 @@
             jnp.concatenate([w_query, w_key, w_value], axis=1).astype(low),
             w_out.T.astype(low),
             w_up.astype(low),
+            w_down.T.astype(low),
         ),
+        vectors,
     )
 
     sibling = column + 1 - 2 * lax.rem(column, 2)
@@ -1657,13 +1711,14 @@
         cols // 2,
         lax.axis_size("row"),
         context,
-        own_features,
+        context_sib,
         upstream,
         own_valid,
-        full_out,
-        full_up,
-        w_down.T.astype(low),
-        jnp.stack([b_out, ln1_gain, ln1_bias, b_down, ln2_gain, ln2_bias, b_out, b_out]),
+        (full_out, out_sib, full_up, up_sib, full_down, down_sib),
+        normed_full,
+        unit1,
+        inv1,
+        vectors,
         jnp.stack(
             [
                 lax.dynamic_slice_in_dim(b_up, unit_start, unit_cols),
@@ -1672,7 +1727,7 @@
         ),
     )
     query_key_value, bias_sums = attend_back(
-        queries, key_rows, value_rows, tables, stats, context_grad
+        queries, key_rows, value_rows, tables, (highest, scale), context_grad
     )
     up_sums = into_full(up_small[0], unit_start, units_all) + into_full(
         up_small[1], sibling * unit_cols, units_all

time: 372 us -> 374 us (level); the launches traced: 371 us -> 367 us
  Pallas kernels: 338 us -> 333 us
    pallas_call x1, Pallas kernels: 175 us -> 125 us  [middle(): pl.pallas_call(functools.partial(middle_kernel, levels, across, along), o...]
    pallas_call x1, Pallas kernels: 70.5 us -> 120 us  [front(): pl.pallas_call(functools.partial(front_kernel, levels, across, along), ou...]
    unnamed x66 -> x68, local copies, waits for them, and re-layouts: 17 us -> 13.9 us
where the time goes in v6:
time: 374 us; the launch traced here: 367 us
  Pallas kernels  333 us (89%)
  local copies, waits for them, and re-layouts  24.9 us (7%)
  other arithmetic  7.13 us (2%)
    pallas_call x1, Pallas kernels, middle(): pl.pallas_call(functools.partial(middle_kernel, levels, across, along), o...  125 us
    pallas_call x1, Pallas kernels, front(): pl.pallas_call(functools.partial(front_kernel, levels, across, along), ou...  120 us
    pallas_call x1, Pallas kernels, finish(): pl.pallas_call(functools.partial(end_kernel, levels, across, along), out_...  64.4 us
    pallas_call x1, Pallas kernels, attend_back(): pl.pallas_call(functools.partial(attend_back_kernel, head_count, 8), out_...  23.8 us
    unnamed x68, local copies, waits for them, and re-layouts  13.9 us

profile of v6, /device:TPU:0, one launch (start us, length us, event | category | flops | bytes accessed | tf_op | source)
XLA Modules:
  0.0 367.1 jit_solution(12386755951392200107)
XLA Ops:
  0.8 0.8 fusion.5
  2.1 1.3 dynamic_slice.12
  3.5 1.3 dynamic_slice.13
  8.6 0.8 pad_add_fusion.limits_ref
  9.3 1.2 broadcast_select_fusion.grads_ref
  10.7 0.8 reshape.138.random_ref
  13.0 0.8 copy.71
  15.3 120.0 %shard_map.323 = (bf16[2048,1024]{1,0:T(8,128)(2,1)}, bf16[512,1024]{1,0:T(8,128)(2,1)}, bf16[512,1024]{1,0:T(8,128)(2,1)}, bf16[2048,256]{1,0:T(8,128)(2,1)}, b...) custom-call(s32[2]{0:T(128)} %bitcast.47, ...), custom_call_target="tpu_custom_call" | custom-call | flops 3221225472 | bytes 20971520 | tf_op jit(solution)/shard_map/pallas_call | solution.py:657
  136.1 124.7 %shard_map.324 = (bf16[512,1024]{1,0:T(8,128)(2,1)}, bf16[2048,256]{1,0:T(8,128)(2,1)}, bf16[1024,1024]{1,0:T(8,128)(2,1)}, f32[8,1024]{1,0:T(8,128)}, f32[2,102...) custom-call(bf16[2048,256]{1,0:T(8,128)(2,1)} %get-tuple-element.55.context_ref, ...), custom_call_target="tpu_custom_call" | custom-call | flops 28991029248 | bytes 20971520 | tf_op jit(solution)/shard_map/pallas_call | solution.py:1145
  260.8 0.8 fusion.6
  262.0 1.2 copy-done.5
  263.2 1.2 copy-done.6
  264.5 1.2 copy-done.7
  265.7 23.8 %shard_map.325 = (bf16[2048,768]{1,0:T(8,128)(2,1)S(1)}, f32[2,256]{1,0:T(2,128)S(1)}) custom-call(s32[2]{0:T(128)S(1)} %bitcast.48, s32[384]{0:T(512)S(1)} %copy-done.1, s32[32,8,256]{2,1,0:T(8,128)S(1)} %copy-done, bf16[2048,256]{1,0:T(8,128)(2,1)S(1)} %copy-done.4, bf16[32,64,256]{2,1,0:T(8,128)(2,1)S(1)} %copy-done.5, ...), custom_call_target="tpu_custom_call" | custom-call | flops 10737418240 | bytes 7340032 | tf_op jit(solution)/shard_map/pallas_call | solution.py:249
  289.5 1.7 copy-done.3
  291.8 64.4 %shard_map.326 = (bf16[2048,256]{1,0:T(8,128)(2,1)}, bf16[2048,256]{1,0:T(8,128)(2,1)}, f32[16,1024]{1,0:T(8,128)}, f32[128,256]{1,0:T(8,128)}, f32[128,768]{1,0:T(8,128)}, /*index=5*/f32[128,1024]{1,0:T(8,128)}) custom-call(bf16[2048,768]{1,0:T(8,128)(2,1)} %copy-done.3, bf16[1024,768]{1,0:T(8,128)(2,1)} %get-tuple-element.71.weights_ref, ...), custom_call_target="tpu_custom_call" | custom-call | flops 6442450944 | bytes 41943040 | tf_op jit(solution)/shard_map/pallas_call | solution.py:1569
  356.2 1.9 fusion.3
  358.1 1.7 copy.73
  359.8 1.7 fusion.4
  361.5 0.8 slice_bitcast_fusion
  362.9 1.0 copy.74
  363.9 1.0 copy.85
  364.9 1.0 copy.86
  365.9 0.8 copy.87
  (86 shorter events, 9.1 us)
Async XLA Ops:
  0.7 9.9 %copy-start.23 = (s32[1,32,4,3]{1,2,3,0:T(4,128)S(1)}, s32[1,32,4,3]{1,2,3,0:T(4,128)}, u32[]{:S(2)}) copy-start(s32[1,32,4,3]{1,2,3,0:T(4,128)} %param.24) | copy-start | bytes 4612
  0.7 8.7 %copy-start.10 = (bf16[2048,256]{1,0:T(8,128)(2,1)S(1)}, bf16[2048,256]{1,0:T(8,128)(2,1)}, u32[]{:S(2)}) copy-start(bf16[2048,256]{1,0:T(8,128)(2,1)} %param.21) | copy-start | bytes 3145732
  0.7 10.8 %copy-start.25 = (f32[1024]{0:T(1024)S(1)}, f32[1024]{0:T(1024)}, u32[]{:S(2)}) copy-start(f32[1024]{0:T(1024)} %param.33) | copy-start | bytes 12292
  0.7 10.8 %copy-start.26 = (f32[1024]{0:T(1024)S(1)}, f32[1024]{0:T(1024)}, u32[]{:S(2)}) copy-start(f32[1024]{0:T(1024)} %param.37) | copy-start | bytes 12292
  0.7 10.8 %copy-start.27 = (f32[1024]{0:T(1024)S(1)}, f32[1024]{0:T(1024)}, u32[]{:S(2)}) copy-start(f32[1024]{0:T(1024)} %param.38) | copy-start | bytes 12292
  0.7 10.8 %copy-start.28 = (f32[1024]{0:T(1024)S(1)}, f32[1024]{0:T(1024)}, u32[]{:S(2)}) copy-start(f32[1024]{0:T(1024)} %param.39) | copy-start | bytes 12292
  0.7 10.8 %copy-start.21 = (f32[1024]{0:T(1024)S(1)}, f32[1024]{0:T(1024)}, u32[]{:S(2)}) copy-start(f32[1024]{0:T(1024)} %param.31) | copy-start | bytes 12292
  0.7 10.8 %copy-start.24 = (f32[1024]{0:T(1024)S(1)}, f32[1024]{0:T(1024)}, u32[]{:S(2)}) copy-start(f32[1024]{0:T(1024)} %param.32) | copy-start | bytes 12292
  0.8 11.4 %copy-start.17 = (f32[128,256]{1,0:T(8,128)S(1)}, f32[128,256]{1,0:T(8,128)}, u32[]{:S(2)}) copy-start(f32[128,256]{1,0:T(8,128)} %param.27) | copy-start | bytes 393220
  7.2 5.0 %copy-start.18 = (f32[128,256]{1,0:T(8,128)S(1)}, f32[128,256]{1,0:T(8,128)}, u32[]{:S(2)}) copy-start(f32[128,256]{1,0:T(8,128)} %param.28) | copy-start | bytes 393220
  8.0 4.2 %copy-start.19 = (f32[128,256]{1,0:T(8,128)S(1)}, f32[128,256]{1,0:T(8,128)}, u32[]{:S(2)}) copy-start(f32[128,256]{1,0:T(8,128)} %param.25) | copy-start | bytes 393220
  8.5 4.5 %copy-start.13 = (f32[1024,128]{1,0:T(8,128)S(1)}, f32[1024,128]{1,0:T(8,128)}, u32[]{:S(2)}) copy-start(f32[1024,128]{1,0:T(8,128)} %param.36) | copy-start | bytes 1572868
  9.3 4.5 %copy-start.14 = (f32[128,1024]{1,0:T(8,128)S(1)}, f32[128,1024]{1,0:T(8,128)}, u32[]{:S(2)}) copy-start(f32[128,1024]{1,0:T(8,128)} %param.34) | copy-start | bytes 1572868
  9.3 5.2 %copy-start.20 = (f32[256,128]{1,0:T(8,128)S(1)}, f32[256,128]{1,0:T(8,128)}, u32[]{:S(2)}) copy-start(f32[256,128]{1,0:T(8,128)} %param.30) | copy-start | bytes 393220
  136.1 125.9 %copy-start = (s32[32,8,256]{2,1,0:T(8,128)S(1)}, s32[32,8,256]{2,1,0:T(8,128)}, u32[]{:S(2)}) copy-start(s32[32,8,256]{2,1,0:T(8,128)} %pad_add_fusion.limits_ref) | copy-start | bytes 786436
  136.1 125.9 %copy-start.1 = (s32[384]{0:T(512)S(1)}, s32[384]{0:T(512)}, u32[]{:S(2)}) copy-start(s32[384]{0:T(512)} %reshape.138.random_ref) | copy-start | bytes 4612
  136.1 125.9 %copy-start.2 = (s32[1,2]{1,0:T(1,128)S(1)}, s32[1,2]{1,0:T(1,128)}, u32[]{:S(2)}) copy-start(s32[1,2]{1,0:T(1,128)} %param.23) | copy-start | bytes 28
  136.1 125.9 %copy-start.4 = (bf16[2048,256]{1,0:T(8,128)(2,1)S(1)}, bf16[2048,256]{1,0:T(8,128)(2,1)}, u32[]{:S(2)}) copy-start(bf16[2048,256]{1,0:T(8,128)(2,1)} %get-tuple-element.52.queries_ref) | copy-start | bytes 3145732
  136.1 125.9 %copy-start.8 = (f32[32,1,256]{2,1,0:T(1,128)S(1)}, f32[32,1,256]{2,1,0:T(1,128)}, u32[]{:S(2)}) copy-start(f32[32,1,256]{2,1,0:T(1,128)} %get-tuple-element.68.highest_ref) | copy-start | bytes 98308
  136.1 125.9 %copy-start.9 = (f32[32,1,256]{2,1,0:T(1,128)S(1)}, f32[32,1,256]{2,1,0:T(1,128)}, u32[]{:S(2)}) copy-start(f32[32,1,256]{2,1,0:T(1,128)} %get-tuple-element.69.scale_ref) | copy-start | bytes 98308
  265.7 25.5 %copy-start.22 = (f32[8,1024]{1,0:T(8,128)S(1)}, f32[8,1024]{1,0:T(8,128)}, u32[]{:S(2)}) copy-start(f32[8,1024]{1,0:T(8,128)} %get-tuple-element.75) | copy-start | bytes 98308
  291.8 71.1 %copy-start.15 = (f32[128,1024]{1,0:T(8,128)S(1)}, f32[128,1024]{1,0:T(8,128)}, u32[]{:S(2)}) copy-start(f32[128,1024]{1,0:T(8,128)} %get-tuple-element.86) | copy-start | bytes 1572868
  356.2 7.7 %copy-start.12 = (bf16[2048,256]{1,0:T(8,128)(2,1)S(1)}, bf16[2048,256]{1,0:T(8,128)(2,1)}, u32[]{:S(2)}) copy-start(bf16[2048,256]{1,0:T(8,128)(2,1)} %get-tuple-element.204) | copy-start | bytes 3145732
  356.2 8.7 %copy-start.11 = (bf16[2048,256]{1,0:T(8,128)(2,1)S(1)}, bf16[2048,256]{1,0:T(8,128)(2,1)}, u32[]{:S(2)}) copy-start(bf16[2048,256]{1,0:T(8,128)(2,1)} %get-tuple-element.205) | copy-start | bytes 3145732
  (5 other events, 7.3 us)

commit v7 on v6

--- a/solution.py
+++ b/solution.py
@@ -87,23 +87,31 @@
                 )
 
 
-def masked_scores(picked_keys, grouped, limits_ref, step, width):
+def masked_scores(picked_keys, grouped, step, num_blocks, length, shared, apart):
+    width = grouped.shape[1]
     scores = lax.dot_general(
         picked_keys, grouped, (((1,), (1,)), ((), ())), preferred_element_type=jnp.float32
     )
+    listed = [step >= 1, True, step + 1 < num_blocks]
+    listed += [(block < step - 1) | (block > step + 1) for block in shared[3:]]
+    limits = [
+        jnp.where(there, length - block * BLK, 0) for there, block in zip(listed, shared)
+    ]
+    lane_head = lane_heads(1, width)
+    for blocks in apart:
+        limit = length - jnp.full((1, width), blocks[0], jnp.int32) * BLK
+        for head, block in enumerate(blocks[1:], 1):
+            limit = jnp.where(lane_head >= head, length - block * BLK, limit)
+        limits.append(limit)
     row = lax.broadcasted_iota(jnp.int32, (BLK, width), 0)
     return [
-        jnp.where(
-            row < limits_ref[step, slot : slot + 1, :],
-            scores[slot * BLK : (slot + 1) * BLK, :],
-            -1e30,
-        )
-        for slot in range(8)
+        jnp.where(row < limit, scores[slot * BLK : (slot + 1) * BLK, :], -1e30)
+        for slot, limit in enumerate(limits)
     ]
 
 
 def attend_blocks(
-    first, count, unroll, globals_ref, random_ref, limits_ref, refs, context_ref, stat_refs
+    first, count, unroll, length_ref, globals_ref, random_ref, refs, context_ref, stat_refs
 ):
     queries_ref, keys_ref, values_ref = refs
     highest_ref, scale_ref = stat_refs
@@ -116,7 +124,13 @@
         own = pl.ds(pl.multiple_of(step * BLK, BLK), BLK)
         grouped = by_diagonal(queries_ref[own, :] * jnp.bfloat16(1.0 / math.sqrt(DH)), width)
         scores = masked_scores(
-            picked_rows(keys_ref, shared, apart, head_count), grouped, limits_ref, step, width
+            picked_rows(keys_ref, shared, apart, head_count),
+            grouped,
+            step,
+            num_blocks,
+            length_ref[0],
+            shared,
+            apart,
         )
         highest = jnp.max(functools.reduce(jnp.maximum, scores), axis=0, keepdims=True)
         exponent = [jnp.exp(piece - highest) for piece in scores]
@@ -144,9 +158,9 @@
 def attend_back_kernel(
     head_count,
     unroll,
+    length_ref,
     globals_ref,
     random_ref,
-    limits_ref,
     queries_ref,
     keys_ref,
     values_ref,
@@ -173,7 +187,9 @@
         grouped_grad = by_diagonal(grads_ref[own, :], width)
         picked_keys = picked_rows(keys_ref, shared, apart, head_count)
         picked_values = picked_rows(values_ref, shared, apart, head_count)
-        scores = masked_scores(picked_keys, grouped, limits_ref, step, width)
+        scores = masked_scores(
+            picked_keys, grouped, step, num_blocks, length_ref[0], shared, apart
+        )
         highest = highest_ref[step]
         scale = scale_ref[step]
         attn_probs = [jnp.exp(piece - highest) * scale for piece in scores]
@@ -220,25 +236,6 @@
     bias_ref[1:2, :] = jnp.sum(value_grad.astype(jnp.float32), axis=0, keepdims=True)
 
 
-def limits_of(length, global_ids, random_ids, num_blocks, head_count):
-    blocks = jnp.arange(num_blocks, dtype=jnp.int32)
-    nearby_raw = blocks[:, None] + jnp.arange(-1, 2, dtype=jnp.int32)[None, :]
-    near_ok = (nearby_raw >= 0) & (nearby_raw < num_blocks)
-    global_rows = jnp.broadcast_to(global_ids[None, :], (num_blocks, 2))
-    global_ok = jnp.all(global_rows[:, :, None] != nearby_raw[:, None, :], axis=2)
-    common = jnp.concatenate([nearby_raw, global_rows], axis=1)
-    common_ok = jnp.concatenate([near_ok, global_ok], axis=1)
-    common_limit = jnp.where(common_ok, length - common * BLK, 0)
-    random_limit = jnp.transpose(length - random_ids * BLK, (0, 2, 1))
-    return jnp.concatenate(
-        [
-            jnp.broadcast_to(common_limit[:, :, None], (num_blocks, 5, head_count * DH)),
-            jnp.repeat(random_limit, DH, axis=2),
-        ],
-        axis=1,
-    )
-
-
 VMEM = pl.BlockSpec(memory_space=pltpu.VMEM)
 SMEM = pl.BlockSpec(memory_space=pltpu.SMEM)
 
@@ -252,7 +249,7 @@
             jax.ShapeDtypeStruct((seq_len, 3 * width), jnp.bfloat16),
             jax.ShapeDtypeStruct((2, width), jnp.float32),
         ),
-        in_specs=[SMEM] * 2 + [VMEM] * 7,
+        in_specs=[SMEM] * 3 + [VMEM] * 6,
         out_specs=[VMEM] * 2,
         scratch_shapes=[pltpu.VMEM((seq_len // BLK, BLK, width), jnp.float32)] * 2
         + [pltpu.VMEM((8, width), jnp.float32)],
@@ -273,18 +270,22 @@
     levels,
     across,
     along,
+    length_ref,
     globals_ref,
     random_ref,
-    limits_ref,
     hidden_ref,
     grads_ref,
     b_query_ref,
     b_value_ref,
-    part_qkv_ref,
-    part_out_ref,
-    part_up_ref,
-    part_down_ref,
-    vectors_ref,
+    w_query_ref,
+    w_key_ref,
+    w_value_ref,
+    w_out_ref,
+    w_up_ref,
+    w_down_ref,
+    b_out,
+    gain1,
+    shift1,
     features_ref,
     own_ref,
     upstream_ref,
@@ -333,7 +334,7 @@
     cols = 2 * levels
     seq_len, width = hidden_ref.shape
     own_len = seq_len // cols
-    shard = part_qkv_ref.shape[0]
+    shard = w_query_ref.shape[0]
     other = 1 - core
     sibling = (row, level * 2 + other)
     offsets = range(1, levels)
@@ -344,15 +345,17 @@
     def fast_peer(offset):
         return slow * across + lax.rem(fast + offset, across)
 
-    def slow_peer(offset):
-        return lax.rem(slow + offset, along) * across + fast
+    def line_peer(shift):
+        return ((slow + shift) * across + fast, column)
 
     barrier = pltpu.get_barrier_semaphore()
     greeted = [sibling]
     for offset in offsets:
         greeted += [(row, peer_level(offset) * 2 + core), (row, peer_level(offset) * 2 + other)]
     greeted += [(fast_peer(offset), column) for offset in range(1, across)]
-    greeted += [(slow_peer(offset), column) for offset in range(1, along)]
+    greeted += [
+        (lax.rem(slow + offset, along) * across + fast, column) for offset in range(1, along)
+    ]
     for device in greeted:
         pl.semaphore_signal(barrier, inc=1, device_id=device, device_id_type=MESH)
     pl.semaphore_wait(barrier, len(greeted))
@@ -394,22 +397,48 @@
         features_ref[rows, block(column, width)] = hidden_ref[rows, :]
         core_copy(turn, 0).start()
 
-    parts = (part_qkv_ref, part_out_ref, part_up_ref, part_down_ref)
     fulls = (full_qkv_ref, full_out_ref, full_up_ref, full_down_ref)
     sibs = (None, out_sib, up_sib, down_sib)
 
     def shard_rows(place):
         return block(place * across + fast, shard)
 
-    def along_copy(kind, offset):
-        view = fulls[kind].at[shard_rows(slow)]
+    def line_copy(kind, way, hop):
+        view = fulls[kind].at[shard_rows(slow - (1 - 2 * way) * hop)]
         return remote(
             view,
             view,
-            along_send.at[kind, offset - 1],
-            along_recv.at[kind, along - offset - 1],
-            (slow_peer(offset), column),
-        )
+            along_send.at[kind, way, hop],
+            along_recv.at[kind, way, hop],
+            line_peer(1 - 2 * way),
+        )
+
+    def line_can_send(way, hop):
+        if way == 0:
+            return (slow >= hop) & (slow < along - 1)
+        return (slow < along - hop) & (slow > 0)
+
+    def line_send(kind, hop):
+        for way in range(2):
+
+            @pl.when(line_can_send(way, hop))
+            def _():
+                line_copy(kind, way, hop).start()
+
+    def line_got(way, hop):
+        place = slow - (1 - 2 * way) * (hop + 1)
+        return place, ((place >= 0) if way == 0 else (place < along))
+
+    def line_wait(kind, way, hop):
+        place, _ = line_got(way, hop)
+        view = fulls[kind].at[shard_rows(place)]
+        remote(
+            view,
+            view,
+            along_send.at[kind, way, hop],
+            along_recv.at[kind, way, hop],
+            line_peer(-(1 - 2 * way)),
+        ).wait_recv()
 
     def across_copy(kind, place, offset):
         view = fulls[kind].at[shard_rows(place)]
@@ -431,14 +460,12 @@
             sibling,
         )
 
-    for kind in range(KINDS):
-        fulls[kind][shard_rows(slow), :] = parts[kind][...]
-        for offset in range(1, along):
-            along_copy(kind, offset).start()
-        for offset in range(1, across):
-            across_copy(kind, slow, offset).start()
-        if kind > 0:
-            core_shard(kind, slow, 0).start()
+    for place, ref in enumerate((w_query_ref, w_key_ref, w_value_ref)):
+        full_qkv_ref[shard_rows(slow), place * width : (place + 1) * width] = ref[...].astype(low)
+    line_send(0, 0)
+    full_out_ref[shard_rows(slow), :] = w_out_ref[...].T.astype(low)
+    full_up_ref[shard_rows(slow), :] = w_up_ref[...].astype(low)
+    full_down_ref[shard_rows(slow), :] = w_down_ref[...].T.astype(low)
 
     def swap_copy(target, place_out, place_in):
         return remote(
@@ -458,17 +485,38 @@
         copy.start()
     upstream_ref[:, block(column, width)] = grads_ref[block(column, own_len), :]
 
-    waiting = [(kind, offset) for kind in range(KINDS) for offset in range(1, along)]
-
-    def pass_on(count):
-        for kind, offset in waiting[:count]:
-            along_copy(kind, along - offset).wait_recv()
-            for step in range(1, across):
-                across_copy(kind, lax.rem(slow + offset, along), step).start()
-            if kind > 0:
-                core_shard(kind, lax.rem(slow + offset, along), 0).start()
+    def pass_shard(kind, place):
+        for step in range(1, across):
+            across_copy(kind, place, step).start()
+        if kind > 0:
+            core_shard(kind, place, 0).start()
+
+    hops = range(along - 1)
+    waiting = [(1, hop) for hop in hops] + [(3, -1), (2, 0), (3, 0)]
+    waiting += [(kind, hop) for hop in hops if hop > 0 for kind in (2, 3)]
+
+    def pass_on(count=1):
+        pass_these(waiting[:count])
         del waiting[:count]
 
+    def pass_these(shards):
+        for kind, hop in shards:
+            if hop < 0:
+                pass_shard(kind, slow)
+                continue
+            for way in range(2):
+                place, there = line_got(way, hop)
+
+                @pl.when(there)
+                def _():
+                    line_wait(kind, way, hop)
+                    if hop < along - 2:
+
+                        @pl.when(line_can_send(way, hop + 1))
+                        def _():
+                            line_copy(kind, way, hop + 1).start()
+
+                    pass_shard(kind, place)
     def await_shards(kind):
         @pl.loop(0, along)
         def _(place):
@@ -483,7 +531,10 @@
             for offset in range(across):
                 core_shard(kind, place, offset).wait_recv()
 
-    pass_on(along - 1)
+    pass_these([(0, hop) for hop in range(-1, along - 2)])
+    for kind in range(1, KINDS):
+        line_send(kind, 0)
+    pass_these([(0, along - 2), (1, -1), (2, -1)])
     await_shards(0)
 
     def project(turn):
@@ -495,7 +546,7 @@
             core_copy(turn, offset).wait_recv()
         values_in = features_ref[rows, :]
         queries_ref[rows, :] = (
-            dot(values_in, full_qkv_ref[:, :width]) + b_query_ref[...]
+            dot(values_in, full_qkv_ref[:, :width]) + b_query_ref[:, block(column, width)]
         ).astype(low)
         blocks = pl.ds(turn * (own_len // BLK), own_len // BLK)
         by_block = (own_len // BLK, BLK, width)
@@ -503,28 +554,29 @@
             dot(values_in, full_qkv_ref[:, width : 2 * width]).astype(low).reshape(by_block)
         )
         values_ref[blocks] = (
-            (dot(values_in, full_qkv_ref[:, 2 * width :]) + b_value_ref[...])
+            (dot(values_in, full_qkv_ref[:, 2 * width :]) + b_value_ref[:, block(column, width)])
             .astype(low)
             .reshape(by_block)
         )
 
     for turn in range(cols):
         project(turn)
-        pass_on(1)
+        pass_on(1 if (3, -1) in waiting else 0)
+    while (2, 0) in waiting:
+        pass_on()
     own_ref[...] = features_ref[block(column, own_len), :]
     step = own_len // CHUNKS
     halves = 2
     count = own_len // BLK // halves
-    b_out, gain1, shift1 = (vectors_ref.at[place : place + 1, :] for place in range(3))
 
     def attend_half(quarter, half):
         attend_blocks(
             (quarter * halves + half) * count,
             count,
             min(count, 4),
+            length_ref,
             globals_ref,
             random_ref,
-            limits_ref,
             (queries_ref, keys_ref, values_ref),
             context_ref,
             (highest_ref, scale_ref),
@@ -573,7 +625,7 @@
         for half in range(halves):
             attend_half(place * 2 + other, half)
             context_copy(place, half).start()
-            pass_on(half if len(waiting) > along - 1 else 0)
+            pass_on(1 - half if offset else half)
         if offset == 1:
             await_shards(1)
         for half in range(halves):
@@ -588,9 +640,8 @@
                         low
                     )
                     sum_copy(chunk, offset).start()
-        pass_on(1 if len(waiting) > along - 1 else 0)
-    pass_on(max(len(waiting) - (along - 1), 0))
-    await_shards(2)
+            pass_on(1 if offset else half)
+    pass_on(len(waiting))
     for chunk in range(CHUNKS):
         rows = block(chunk, step)
         summed = own_ref[rows, :].astype(full) + attn_part(level, chunk) + b_out[...]
@@ -604,8 +655,7 @@
         normed_full[chunk_rows(level, chunk), :] = (normed * gain1[...] + shift1[...]).astype(low)
         for offset in offsets:
             normed_copy(chunk, offset).start()
-        pass_on(1 if chunk else 0)
-    pass_on(len(waiting))
+    await_shards(2)
     await_shards(3)
     for chunk in range(CHUNKS):
         for offset in offsets:
@@ -619,8 +669,12 @@
     for copy in swaps:
         copy.wait()
     for kind in range(KINDS):
-        for offset in range(1, along):
-            along_copy(kind, offset).wait_send()
+        for hop in range(along - 1):
+            for way in range(2):
+
+                @pl.when(line_can_send(way, hop))
+                def _():
+                    line_copy(kind, way, hop).wait_send()
 
         @pl.loop(0, along)
         def _(place):
@@ -642,7 +696,7 @@
     return 2 if rows <= 8 else rows // 4
 
 
-def front(levels, rows, tables, hidden_in, grads, biases, parts, vectors):
+def front(levels, rows, tables, hidden_in, grads, biases, weights, vectors):
     low, full = jnp.bfloat16, jnp.float32
     shape = jax.ShapeDtypeStruct
     across = across_of(rows)
@@ -651,6 +705,8 @@
     cols = 2 * levels
     own_len = seq_len // cols
     features_all = width * cols
+    units = weights[4].shape[1]
+    widths = (3 * width, width, units, units)
     others = levels - 1
     stat = shape((seq_len // BLK, 1, width), full)
     dma = pltpu.SemaphoreType.DMA
@@ -666,14 +722,14 @@
             shape((seq_len, width), low),
             stat,
             stat,
-            *(shape((part.shape[0] * rows, part.shape[1]), low) for part in parts),
-            *(shape((part.shape[0] * rows, part.shape[1]), low) for part in parts[1:]),
+            *(shape((features_all, each), low) for each in widths),
+            *(shape((features_all, each), low) for each in widths[1:]),
             shape((levels * own_len, width), low),
             shape((levels * own_len, features_all), low),
             shape((own_len, features_all), full),
             shape((own_len, 1), full),
         ),
-        in_specs=[SMEM] * 2 + [VMEM] * 10,
+        in_specs=[SMEM] * 3 + [VMEM] * 13,
         out_specs=[VMEM] * 20,
         scratch_shapes=[
             pltpu.VMEM((others, own_len, features_all), low),
@@ -684,8 +740,8 @@
             dma((cols, levels)),
             dma((cols,)),
             dma((cols,)),
-            dma((KINDS, along - 1)),
-            dma((KINDS, along - 1)),
+            dma((KINDS, 2, along - 1)),
+            dma((KINDS, 2, along - 1)),
             dma((KINDS, along, across - 1)),
             dma((KINDS, along, across - 1)),
             dma((KINDS - 1, along, across)),
@@ -702,7 +758,7 @@
             bytes_accessed=20 * 1024 * 1024,
             transcendentals=seq_len * 512 * (width // DH),
         ),
-    )(*tables, hidden_in, grads, *biases, *parts, vectors)
+    )(*tables, hidden_in, grads, *biases, *weights, *vectors)
 
 
 def dot(left, right):
@@ -750,10 +806,10 @@
     levels,
     across,
     along,
+    length_ref,
     context_ref,
     context_sib,
     upstream_ref,
-    valid_ref,
     out_ref,
     out_sib,
     up_ref,
@@ -763,7 +819,11 @@
     normed_full,
     unit1,
     inv1,
-    vectors_ref,
+    gain1,
+    shift1,
+    b_down,
+    gain2,
+    shift2,
     b_up_ref,
     layer_out_ref,
     context_grad_ref,
@@ -772,6 +832,7 @@
     up_small_ref,
     share_down_ref,
     up_part_ref,
+    up_own_ref,
     grad_out_ref,
     ffn_full,
     hidden,
@@ -807,25 +868,22 @@
     fast, slow = lax.rem(row, across), lax.div(row, across)
     shard = share_down_ref.shape[0]
     own_len = upstream_ref.shape[0]
+    units = up_ref.shape[1]
     step = own_len // CHUNKS
-    b_out, gain1, shift1, b_down, gain2, shift2 = (
-        vectors_ref.at[place : place + 1, :] for place in range(6)
-    )
 
     def peer_level(offset):
         return lax.rem(level + offset, levels)
 
     def fast_peer(offset):
         return slow * across + lax.rem(fast + offset, across)
-
-    def slow_peer(offset):
-        return lax.rem(slow + offset, along) * across + fast
 
     barrier = pltpu.get_barrier_semaphore()
     greeted = [sibling]
     greeted += [(row, peer_level(offset) * 2 + core) for offset in range(1, levels)]
     greeted += [(fast_peer(offset), column) for offset in range(1, across)]
-    greeted += [(slow_peer(offset), column) for offset in range(1, along)]
+    greeted += [
+        (lax.rem(slow + offset, along) * across + fast, column) for offset in range(1, along)
+    ]
     for device in greeted:
         pl.semaphore_signal(barrier, inc=1, device_id=device, device_id_type=MESH)
     pl.semaphore_wait(barrier, len(greeted))
@@ -896,7 +954,8 @@
         normed = normed_full[rows, :]
         total = None
         for side, (up_side, down_side) in enumerate(sides):
-            active, bend = gelu_parts(dot(normed, up_side[...]) + b_up_ref[side : side + 1, :])
+            bias = b_up_ref[:, block(column + side * (1 - 2 * core), units)]
+            active, bend = gelu_parts(dot(normed, up_side[...]) + bias)
             active = active.astype(low)
             hidden[side, rows, :] = active
             slope[side, rows, :] = bend.astype(low)
@@ -921,10 +980,14 @@
         for offset in offsets:
             sum_copy(2, chunk, offset).wait_recv()
         normed, inv_std = norm_parts(summed + received(2, chunk))
+        position = lax.broadcasted_iota(jnp.int32, (step, 1), 0) + (
+            column * own_len + chunk * step
+        )
+        valid = position < length_ref[0]
         layer_out_ref[rows, :] = jnp.where(
-            valid_ref[rows, :] > 0, normed * gain2[...] + shift2[...], 0.0
+            valid, normed * gain2[...] + shift2[...], 0.0
         ).astype(low)
-        upstream = upstream_ref[rows, :].astype(jnp.float32)
+        upstream = jnp.where(valid, upstream_ref[rows, :].astype(jnp.float32), 0.0)
         grad = norm_back(upstream, normed, inv_std, gain2[...])
         ffn_keep[rows, :] = grad
         grad_low = grad.astype(low)
@@ -982,15 +1045,6 @@
             (fast_peer(offset), column),
         )
 
-    def along_grad(offset):
-        return remote(
-            down_pass.at[offset - 1],
-            down_in.at[along - offset - 1],
-            along_send.at[offset - 1],
-            along_recv.at[along - offset - 1],
-            (slow_peer(offset), column),
-        )
-
     def own_shard(kind, turn):
         for offset in range(1, across):
             across_grad(kind, turn, offset).wait_recv()
@@ -999,14 +1053,50 @@
             total += got[kind][place, block(turn, shard), :].astype(jnp.float32)
         return total
 
-    for kind in range(2):
-
-        @pl.loop(0, along)
-        def _(turn):
-            slope[kind, block(turn, tile), :] = grad_tile(kind, 1, turn).astype(low)
-
-        core_grad(kind).start()
-    for kind in range(2):
+    def line_peer(shift):
+        return ((slow + shift) * across + fast, column)
+
+    def line_copy(kind, way, target):
+        return remote(
+            line_out[kind].at[way, target],
+            line_in[kind].at[way, target],
+            along_send.at[kind, way, target],
+            along_recv.at[kind, way, target],
+            line_peer(1 - 2 * way),
+        )
+
+    def line_step(kind, hop):
+        for way in range(2):
+            position = hop if way == 0 else along - 1 - hop
+            targets = range(along - 1, hop, -1) if way == 0 else range(0, along - 1 - hop)
+
+            @pl.when(slow == position)
+            def _():
+                for target in targets:
+                    total = own_shard(kind, target)
+                    if hop > 0:
+                        line_copy(kind, way, target).wait_recv()
+                        total += line_in[kind][way, target].astype(jnp.float32)
+                    line_out[kind][way, target] = total.astype(jnp.bfloat16)
+                    line_copy(kind, way, target).start()
+
+    def line_finish(kind):
+        for way in range(2):
+
+            @pl.when((slow > 0) if way == 0 else (slow < along - 1))
+            def _():
+                line_copy(kind, way, slow).wait_recv()
+                shares[kind][...] += line_in[kind][way, slow].astype(jnp.float32)
+
+    def line_sent(kind):
+        for way in range(2):
+            for target in range(along):
+
+                @pl.when((slow < target) if way == 0 else (slow > target))
+                def _():
+                    line_copy(kind, way, target).wait_send()
+
+    def sum_grad(kind):
         core_grad(kind).wait_recv()
 
         @pl.loop(0, along)
@@ -1017,6 +1107,18 @@
             ).astype(low)
             for offset in range(1, across):
                 across_grad(kind, turn, offset).start()
+
+    line_out, line_in, shares = (down_pass,), (down_in,), (share_down_ref,)
+    for kind in range(2):
+
+        @pl.loop(0, along)
+        def _(turn):
+            slope[kind, block(turn, tile), :] = grad_tile(kind, 1, turn).astype(low)
+
+        core_grad(kind).start()
+        if kind:
+            sum_grad(kind - 1)
+    sum_grad(1)
 
     @pl.loop(0, CHUNKS)
     def _(chunk):
@@ -1034,10 +1136,8 @@
         small_ref[4:5, :] += jnp.sum(upstream, axis=0, keepdims=True)
         small_ref[5:6, :] += jnp.sum(grad_low.astype(jnp.float32), axis=0, keepdims=True)
 
-    for offset in range(1, along):
-        down_pass[offset - 1] = own_shard(0, lax.rem(slow + offset, along)).astype(low)
-        along_grad(offset).start()
     share_down_ref[...] = own_shard(0, slow)
+    line_step(0, 0)
 
     def context_back(place, chunk):
         rows = rows_of(place, chunk)
@@ -1045,12 +1145,15 @@
         context_grad_ref[context_rows(place, chunk), :] = dot(upstream, out_ref[...]).astype(low)
         context_send[rows, :] = dot(upstream, out_sib[...]).astype(low)
 
-    @pl.loop(0, CHUNKS)
-    def _(chunk):
+    for chunk in range(CHUNKS):
         context_back(level, chunk)
         for offset in offsets:
             spread_copy(5, chunk, levels - offset).wait_recv()
             context_back(peer_level(offset), chunk)
+        if 0 < chunk < along - 1:
+            line_step(0, chunk)
+    for hop in range(CHUNKS, along - 1):
+        line_step(0, hop)
 
     back_copies = [
         to_sibling(
@@ -1081,20 +1184,15 @@
     for side, right in enumerate((own_context, context_sib[...])):
         stage[side] = dot_tn(attn_full[...], right).astype(low)
         out_put(side).start()
-    for turn in range(along):
-        up_part_ref[turn] = own_shard(1, turn).astype(low)
-    total = share_down_ref[...]
-    for offset in range(1, along):
-        along_grad(offset).wait_recv()
-    for place in range(along - 1):
-        total += down_in[place].astype(jnp.float32)
-    share_down_ref[...] = total
+    for shift in range(1, along):
+        up_part_ref[shift - 1] = own_shard(1, lax.rem(slow + shift, along)).astype(low)
+    up_own_ref[...] = own_shard(1, slow)
+    line_finish(0)
     for side in range(2):
         out_put(side).wait()
     for kind in range(2):
         core_grad(kind).wait_send()
-    for offset in range(1, along):
-        along_grad(offset).wait_send()
+    line_sent(0)
 
     @pl.loop(0, along)
     def _(place):
@@ -1118,16 +1216,16 @@
 def middle(
     levels,
     rows,
+    length,
     context,
     context_sib,
     upstream,
-    valid,
     weights,
     normed_full,
     unit1,
     inv1,
     vectors,
-    b_up_pair,
+    b_up,
 ):
     low, full = jnp.bfloat16, jnp.float32
     across = across_of(rows)
@@ -1151,11 +1249,12 @@
             shape((8, features), full),
             shape((2, units), full),
             shape((shard, units), full),
-            shape((along, shard, units), low),
+            shape((along - 1, shard, units), low),
+            shape((shard, units), full),
             shape((2, features, width), low),
         ),
-        in_specs=[VMEM] * 15,
-        out_specs=[VMEM] * 7 + [hbm],
+        in_specs=[SMEM] + [VMEM] * 18,
+        out_specs=[VMEM] * 8 + [hbm],
         scratch_shapes=[
             vmem((tokens, features), low),
             vmem((2, tokens, units), low),
@@ -1171,14 +1270,14 @@
             vmem((features, units), low),
             vmem((across - 1, along * shard, units), low),
             vmem((across - 1, along * shard, units), low),
-            vmem((along - 1, shard, units), low),
-            vmem((along - 1, shard, units), low),
+            vmem((2, along, shard, units), low),
+            vmem((2, along, shard, units), low),
             dma((4, CHUNKS, others)),
             dma((4, CHUNKS, others)),
             dma((levels + 2,)),
             dma((levels + 2,)),
-            dma((along - 1,)),
-            dma((along - 1,)),
+            dma((1, 2, along)),
+            dma((1, 2, along)),
             dma((2, along, across - 1)),
             dma((2, along, across - 1)),
             dma((2,)),
@@ -1192,16 +1291,16 @@
             transcendentals=2 * tokens * units,
         ),
     )(
+        length,
         context,
         context_sib,
         upstream,
-        valid,
         *weights,
         normed_full,
         unit1,
         inv1,
-        vectors,
-        b_up_pair,
+        *vectors,
+        b_up,
     )
 
 
@@ -1215,23 +1314,18 @@
     attn_ref,
     layer_ref,
     small_ref,
+    up_small_ref,
+    bias_ref,
     out_ref,
-    up_ref,
     grad_input_ref,
     layer_out_ref,
     small_out_ref,
-    share_out_ref,
-    share_qkv_ref,
-    share_up_ref,
+    share_ref,
     out_sib,
-    qkv_sums,
-    out_got,
-    qkv_got,
-    out_pass,
-    qkv_pass,
-    out_in,
-    qkv_in,
-    up_in,
+    sums,
+    got,
+    line_out,
+    line_in,
     core_out,
     core_in,
     level_out,
@@ -1263,7 +1357,7 @@
     seq_len = features_ref.shape[0]
     own_len = seq_len // cols
     width = grad_input_ref.shape[1]
-    shard = share_qkv_ref.shape[0]
+    shard = share_ref.shape[0]
     other = 1 - core
     sibling = (row, level * 2 + other)
     offsets = range(1, levels)
@@ -1361,7 +1455,20 @@
         layer_ref.at[:, block(column, width)], layer_out_ref.at[block(column, own_len)], keep_sem
     )
 
-    small_sums[0] = small_ref[...]
+    features_all = weights_ref.shape[0]
+    units = up_small_ref.shape[1]
+    first_up = small_ref.shape[0]
+    small_sums[0] = jnp.zeros_like(small_in[0])
+    small_sums[0, :first_up, :] = small_ref[...]
+    for side in range(2):
+        start = (column + side * (1 - 2 * core)) * units
+        small_sums[
+            0,
+            pl.ds(first_up + lax.div(start, features_all), 1),
+            pl.ds(pl.multiple_of(lax.rem(start, features_all), units), units),
+        ] = up_small_ref[side : side + 1, :]
+    first_bias = small_in.shape[1] - 4
+    small_sums[0, first_bias : first_bias + 2, block(column, width)] = bias_ref[...]
     small_step()
     out_copy.start()
     attn_copy.start()
@@ -1393,55 +1500,25 @@
                 ).astype(low)
                 part_copy(turn, place).start()
 
-    sums = (out_sib, qkv_sums)
-    got = (out_got, qkv_got)
-    passed = (out_pass, qkv_pass)
-    landed = (out_in, qkv_in, up_in)
-    shares = (share_out_ref, share_qkv_ref, share_up_ref)
-
-    def across_copy(kind, turn, offset):
+    def across_copy(turn, offset):
         return remote(
-            sums[kind].at[block(turn * across + lax.rem(fast + offset, across), shard)],
-            got[kind].at[across - offset - 1, block(turn, shard)],
-            across_send.at[kind, turn, offset - 1],
-            across_recv.at[kind, turn, across - offset - 1],
+            sums.at[block(turn * across + lax.rem(fast + offset, across), shard)],
+            got.at[across - offset - 1, block(turn, shard)],
+            across_send.at[turn, offset - 1],
+            across_recv.at[turn, across - offset - 1],
             (fast_peer(offset), column),
         )
 
-    def along_copy(kind, offset):
-        if kind == 2:
-            source = up_ref.at[lax.rem(slow + offset, along)]
-        else:
-            source = passed[kind].at[offset - 1]
-        return remote(
-            source,
-            landed[kind].at[along - offset - 1],
-            along_send.at[kind, offset - 1],
-            along_recv.at[kind, along - offset - 1],
-            (slow_peer(offset), column),
-        )
-
-    def give_across(kind, turn):
+    def weight_grad(turn):
+        rows = block(turn, across * shard)
+        sums[rows, : 3 * width] = dot_tn(features_ref[:, rows], query_key_value_ref[...]).astype(
+            low
+        )
+        sums[rows, 3 * width :] = (
+            out_ref[0, rows, :].astype(full) + out_sib[rows, :].astype(full)
+        ).astype(low)
         for offset in range(1, across):
-            across_copy(kind, turn, offset).start()
-
-    def sum_cores():
-        out_copy.wait()
-
-        @pl.loop(0, along)
-        def _(turn):
-            rows = block(turn, across * shard)
-            out_sib[rows, :] = (
-                out_ref[0, rows, :].astype(full) + out_sib[rows, :].astype(full)
-            ).astype(low)
-            give_across(0, turn)
-
-    def weight_grad():
-        @pl.loop(0, along)
-        def _(turn):
-            rows = block(turn, across * shard)
-            qkv_sums[rows, :] = dot_tn(features_ref[:, rows], query_key_value_ref[...]).astype(low)
-            give_across(1, turn)
+            across_copy(turn, offset).start()
 
     def level_copy(turn, offset):
         rows = block(turn, own_len)
@@ -1466,20 +1543,38 @@
                 ).astype(low)
                 level_copy(turn, offset).start()
 
-    def own_shard(kind, turn):
+    def own_shard(turn):
         for offset in range(1, across):
-            across_copy(kind, turn, offset).wait_recv()
-        total = sums[kind][block(turn * across + fast, shard), :].astype(full)
+            across_copy(turn, offset).wait_recv()
+        total = sums[block(turn * across + fast, shard), :].astype(full)
         for place in range(across - 1):
-            total += got[kind][place, block(turn, shard), :].astype(full)
+            total += got[place, block(turn, shard), :].astype(full)
         return total
 
-    def give_along(kind):
-        for offset in range(1, along):
-            turn = lax.rem(slow + offset, along)
-            passed[kind][offset - 1] = own_shard(kind, turn).astype(low)
-            along_copy(kind, offset).start()
-        shares[kind][...] = own_shard(kind, slow)
+    def line_copy(way, target):
+        return remote(
+            line_out.at[way, target],
+            line_in.at[way, target],
+            along_send.at[way, target],
+            along_recv.at[way, target],
+            ((slow + 1 - 2 * way) * across + fast, column),
+        )
+
+    def line_step(hop, near):
+        if hop >= along - 1 - near:
+            return
+        for way in range(2):
+            target = along - 1 - near if way == 0 else near
+            position = hop if way == 0 else along - 1 - hop
+
+            @pl.when(slow == position)
+            def _():
+                total = own_shard(target)
+                if hop > 0:
+                    line_copy(way, target).wait_recv()
+                    total += line_in[way, target].astype(full)
+                line_out[way, target] = total.astype(low)
+                line_copy(way, target).start()
 
     def finish_input(turn, attn_part):
         rows = block(turn, own_len)
@@ -1492,54 +1587,55 @@
             total += level_in[place, rows, :].astype(full)
         grad_input_ref[rows, :] = total.astype(low)
 
-    def finish_inputs():
-        attn_copy.wait()
-
-        @pl.loop(0, levels)
-        def _(place):
-            rows = block(place, own_len)
-            finish_input(place * 2 + core, attn_ref[rows, block(column, width)])
-            finish_input(place * 2 + other, attn_in[rows, :])
-
-    for offset in range(1, along):
-        along_copy(2, offset).start()
-    share_up_ref[...] = up_ref[slow].astype(full)
-    weight_grad()
+    ends = [turn for place in range(along // 2) for turn in (along - 1 - place, place)]
+    out_copy.wait()
+    for turn in ends:
+        weight_grad(turn)
     small_step()
     give_core()
-    sum_cores()
     small_step()
     give_levels()
-    small_step()
-    give_along(1)
-    small_step()
-    give_along(0)
-    small_step()
-    finish_inputs()
+    line_steps = sorted(
+        ((hop, near) for near in range(along - 1) for hop in range(along - 1 - near)),
+        key=lambda step: step[0] + 2 * step[1],
+    )
+    for step in line_steps[: len(line_steps) // 3]:
+        line_step(*step)
+        small_step()
+    attn_copy.wait()
+    for place in range(levels):
+        for step in line_steps[len(line_steps) // 3 :][place::levels]:
+            line_step(*step)
+        rows = block(place, own_len)
+        finish_input(place * 2 + core, attn_ref[rows, block(column, width)])
+        finish_input(place * 2 + other, attn_in[rows, :])
+        small_step()
+    share_ref[...] = own_shard(slow)
     while small_turn[0] <= len(partners):
         small_step()
     small_out_ref[...] = small_sums[len(partners)]
 
-    for kind in range(3):
-        total = shares[kind][...]
-        for offset in range(1, along):
-            along_copy(kind, offset).wait_recv()
-        for place in range(along - 1):
-            total += landed[kind][place].astype(full)
-        shares[kind][...] = total
+    for way in range(2):
+
+        @pl.when((slow > 0) if way == 0 else (slow < along - 1))
+        def _():
+            line_copy(way, slow).wait_recv()
+            share_ref[...] += line_in[way, slow].astype(full)
 
     layer_keep.wait()
     for copy in layer_copies:
         copy.wait()
-    for kind in range(3):
-        for offset in range(1, along):
-            along_copy(kind, offset).wait_send()
-    for kind in range(2):
-
-        @pl.loop(0, along)
-        def _(turn):
-            for offset in range(1, across):
-                across_copy(kind, turn, offset).wait_send()
+    for way in range(2):
+        for target in range(along):
+
+            @pl.when((slow < target) if way == 0 else (slow > target))
+            def _():
+                line_copy(way, target).wait_send()
+
+    @pl.loop(0, along)
+    def _(turn):
+        for offset in range(1, across):
+            across_copy(turn, offset).wait_send()
 
     @pl.loop(0, cols)
     def _(turn):
@@ -1550,7 +1646,7 @@
 
 
 def finish(
-    levels, rows, query_key_value, weights, features, attn_full, layer_own, small, out, up
+    levels, rows, query_key_value, weights, features, attn_full, layer_own, small, up_small, bias, out
 ):
     low, full = jnp.bfloat16, jnp.float32
     shape = jax.ShapeDtypeStruct
@@ -1560,34 +1656,35 @@
     width = query_key_value.shape[1] // 3
     own_len = layer_own.shape[0]
     shard = features_all // rows
-    widths = [out.shape[2], 3 * width]
-    units = up.shape[2]
     others = levels - 1
     cols = 2 * levels
     turns = 1 + (levels - 1).bit_length() + (rows - 1).bit_length()
+    small_rows = small.shape[0] + up_small.shape[1] * cols // features_all + 4
     dma = pltpu.SemaphoreType.DMA
+    vmem = pltpu.VMEM
     return pl.pallas_call(
         functools.partial(end_kernel, levels, across, along),
         out_shape=(
             shape((seq_len, width), low),
             shape((seq_len, width), low),
-            shape(small.shape, full),
-            *(shape((shard, each), full) for each in widths + [units]),
+            shape((small_rows, features_all), full),
+            shape((shard, 4 * width), full),
         ),
-        in_specs=[VMEM] * 8,
-        out_specs=[VMEM] * 6,
+        in_specs=[VMEM] * 9,
+        out_specs=[VMEM] * 4,
         scratch_shapes=[
-            *(pltpu.VMEM((features_all, each), low) for each in widths),
-            *(pltpu.VMEM((across - 1, along * shard, each), low) for each in widths),
-            *(pltpu.VMEM((along - 1, shard, each), low) for each in widths),
-            *(pltpu.VMEM((along - 1, shard, each), low) for each in widths + [units]),
-            pltpu.VMEM((levels, seq_len, width), low),
-            pltpu.VMEM((levels, seq_len, width), low),
-            pltpu.VMEM((others, seq_len, width), low),
-            pltpu.VMEM((others, seq_len, width), low),
-            pltpu.VMEM((levels * own_len, width), low),
-            pltpu.VMEM((turns + 1, *small.shape), full),
-            pltpu.VMEM((turns, *small.shape), full),
+            vmem((features_all, width), low),
+            vmem((features_all, 4 * width), low),
+            vmem((across - 1, along * shard, 4 * width), low),
+            vmem((2, along, shard, 4 * width), low),
+            vmem((2, along, shard, 4 * width), low),
+            vmem((levels, seq_len, width), low),
+            vmem((levels, seq_len, width), low),
+            vmem((others, seq_len, width), low),
+            vmem((others, seq_len, width), low),
+            vmem((levels * own_len, width), low),
+            vmem((turns + 1, small_rows, features_all), full),
+            vmem((turns, small_rows, features_all), full),
             dma((2,)),
             dma((2,)),
             dma((cols, levels)),
@@ -1596,29 +1693,127 @@
             dma((cols, others)),
             dma((cols,)),
             dma((cols,)),
-            dma((2, along, across - 1)),
-            dma((2, along, across - 1)),
-            dma((3, along - 1)),
-            dma((3, along - 1)),
+            dma((along, across - 1)),
+            dma((along, across - 1)),
+            dma((2, along)),
+            dma((2, along)),
             dma((turns,)),
             dma((turns,)),
             dma,
         ],
         compiler_params=pltpu.CompilerParams(
-            collective_id=2, has_side_effects=True, vmem_limit_bytes=60 * 1024 * 1024
+            collective_id=2, has_side_effects=True, vmem_limit_bytes=56 * 1024 * 1024
         ),
         cost_estimate=pl.CostEstimate(
             flops=4 * seq_len * features_all * 3 * width,
-            bytes_accessed=40 * 1024 * 1024,
+            bytes_accessed=20 * 1024 * 1024,
             transcendentals=0,
         ),
-    )(query_key_value, weights, features, attn_full, layer_own, small, out, up)
-
-
-def into_full(portion, start_at, full_len):
-    return lax.dynamic_update_slice_in_dim(
-        jnp.zeros((full_len,), jnp.float32), portion, start_at, 0
-    )
+    )(query_key_value, weights, features, attn_full, layer_own, small, up_small, bias, out)
+
+
+def last_kernel(
+    grad_input_ref,
+    layer_ref,
+    small_ref,
+    share_ref,
+    down_ref,
+    up_own_ref,
+    up_first_ref,
+    *refs,
+):
+    more, outs = refs[: len(refs) - 18], refs[len(refs) - 18 :]
+    (
+        layer_out,
+        grad_input,
+        grad_query,
+        bias_query,
+        grad_key,
+        grad_value,
+        bias_value,
+        grad_out,
+        bias_out,
+        gain1,
+        shift1,
+        grad_up,
+        bias_up,
+        grad_down,
+        bias_down,
+        gain2,
+        shift2,
+        sems,
+    ) = outs
+    copies = [
+        pltpu.make_async_copy(grad_input_ref, grad_input, sems.at[0]),
+        pltpu.make_async_copy(layer_ref, layer_out, sems.at[1]),
+    ]
+    for copy in copies:
+        copy.start()
+    width = grad_query.shape[1]
+    for place, ref in enumerate((grad_query, grad_key, grad_value)):
+        ref[...] = share_ref[:, place * width : (place + 1) * width]
+    grad_out[...] = share_ref[:, 3 * width :].T
+    grad_down[...] = down_ref[...].T
+    total = up_own_ref[...]
+    for ref in (up_first_ref, *more):
+        total += ref[...].astype(jnp.float32)
+    grad_up[...] = total
+    features_all = small_ref.shape[1]
+    last = small_ref.shape[0] - 4
+    for place, ref in (
+        (0, gain2),
+        (1, shift2),
+        (2, bias_down),
+        (3, gain1),
+        (4, shift1),
+        (5, bias_out),
+        (last, bias_query),
+        (last + 1, bias_value),
+    ):
+        ref[...] = small_ref[place : place + 1, :]
+    for place in range(8, last):
+        bias_up[:, (place - 8) * features_all : (place - 7) * features_all] = small_ref[
+            place : place + 1, :
+        ]
+    for copy in copies:
+        copy.wait()
+
+
+def put_out(grad_input, layer_out, small, share, down, up_own, up_others):
+    low, full = jnp.bfloat16, jnp.float32
+    shape = jax.ShapeDtypeStruct
+    hbm = pl.BlockSpec(memory_space=pl.ANY)
+    seq_len, width = grad_input.shape
+    shard, units = up_own.shape
+    features_all = small.shape[1]
+    vector = shape((1, features_all), full)
+    units_all = (small.shape[0] - 12) * features_all
+    grad = shape((shard, width), full)
+    return pl.pallas_call(
+        last_kernel,
+        out_shape=(
+            shape((seq_len, width), low),
+            shape((seq_len, width), low),
+            grad,
+            vector,
+            grad,
+            grad,
+            vector,
+            shape((width, shard), full),
+            vector,
+            vector,
+            vector,
+            shape((shard, units), full),
+            shape((1, units_all), full),
+            shape((units, shard), full),
+            vector,
+            vector,
+            vector,
+        ),
+        in_specs=[hbm] * 2 + [VMEM] * (4 + len(up_others)),
+        out_specs=[hbm] * 2 + [VMEM] * 15,
+        scratch_shapes=[pltpu.SemaphoreType.DMA((2,))],
+    )(grad_input, layer_out, small, share, down, up_own, *up_others)
 
 
 def on_device(
@@ -1643,29 +1838,10 @@
     ln2_gain,
     ln2_bias,
 ):
-    low = jnp.bfloat16
-    seq_len = hidden_in.shape[0]
-    feat_cols = hidden_in.shape[1]
-    unit_cols = w_up.shape[1]
     cols = lax.axis_size("col")
-    features_all = feat_cols * cols
-    units_all = unit_cols * cols
-    num_blocks = seq_len // BLK
-    head_count = feat_cols // DH
-    own_len = seq_len // cols
-    column = lax.axis_index("col")
-    feat_start = column * feat_cols
-    unit_start = column * unit_cols
-    own_start = column * own_len
-    length = lengths[0]
-    tables = (
-        global_blocks.reshape(-1),
-        rand_blocks.reshape(-1),
-        limits_of(length, global_blocks[0], rand_blocks[0], num_blocks, head_count),
-    )
-    vectors = jnp.stack([b_out, ln1_gain, ln1_bias, b_down, ln2_gain, ln2_bias, b_out, b_out])
-    valid = (jnp.arange(seq_len) < length)[:, None]
-    own_valid = (own_start + jnp.arange(own_len) < length).astype(jnp.float32)[:, None]
+    rows = lax.axis_size("row")
+    tables = (lengths, global_blocks.reshape(-1), rand_blocks.reshape(-1))
+    as_row = lambda vector: vector[None, :]
     (
         features,
         own_features,
@@ -1689,83 +1865,65 @@
         inv1,
     ) = front(
         cols // 2,
-        lax.axis_size("row"),
+        rows,
         tables,
         hidden_in,
-        jnp.where(valid, out_grad, 0),
-        (
-            lax.dynamic_slice_in_dim(b_query, feat_start, feat_cols)[None, :],
-            lax.dynamic_slice_in_dim(b_value, feat_start, feat_cols)[None, :],
-        ),
-        (
-            jnp.concatenate([w_query, w_key, w_value], axis=1).astype(low),
-            w_out.T.astype(low),
-            w_up.astype(low),
-            w_down.T.astype(low),
-        ),
-        vectors,
+        out_grad,
+        (as_row(b_query), as_row(b_value)),
+        (w_query, w_key, w_value, w_out, w_up, w_down),
+        (as_row(b_out), as_row(ln1_gain), as_row(ln1_bias)),
     )
-
-    sibling = column + 1 - 2 * lax.rem(column, 2)
-    layer_own, context_grad, attn_full, small, up_small, down_share, up_part, grad_out = middle(
+    (
+        layer_own,
+        context_grad,
+        attn_full,
+        small,
+        up_small,
+        down_share,
+        up_part,
+        up_own,
+        grad_out,
+    ) = middle(
         cols // 2,
-        lax.axis_size("row"),
+        rows,
+        lengths,
         context,
         context_sib,
         upstream,
-        own_valid,
         (full_out, out_sib, full_up, up_sib, full_down, down_sib),
         normed_full,
         unit1,
         inv1,
-        vectors,
-        jnp.stack(
-            [
-                lax.dynamic_slice_in_dim(b_up, unit_start, unit_cols),
-                lax.dynamic_slice_in_dim(b_up, sibling * unit_cols, unit_cols),
-            ]
-        ),
+        tuple(as_row(each) for each in (ln1_gain, ln1_bias, b_down, ln2_gain, ln2_bias)),
+        as_row(b_up),
     )
+    across = across_of(rows)
+    up_others = [
+        lax.ppermute(
+            up_part[shift - 1],
+            "row",
+            [(place, (place + shift * across) % rows) for place in range(rows)],
+        )
+        for shift in range(1, rows // across)
+    ]
     query_key_value, bias_sums = attend_back(
         queries, key_rows, value_rows, tables, (highest, scale), context_grad
     )
-    up_sums = into_full(up_small[0], unit_start, units_all) + into_full(
-        up_small[1], sibling * unit_cols, units_all
-    )
-    bias_full = lax.dynamic_update_slice(
-        jnp.zeros((4, features_all), jnp.float32), bias_sums, (0, feat_start)
-    )
-    grad_input, layer_out, small, out_share, qkv_share, up_share = finish(
+    grad_input, layer_out, small, share = finish(
         cols // 2,
-        lax.axis_size("row"),
+        rows,
         query_key_value,
         full_qkv,
         features,
         attn_full,
         layer_own,
-        jnp.concatenate([small, up_sums.reshape(-1, features_all), bias_full], axis=0),
+        small,
+        up_small,
+        bias_sums,
         grad_out,
-        up_part,
     )
-    return (
-        layer_out,
-        grad_input,
-        qkv_share[:, :feat_cols],
-        small[-4],
-        qkv_share[:, feat_cols : 2 * feat_cols],
-        qkv_share[:, 2 * feat_cols :],
-        small[-3],
-        out_share.T,
-        small[5],
-        small[3],
-        small[4],
-        up_share,
-        small[8:-4].reshape(-1),
-        down_share.T,
-        small[2],
-        small[0],
-        small[1],
-    )
+    outs = put_out(grad_input, layer_out, small, share, down_share, up_own, up_others)
+    return tuple(each.reshape(-1) if each.shape[0] == 1 else each for each in outs)
 
 
 def solution(mesh):

time: 374 us -> 398 us (1.064)
  Pallas kernels: 333 us -> 376 us
  local copies, waits for them, and re-layouts: 24.9 us -> 9.59 us
  other arithmetic: 7.13 us -> 0 us
    pallas_call x0 -> x1, Pallas kernels: none -> 67.4 us  [put_out(): pl.pallas_call(last_kernel, out_shape=(shape((seq_len, width), low), shap...]
    pallas_call x1, Pallas kernels: 120 us -> 105 us  [front(): pl.pallas_call(functools.partial(front_kernel, levels, across, along), ou...]
    unnamed x68 -> x27, local copies, waits for them, and re-layouts: 13.9 us -> 7.63 us
    pallas_call x1, Pallas kernels: 64.4 us -> 59.5 us  [finish(): pl.pallas_call(functools.partial(end_kernel, levels, across, along), out_...]
    pallas_call x1, Pallas kernels: 125 us -> 120 us  [middle(): pl.pallas_call(functools.partial(middle_kernel, levels, across, along), o...]
    slice x3 -> x0, local copies, waits for them, and re-layouts: 4.44 us -> none  [the longest x1 1.93 us: on_device(): qkv_share[:, 2 * feat_cols:]]
  transfers between devices with their start and end apart: 0 -> 3, of which waited for: 0 -> 0; matrix products, arithmetic and copies ran while one was open for 0% -> 0% of each run, Pallas kernels for 0% -> 21%
where the time goes in v7:
time: 398 us; the launch traced here: 390 us
  Pallas kernels  376 us (94%)
  local copies, waits for them, and re-layouts  9.59 us (2%)
    pallas_call x1, Pallas kernels, middle(): pl.pallas_call(functools.partial(middle_kernel, levels, across, along), o...  120 us
    pallas_call x1, Pallas kernels, front(): pl.pallas_call(functools.partial(front_kernel, levels, across, along), ou...  105 us
    pallas_call x1, Pallas kernels, put_out(): pl.pallas_call(last_kernel, out_shape=(shape((seq_len, width), low), shap...  67.4 us
    pallas_call x1, Pallas kernels, finish(): pl.pallas_call(functools.partial(end_kernel, levels, across, along), out_...  59.5 us
    pallas_call x1, Pallas kernels, attend_back(): pl.pallas_call(functools.partial(attend_back_kernel, head_count, 8), out_...  23.4 us
  transfers between devices with their start and end apart: 3, of which 0 were waited for; matrix products, arithmetic and copies ran while one was open for 0% of the time, Pallas kernels for 21%

profile of v7, /device:TPU:0, one launch (start us, length us, event | category | flops | bytes accessed | tf_op | source)
XLA Modules:
  0.0 390.1 jit_solution(13184022765420617184)
XLA Ops:
  1.3 0.8 copy.37
  2.1 0.8 reshape.68.random_ref
  2.9 105.5 %shard_map.323 = (bf16[2048,1024]{1,0:T(8,128)(2,1)}, bf16[512,1024]{1,0:T(8,128)(2,1)}, bf16[512,1024]{1,0:T(8,128)(2,1)}, bf16[2048,256]{1,0:T(8,128)(2,1)}, b...) custom-call(s32[1]{0:T(128)S(6)} %copy.38.length_ref, ...), custom_call_target="tpu_custom_call" | custom-call | flops 3221225472 | bytes 20971520 | tf_op jit(solution)/shard_map/pallas_call | solution.py:713
  108.4 0.0 copy-start
  108.4 0.0 copy-start.1
  108.5 120.2 %shard_map.324 = (bf16[512,1024]{1,0:T(8,128)(2,1)}, bf16[2048,256]{1,0:T(8,128)(2,1)}, bf16[1024,1024]{1,0:T(8,128)(2,1)}, f32[8,1024]{1,0:T(8,128)}, f32[2,102...) custom-call(s32[1]{0:T(128)S(6)} %copy.38.length_ref, ...), custom_call_target="tpu_custom_call" | custom-call | flops 28991029248 | bytes 20971520 | tf_op jit(solution)/shard_map/pallas_call | solution.py:1243
  228.6 1.2 slice_bitcast_fusion
  229.8 1.5 collective-permute-start.2
  231.3 0.0 collective-permute-start.1
  231.3 1.4 collective-permute-start
  232.7 1.2 copy-done.4
  233.9 1.2 copy-done.5
  235.1 1.2 copy-done.6
  236.4 23.4 %shard_map.325 = (bf16[2048,768]{1,0:T(8,128)(2,1)S(1)}, f32[2,256]{1,0:T(2,128)S(1)}) custom-call(s32[1]{0:T(128)S(6)} %copy.38.length_ref, s32[2]{0:T(128)S(1)} %bitcast.26, s32[384]{0:T(512)S(1)} %copy-done, bf16[2048,256]{1,0:T(8,128)(2,1)S(1)} %copy-done.3, bf16[32,64,256]{2,1,0:T(8,128)(2,1)S(1)} %copy-done.4, bf16[32,64,256]{2,1,0:T(8,128)(2,1)S(1)} %copy-done.5, ...), custom_call_target="tpu_custom_call" | custom-call | flops 10737418240 | bytes 7340032 | tf_op jit(solution)/shard_map/pallas_call | solution.py:246
  259.8 1.7 copy-done.2
  261.4 0.6 copy-done.9
  262.0 59.5 %shard_map.326 = (bf16[2048,256]{1,0:T(8,128)(2,1)}, bf16[2048,256]{1,0:T(8,128)(2,1)}, f32[16,1024]{1,0:T(8,128)}, f32[128,1024]{1,0:T(8,128)}) custom-call(bf16[2048,768]{1,0:T(8,128)(2,1)} %copy-done.2, bf16[1024,768]{1,0:T(8,128)(2,1)} %get-tuple-element.87.weights_ref, bf16[2048,1024]{1,0:T(8,128)(2,1)} %get-tuple-element.88.features_ref, ...), custom_call_target="tpu_custom_call" | custom-call | flops 6442450944 | bytes 20971520 | tf_op jit(solution)/shard_map/pallas_call | solution.py:1665
  321.6 0.0 collective-permute-done.2.refs_1_
  321.6 0.0 collective-permute-done.1.refs_0_
  321.6 0.0 collective-permute-done.up_first_ref
  321.6 0.7 copy-done.10
  322.3 0.1 copy-done.11
  322.4 0.1 copy-done.12
  322.5 67.4 %shard_map.327 = (bf16[2048,256]{1,0:T(8,128)(2,1)}, bf16[2048,256]{1,0:T(8,128)(2,1)}, f32[128,256]{1,0:T(8,128)}, f32[1,1024]{1,0:T(1,128)}, f32[128,256]{1,0:...) custom-call(bf16[2048,256]{1,0:T(8,128)(2,1)} %get-tuple-element.95., ...), custom_call_target="tpu_custom_call" | custom-call | tf_op jit(solution)/shard_map/pallas_call | solution.py:1792
  (16 shorter events, 0.0 us)
Async XLA Ops:
  108.4 124.3 %copy-start = (s32[384]{0:T(512)S(1)}, s32[384]{0:T(512)}, u32[]{:S(2)}) copy-start(s32[384]{0:T(512)} %reshape.68.random_ref) | copy-start | bytes 4612
  108.4 124.3 %copy-start.1 = (s32[1,2]{1,0:T(1,128)S(1)}, s32[1,2]{1,0:T(1,128)}, u32[]{:S(2)}) copy-start(s32[1,2]{1,0:T(1,128)} %param.23) | copy-start | bytes 28
  108.4 124.3 %copy-start.3 = (bf16[2048,256]{1,0:T(8,128)(2,1)S(1)}, bf16[2048,256]{1,0:T(8,128)(2,1)}, u32[]{:S(2)}) copy-start(bf16[2048,256]{1,0:T(8,128)(2,1)} %get-tuple-element.68.queries_ref) | copy-start | bytes 3145732
  108.4 124.2 %copy-start.7 = (f32[32,1,256]{2,1,0:T(1,128)S(1)}, f32[32,1,256]{2,1,0:T(1,128)}, u32[]{:S(2)}) copy-start(f32[32,1,256]{2,1,0:T(1,128)} %get-tuple-element.84.highest_ref) | copy-start | bytes 98308
  108.4 124.2 %copy-start.8 = (f32[32,1,256]{2,1,0:T(1,128)S(1)}, f32[32,1,256]{2,1,0:T(1,128)}, u32[]{:S(2)}) copy-start(f32[32,1,256]{2,1,0:T(1,128)} %get-tuple-element.85.scale_ref) | copy-start | bytes 98308
  229.8 91.8 %collective-permute-start.2 = (bf16[128,1024]{1,0:T(8,128)(2,1)S(1)}, bf16[128,1024]{1,0:T(8,128)(2,1)S(1)}, u32[]{:S(2)}, u32[]{:S(2)}) collective-permute-start(bf16[128,1024]{1,0:T(8,128)(2,1)S(1)} %get-tuple-element.119), channel_id=1, source_target_pairs={{0,24},{4,28},{8,0},{12,4},{16,8},{20,12},{24,16},{28,20},{1,25},{... | collective-permute-start | bytes 786440 | tf_op jit(solution)/shard_map/ppermute | solution.py:1902
  231.3 90.3 %collective-permute-start.1 = (bf16[128,1024]{1,0:T(8,128)(2,1)S(1)}, bf16[128,1024]{1,0:T(8,128)(2,1)S(1)}, u32[]{:S(2)}, u32[]{:S(2)}) collective-permute-start(bf16[128,1024]{1,0:T(8,128)(2,1)S(1)} %get-tuple-element.120), channel_id=1, source_target_pairs={{0,16},{4,20},{8,24},{12,28},{16,0},{20,4},{24,8},{28,12},{1,17},{... | collective-permute-start | bytes 786440 | tf_op jit(solution)/shard_map/ppermute | solution.py:1902
  231.3 90.3 %collective-permute-start = (bf16[128,1024]{1,0:T(8,128)(2,1)S(1)}, bf16[128,1024]{1,0:T(8,128)(2,1)S(1)}, u32[]{:S(2)}, u32[]{:S(2)}) collective-permute-start(bf16[128,1024]{1,0:T(8,128)(2,1)S(1)} %get-tuple-element.121), channel_id=1, source_target_pairs={{0,8},{4,12},{8,16},{12,20},{16,24},{20,28},{24,0},{28,4},{1,9},{5... | collective-permute-start | bytes 786440 | tf_op jit(solution)/shard_map/ppermute | solution.py:1902
  232.7 1.2 copy-start.4
  233.9 1.2 copy-start.5
  235.1 1.2 copy-start.6
  259.7 1.7 copy-start.2
  261.4 0.6 copy-start.9
  321.6 0.8 copy-start.10
  321.6 0.8 copy-start.11
  321.6 0.9 copy-start.12

commit v8 on v7

--- a/solution.py
+++ b/solution.py
@@ -1722,7 +1722,7 @@
     up_first_ref,
     *refs,
 ):
-    more, outs = refs[: len(refs) - 18], refs[len(refs) - 18 :]
+    more, outs = refs[: len(refs) - 17], refs[len(refs) - 17 :]
     (
         layer_out,
         grad_input,
@@ -1741,14 +1741,9 @@
         bias_down,
         gain2,
         shift2,
-        sems,
     ) = outs
-    copies = [
-        pltpu.make_async_copy(grad_input_ref, grad_input, sems.at[0]),
-        pltpu.make_async_copy(layer_ref, layer_out, sems.at[1]),
-    ]
-    for copy in copies:
-        copy.start()
+    grad_input[...] = grad_input_ref[...]
+    layer_out[...] = layer_ref[...]
     width = grad_query.shape[1]
     for place, ref in enumerate((grad_query, grad_key, grad_value)):
         ref[...] = share_ref[:, place * width : (place + 1) * width]
@@ -1775,14 +1770,11 @@
         bias_up[:, (place - 8) * features_all : (place - 7) * features_all] = small_ref[
             place : place + 1, :
         ]
-    for copy in copies:
-        copy.wait()
 
 
 def put_out(grad_input, layer_out, small, share, down, up_own, up_others):
     low, full = jnp.bfloat16, jnp.float32
     shape = jax.ShapeDtypeStruct
-    hbm = pl.BlockSpec(memory_space=pl.ANY)
     seq_len, width = grad_input.shape
     shard, units = up_own.shape
     features_all = small.shape[1]
@@ -1810,9 +1802,9 @@
             vector,
             vector,
         ),
-        in_specs=[hbm] * 2 + [VMEM] * (4 + len(up_others)),
-        out_specs=[hbm] * 2 + [VMEM] * 15,
-        scratch_shapes=[pltpu.SemaphoreType.DMA((2,))],
+        in_specs=[VMEM] * (6 + len(up_others)),
+        out_specs=[VMEM] * 17,
+        compiler_params=pltpu.CompilerParams(vmem_limit_bytes=24 * 1024 * 1024),
     )(grad_input, layer_out, small, share, down, up_own, *up_others)
 
 

time: 398 us -> 336 us (0.84)
  the two profiles are of different devices: /device:TPU:0 before, /device:TPU:8 now
where the time goes in v8:
time: 336 us; the launch traced here: 329 us
  Pallas kernels  310 us (92%)
  local copies, waits for them, and re-layouts  13 us (4%)
  starting transfers between devices  5.14 us (2%)
    pallas_call x1, Pallas kernels, middle(): pl.pallas_call(functools.partial(middle_kernel, levels, across, along), o...  122 us
    pallas_call x1, Pallas kernels, front(): pl.pallas_call(functools.partial(front_kernel, levels, across, along), ou...  100 us
    pallas_call x1, Pallas kernels, finish(): pl.pallas_call(functools.partial(end_kernel, levels, across, along), out_...  61.8 us
    pallas_call x1, Pallas kernels, attend_back(): pl.pallas_call(functools.partial(attend_back_kernel, head_count, 8), out_...  23.3 us
    unnamed x33, local copies, waits for them, and re-layouts  11.1 us
  transfers between devices with their start and end apart: 3, of which 0 were waited for; matrix products, arithmetic and copies ran while one was open for 0% of the time, Pallas kernels for 26%

profile of v8, /device:TPU:8, one launch (start us, length us, event | category | flops | bytes accessed | tf_op | source)
XLA Modules:
  0.0 329.4 jit_solution(4432742128800092983)
XLA Ops:
  1.3 0.8 copy.37
  2.1 0.8 reshape.68.random_ref
  2.9 100.5 %shard_map.323 = (bf16[2048,1024]{1,0:T(8,128)(2,1)}, bf16[512,1024]{1,0:T(8,128)(2,1)}, bf16[512,1024]{1,0:T(8,128)(2,1)}, bf16[2048,256]{1,0:T(8,128)(2,1)}, b...) custom-call(s32[1]{0:T(128)S(6)} %copy.38.length_ref, ...), custom_call_target="tpu_custom_call" | custom-call | flops 3221225472 | bytes 20971520 | tf_op jit(solution)/shard_map/pallas_call | solution.py:713
  103.4 0.0 copy-start.6
  103.4 0.0 copy-start.7
  103.4 121.9 %shard_map.324 = (bf16[512,1024]{1,0:T(8,128)(2,1)}, bf16[2048,256]{1,0:T(8,128)(2,1)}, bf16[1024,1024]{1,0:T(8,128)(2,1)}, f32[8,1024]{1,0:T(8,128)}, f32[2,102...) custom-call(s32[1]{0:T(128)S(6)} %copy.38.length_ref, ...), custom_call_target="tpu_custom_call" | custom-call | flops 28991029248 | bytes 20971520 | tf_op jit(solution)/shard_map/pallas_call | solution.py:1243
  225.4 1.2 slice_bitcast_fusion
  226.5 2.2 collective-permute-start.2
  228.8 0.8 collective-permute-start.1
  229.6 2.1 collective-permute-start
  231.7 1.2 copy-done.10
  232.9 1.2 copy-done.11
  234.2 1.2 copy-done.12
  235.4 23.3 %shard_map.325 = (bf16[2048,768]{1,0:T(8,128)(2,1)S(1)}, f32[2,256]{1,0:T(2,128)S(1)}) custom-call(s32[1]{0:T(128)S(6)} %copy.38.length_ref, s32[2]{0:T(128)S(1)} %bitcast.26, s32[384]{0:T(512)S(1)} %copy-done.6, bf16[2048,256]{1,0:T(8,128)(2,1)S(1)} %copy-done.9, bf16[32,64,256]{2,1,0:T(8,128)(2,1)S(1)} %copy-done.10, bf16[32,64,256]{2,1,0:T(8,128)(2,1)S(1)} %copy-done.11, ...), custom_call_target="tpu_custom_call" | custom-call | flops 10737418240 | bytes 7340032 | tf_op jit(solution)/shard_map/pallas_call | solution.py:246
  258.8 1.7 copy-done.8
  260.4 0.6 copy-done.15
  261.0 61.8 %shard_map.326 = (bf16[2048,256]{1,0:T(8,128)(2,1)}, bf16[2048,256]{1,0:T(8,128)(2,1)}, f32[16,1024]{1,0:T(8,128)}, f32[128,1024]{1,0:T(8,128)}) custom-call(bf16[2048,768]{1,0:T(8,128)(2,1)} %copy-done.8, bf16[1024,768]{1,0:T(8,128)(2,1)} %get-tuple-element.87.weights_ref, bf16[2048,1024]{1,0:T(8,128)(2,1)} %get-tuple-element.88.features_ref, ...), custom_call_target="tpu_custom_call" | custom-call | flops 6442450944 | bytes 20971520 | tf_op jit(solution)/shard_map/pallas_call | solution.py:1665
  322.8 0.0 collective-permute-done.2.refs_1_
  322.8 0.0 collective-permute-done.up_first_ref
  322.8 1.2 copy-done
  324.1 1.2 copy-done.1
  325.3 1.0 copy-done.4
  326.3 0.8 copy-done.5
  327.2 2.0 shard_map.327
  (22 shorter events, 0.0 us)
Async XLA Ops:
  103.4 128.3 %copy-start.6 = (s32[384]{0:T(512)S(1)}, s32[384]{0:T(512)}, u32[]{:S(2)}) copy-start(s32[384]{0:T(512)} %reshape.68.random_ref) | copy-start | bytes 4612
  103.4 128.3 %copy-start.7 = (s32[1,2]{1,0:T(1,128)S(1)}, s32[1,2]{1,0:T(1,128)}, u32[]{:S(2)}) copy-start(s32[1,2]{1,0:T(1,128)} %param.23) | copy-start | bytes 28
  103.4 128.3 %copy-start.9 = (bf16[2048,256]{1,0:T(8,128)(2,1)S(1)}, bf16[2048,256]{1,0:T(8,128)(2,1)}, u32[]{:S(2)}) copy-start(bf16[2048,256]{1,0:T(8,128)(2,1)} %get-tuple-element.68.queries_ref) | copy-start | bytes 3145732
  103.4 128.3 %copy-start.13 = (f32[32,1,256]{2,1,0:T(1,128)S(1)}, f32[32,1,256]{2,1,0:T(1,128)}, u32[]{:S(2)}) copy-start(f32[32,1,256]{2,1,0:T(1,128)} %get-tuple-element.84.highest_ref) | copy-start | bytes 98308
  103.4 128.3 %copy-start.14 = (f32[32,1,256]{2,1,0:T(1,128)S(1)}, f32[32,1,256]{2,1,0:T(1,128)}, u32[]{:S(2)}) copy-start(f32[32,1,256]{2,1,0:T(1,128)} %get-tuple-element.85.scale_ref) | copy-start | bytes 98308
  226.5 96.2 %collective-permute-start.2 = (bf16[128,1024]{1,0:T(8,128)(2,1)S(1)}, bf16[128,1024]{1,0:T(8,128)(2,1)S(1)}, u32[]{:S(2)}, u32[]{:S(2)}) collective-permute-start(bf16[128,1024]{1,0:T(8,128)(2,1)S(1)} %get-tuple-element.119), channel_id=1, source_target_pairs={{0,24},{4,28},{8,0},{12,4},{16,8},{20,12},{24,16},{28,20},{1,25},{... | collective-permute-start | bytes 786440 | tf_op jit(solution)/shard_map/ppermute | solution.py:1894
  228.8 94.0 %collective-permute-start.1 = (bf16[128,1024]{1,0:T(8,128)(2,1)S(1)}, bf16[128,1024]{1,0:T(8,128)(2,1)S(1)}, u32[]{:S(2)}, u32[]{:S(2)}) collective-permute-start(bf16[128,1024]{1,0:T(8,128)(2,1)S(1)} %get-tuple-element.120), channel_id=1, source_target_pairs={{0,16},{4,20},{8,24},{12,28},{16,0},{20,4},{24,8},{28,12},{1,17},{... | collective-permute-start | bytes 786440 | tf_op jit(solution)/shard_map/ppermute | solution.py:1894
  229.6 93.3 %collective-permute-start = (bf16[128,1024]{1,0:T(8,128)(2,1)S(1)}, bf16[128,1024]{1,0:T(8,128)(2,1)S(1)}, u32[]{:S(2)}, u32[]{:S(2)}) collective-permute-start(bf16[128,1024]{1,0:T(8,128)(2,1)S(1)} %get-tuple-element.121), channel_id=1, source_target_pairs={{0,8},{4,12},{8,16},{12,20},{16,24},{20,28},{24,0},{28,4},{1,9},{5... | collective-permute-start | bytes 786440 | tf_op jit(solution)/shard_map/ppermute | solution.py:1894
  231.7 1.2 copy-start.10
  232.9 1.2 copy-start.11
  234.2 1.2 copy-start.12
  258.7 1.7 copy-start.8
  260.4 0.6 copy-start.15
  261.0 61.8 %copy-start.2 = (f32[128,1024]{1,0:T(8,128)S(1)}, f32[128,1024]{1,0:T(8,128)}, u32[]{:S(2)}) copy-start(f32[128,1024]{1,0:T(8,128)} %get-tuple-element.99.down_ref) | copy-start | bytes 1572868
  261.0 61.8 %copy-start.3 = (f32[128,1024]{1,0:T(8,128)S(1)}, f32[128,1024]{1,0:T(8,128)}, u32[]{:S(2)}) copy-start(f32[128,1024]{1,0:T(8,128)} %get-tuple-element.100.up_own_ref) | copy-start | bytes 1572868
  322.8 1.2 copy-start
  324.1 1.2 copy-start.1
  325.3 1.0 copy-start.4
  326.3 0.8 copy-start.5
